TPU v7x, 256 devices: a whole 4x4x8 slice. The times are simulated.
256 devices in a mesh: batch: 16 (over y_hi, z), seq: 16 (over x, y_lo, core).
Axes of the slice: x: 4, y: 4 (y_hi: 2, y_lo: 2; y = y_hi * 2 + y_lo), z: 8, core: 2. Of those that a mesh axis runs over, the one named last changes fastest.
Arguments:
- forward_embed: bfloat16 [98304, 1536], P(('batch', 'seq')), parts along dimension 0, may hold values from -6 to 6
- reverse_embed: bfloat16 [98304, 1536], P(('batch', 'seq')), parts along dimension 0, may hold values from -6 to 6
- conv_weight: bfloat16 [1, 3, 1536, 1536], P(None, None, 'seq'), may hold values from -0.09375 to 0.09375
- conv_bias: float32 [1, 1536], replicated, may hold values from -0.5 to 0.5
- head_weight: bfloat16 [1536, 1024], replicated, may hold values from -0.15625 to 0.15625
- head_bias: float32 [1024], replicated, may hold values from -1 to 1
Outputs:
- averaged: bfloat16 [98304, 1024], P(('batch', 'seq')), parts along dimension 0
There are 16 independent parts, one for each index of `batch`. A program takes and returns all parts, laid end to end along the dimension named above; an argument that names none is the same for every part. Nothing has to cross between parts.
All inputs are finite; a program needn't handle non-finite values.
Results may differ from a plain program's by a relative error of at most 0.008.
Values may be sent and summed in bfloat16 or wider, within the bound.
No kernel may reach another device: no remote copies, remote signals or barrier semaphores. Data moves between devices by JAX's collectives and lax.ppermute only.
A program may use at most 128 MiB of HBM per device.

v0:
```python
import jax
import jax.numpy as jnp
from jax import lax
from jax.sharding import PartitionSpec as P


def with_halo(block, sides, width):
    for axis, dim in sides:
        count = lax.axis_size(axis)
        forward = [(i, i + 1) for i in range(count - 1)]
        backward = [(target, source) for source, target in forward]
        low = lax.ppermute(
            lax.slice_in_dim(block, block.shape[dim] - width, None, axis=dim), axis, forward
        )
        high = lax.ppermute(lax.slice_in_dim(block, 0, width, axis=dim), axis, backward)
        block = jnp.concatenate([low, block, high], axis=dim)
    return block


def partner(block, axis, stride):
    count = lax.axis_size(axis)
    route = []
    for low in range(count):
        high = low | 1 << stride
        if high != low and high < count:
            route += [(low, high), (high, low)]
    return lax.ppermute(block, axis, route)


def convolve(stacked, kernel, bias):
    count = stacked.shape[1]
    padded = with_halo(stacked, (("seq", 1),), 1)
    empty = jnp.zeros((stacked.shape[0], count, kernel.shape[2]), jnp.float32)
    taps = lax.all_gather(kernel, "seq", axis=1, tiled=True)
    term = empty[0]
    for tap in range(3):
        term = term + jnp.dot(
            padded[0, tap : tap + count], taps[tap], preferred_element_type=jnp.float32
        )
    results = [term]
    acc = jnp.stack(results)
    return jax.nn.gelu(acc + bias, approximate=False).astype(jnp.bfloat16)


def run_strands(stacked, conv_weight, conv_bias, head_weight, head_bias):
    hidden = stacked
    hidden = convolve(hidden, conv_weight[0], conv_bias[0])
    logits = (
        jnp.einsum("kbc,ct->kbt", hidden, head_weight, preferred_element_type=jnp.float32)
        + head_bias
    )
    return jax.nn.softplus(logits).astype(jnp.bfloat16)


def per_device(forward_embed, reverse_embed, conv_weight, conv_bias, head_weight, head_bias):
    levels = lax.axis_size("seq").bit_length() - 1
    forward_tracks = run_strands(
        forward_embed[None], conv_weight, conv_bias, head_weight, head_bias
    )[0]
    reverse_tracks = run_strands(
        reverse_embed[None], conv_weight, conv_bias, head_weight, head_bias
    )[0]
    for level in range(levels):
        reverse_tracks = partner(reverse_tracks, "seq", level)
    reverse_tracks = reverse_tracks[::-1]
    mean = 0.5 * (forward_tracks.astype(jnp.float32) + reverse_tracks.astype(jnp.float32))
    return mean.astype(jnp.bfloat16)


def solution(mesh):
    return jax.shard_map(
        per_device,
        mesh=mesh,
        in_specs=(
            P(("batch", "seq"), None),
            P(("batch", "seq"), None),
            P(None, None, "seq", None),
            P(),
            P(),
            P(),
        ),
        out_specs=P(("batch", "seq"), None),
        check_vma=False,
    )
```

profile of v0, /device:TPU:1, one launch (start us, length us, event | category | flops | bytes accessed | tf_op | source)
XLA Modules:
  0.0 199.7 jit_solution(16371048841047240158)
XLA Ops:
  6.5 0.0 copy-start
  6.5 0.0 all-gather.3.cloned.1.call-start
  6.5 0.7 all-gather.3.cloned.1.call-update
  7.3 1.0 fusion.117
  8.2 5.1 %collective-permute-start.3 = (bf16[1,1,1536]{2,1,0:T(2,128)(2,1)S(1)}, bf16[1,1,1536]{2,1,0:T(2,128)(2,1)S(1)}, u32[]{:S(2)}, u32[]{:S(2)}) collective-permute-start(bf16[1,1,1536]{2,1,0:T(2,128)(2,1)S(1)} %get-tuple-element.8), channel_id=1, source_target_pairs={{1,0},{2,1},{3,2},{4,3},{5,4},{6,5},{7,6},{8,7},{9,8},{10,9},{11,1... | collective-permute-start | bytes 9224 | tf_op jit(solution)/shard_map/ppermute | solution.py:15
  13.4 1.9 collective-permute-start.2
  15.3 0.7 reduce
  16.1 79.2 %all-gather.3.cloned.1.call-done = bf16[1,3,1536,1536]{3,2,1,0:T(8,128)(2,1)} async-done(((bf16[1,3,96,1536]{3,2,1,0:T(8,128)(2,1)}), bf16[1,3,1536,1536]{3,2,1,0:T(8,128)(2,1)}) %all-gather.3.cloned.1.call-update) | async-done | bytes 14155792 | tf_op jit(solution)/shard_map/all_gather | solution.py:34
  95.2 0.0 copy-start.1
  95.2 6.2 %fusion.2 = f32[384,1536]{1,0:T(8,128)} fusion(bf16[384,1536]{1,0:T(8,128)(2,1)} %param.7, bf16[1,3,1536,1536]{3,2,1,0:T(8,128)(2,1)} %all-gather.3.cloned.1.call-done), kind=kOutput, calls=%fused_computation.7 | convolution fusion | flops 1811939328 | bytes 8257536 | tf_op jit(solution)/shard_map/dot_general | solution.py:37
  101.4 0.0 copy-start.3
  101.4 0.0 collective-permute-done.3
  101.4 0.0 copy-done.1
  101.4 5.8 %fusion.4 = f32[384,1536]{1,0:T(8,128)} fusion(bf16[1,3,1536,1536]{3,2,1,0:T(8,128)(2,1)} %all-gather.3.cloned.1.call-done, bf16[1,1,1536]{2,1,0:T(2,128)(2,1)S(1)} %collective-permute-done.3, bf16[1,384,1536]{2,1,0:T(8,128)(2,1)S(1)} %bitcast.56), kind=kOutput, calls=%fused_computation.9 | convolution fusion | flops 1814298624 | bytes 8260608 | tf_op jit(solution)/shard_map/dot_general | solution.py:37
  107.2 0.0 collective-permute-done.2
  107.2 0.0 copy-done
  107.2 0.0 copy-done.3
  107.2 12.9 %fusion.33 = bf16[384,1024]{1,0:T(8,128)(2,1)} fusion(bf16[1536,1024]{1,0:T(8,128)(2,1)S(1)} %copy-done, f32[384,1536]{1,0:T(8,128)} %fusion.4, f32[384,1536]{1,0:T(8,128)} %fusion.2, bf16[1,3,1536,1536]{3,2,1,0:T(8,128)(2,1)} %all-gather.3.cloned.1.call-done, bf16[1,384,1536]{2,1,0:T(8,128)(2,1)} %bitcast.55, ...), kind=kOutput, calls=%fused_computation.56 | convolution fusion | flops 3065511936 | bytes 14562304 | tf_op jit(solution)/shard_map/kbc,ct->kbt/dot_general | solution.py:49
  120.1 0.2 collective-permute-start.4
  120.3 2.2 %collective-permute-done.4 = bf16[384,1024]{1,0:T(8,128)(2,1)S(1)} collective-permute-done((bf16[384,1024]{1,0:T(8,128)(2,1)}, bf16[384,1024]{1,0:T(8,128)(2,1)S(1)}, u32[]{:S(2)}, u32[]{:S(2)}) %collective-permute-start.4) | collective-permute-done | bytes 786464 | tf_op jit(solution)/shard_map/ppermute | solution.py:27
  122.6 1.2 collective-permute-start.5
  123.8 0.8 fusion.116
  124.5 2.4 %collective-permute-start.1 = (bf16[1,1,1536]{2,1,0:T(2,128)(2,1)S(1)}, bf16[1,1,1536]{2,1,0:T(2,128)(2,1)S(1)}, u32[]{:S(2)}, u32[]{:S(2)}) collective-permute-start(bf16[1,1,1536]{2,1,0:T(2,128)(2,1)S(1)} %get-tuple-element.6), channel_id=1, source_target_pairs={{1,0},{2,1},{3,2},{4,3},{5,4},{6,5},{7,6},{8,7},{9,8},{10,9},{11,1... | collective-permute-start | bytes 9224 | tf_op jit(solution)/shard_map/ppermute | solution.py:15
  127.0 0.0 copy-start.2
  127.0 3.2 %collective-permute-start = (bf16[1,1,1536]{2,1,0:T(2,128)(2,1)S(1)}, bf16[1,1,1536]{2,1,0:T(2,128)(2,1)S(1)}, u32[]{:S(2)}, u32[]{:S(2)}) collective-permute-start(bf16[1,1,1536]{2,1,0:T(2,128)(2,1)S(1)} %get-tuple-element.5), channel_id=1, source_target_pairs={{0,1},{1,2},{2,3},{3,4},{4,5},{5,6},{6,7},{7,8},{8,9},{9,10},{10,1... | collective-permute-start | bytes 9224 | tf_op jit(solution)/shard_map/ppermute | solution.py:12
  130.2 11.2 %collective-permute-done.5 = bf16[384,1024]{1,0:T(8,128)(2,1)S(1)} collective-permute-done((bf16[384,1024]{1,0:T(8,128)(2,1)S(1)}, bf16[384,1024]{1,0:T(8,128)(2,1)S(1)}, u32[]{:S(2)}, u32[]{:S(2)}) %collective-permute-start.5) | collective-permute-done | bytes 786464 | tf_op jit(solution)/shard_map/ppermute | solution.py:27
  141.5 1.1 collective-permute-start.6
  142.5 6.1 %fusion.3 = f32[384,1536]{1,0:T(8,128)} fusion(bf16[384,1536]{1,0:T(8,128)(2,1)} %param.6, bf16[1,3,1536,1536]{3,2,1,0:T(8,128)(2,1)} %all-gather.3.cloned.1.call-done), kind=kOutput, calls=%fused_computation.8 | convolution fusion | flops 1811939328 | bytes 8257536 | tf_op jit(solution)/shard_map/dot_general | solution.py:37
  148.6 0.0 collective-permute-done.1
  148.6 0.0 copy-done.2
  148.7 5.8 %fusion.5 = f32[384,1536]{1,0:T(8,128)} fusion(bf16[1,3,1536,1536]{3,2,1,0:T(8,128)(2,1)} %all-gather.3.cloned.1.call-done, bf16[1,1,1536]{2,1,0:T(2,128)(2,1)S(1)} %collective-permute-done.1, bf16[1,384,1536]{2,1,0:T(8,128)(2,1)S(1)} %bitcast.59), kind=kOutput, calls=%fused_computation.10 | convolution fusion | flops 1814298624 | bytes 8260608 | tf_op jit(solution)/shard_map/dot_general | solution.py:37
  154.4 5.1 %collective-permute-done.6 = bf16[384,1024]{1,0:T(8,128)(2,1)} collective-permute-done((bf16[384,1024]{1,0:T(8,128)(2,1)S(1)}, bf16[384,1024]{1,0:T(8,128)(2,1)}, u32[]{:S(2)}, u32[]{:S(2)}) %collective-permute-start.6) | collective-permute-done | bytes 786464 | tf_op jit(solution)/shard_map/ppermute | solution.py:27
  159.6 2.2 %collective-permute-start.7 = (bf16[384,1024]{1,0:T(8,128)(2,1)}, bf16[384,1024]{1,0:T(8,128)(2,1)}, u32[]{:S(2)}, u32[]{:S(2)}) collective-permute-start(bf16[384,1024]{1,0:T(8,128)(2,1)} %collective-permute-done.6), channel_id=1, source_target_pairs={{0,8},{8,0},{1,9},{9,1},{2,10},{10,2},{3,11},{11,3},{4,12},{12,4},... | collective-permute-start | bytes 2359304 | tf_op jit(solution)/shard_map/ppermute | solution.py:27
  161.8 0.0 collective-permute-done
  161.8 12.8 %fusion.32 = bf16[384,1024]{1,0:T(8,128)(2,1)} fusion(bf16[1536,1024]{1,0:T(8,128)(2,1)S(1)} %copy-done, f32[384,1536]{1,0:T(8,128)} %fusion.5, f32[384,1536]{1,0:T(8,128)} %fusion.3, bf16[1,3,1536,1536]{3,2,1,0:T(8,128)(2,1)} %all-gather.3.cloned.1.call-done, bf16[1,384,1536]{2,1,0:T(8,128)(2,1)} %bitcast.58, ...), kind=kOutput, calls=%fused_computation.55 | convolution fusion | flops 3065511936 | bytes 14562304 | tf_op jit(solution)/shard_map/kbc,ct->kbt/dot_general | solution.py:49
  174.7 3.8 %collective-permute-done.7 = bf16[384,1024]{1,0:T(8,128)(2,1)} collective-permute-done((bf16[384,1024]{1,0:T(8,128)(2,1)}, bf16[384,1024]{1,0:T(8,128)(2,1)}, u32[]{:S(2)}, u32[]{:S(2)}) %collective-permute-start.7) | collective-permute-done | bytes 786464 | tf_op jit(solution)/shard_map/ppermute | solution.py:27
  178.4 11.9 %rev.3 = bf16[384,1024]{1,0:T(8,128)(2,1)} reverse(bf16[384,1024]{1,0:T(8,128)(2,1)} %collective-permute-done.7), dimensions={0} | reverse | bytes 1572864 | tf_op jit(solution)/shard_map/rev | solution.py:65
  190.3 2.5 %multiply_convert_fusion = bf16[384,1024]{1,0:T(8,128)(2,1)} fusion(bf16[384,1024]{1,0:T(8,128)(2,1)} %rev.3, bf16[384,1024]{1,0:T(8,128)(2,1)} %fusion.32), kind=kLoop, calls=%fused_computation.57 | loop fusion | flops 1966080 | bytes 2359296 | tf_op jit(solution)/shard_map/convert_element_type | solution.py:67
Async XLA Ops:
  6.5 100.7 %copy-start = (bf16[1536,1024]{1,0:T(8,128)(2,1)S(1)}, bf16[1536,1024]{1,0:T(8,128)(2,1)}, u32[]{:S(2)}) copy-start(bf16[1536,1024]{1,0:T(8,128)(2,1)} %param.10) | copy-start | bytes 9437188
  6.5 88.7 %all-gather.3.cloned.1.call-start = ((), (), s32[]{:S(2)}) async-start(), calls=%async_computation | async-start | bytes 15040512 | tf_op jit(solution)/shard_map/all_gather | solution.py:34
  8.2 93.2 %collective-permute-start.3 = (bf16[1,1,1536]{2,1,0:T(2,128)(2,1)S(1)}, bf16[1,1,1536]{2,1,0:T(2,128)(2,1)S(1)}, u32[]{:S(2)}, u32[]{:S(2)}) collective-permute-start(bf16[1,1,1536]{2,1,0:T(2,128)(2,1)S(1)} %get-tuple-element.8), channel_id=1, source_target_pairs={{1,0},{2,1},{3,2},{4,3},{5,4},{6,5},{7,6},{8,7},{9,8},{10,9},{11,1... | collective-permute-start | bytes 9224 | tf_op jit(solution)/shard_map/ppermute | solution.py:15
  13.4 93.8 %collective-permute-start.2 = (bf16[1,1,1536]{2,1,0:T(2,128)(2,1)S(1)}, bf16[1,1,1536]{2,1,0:T(2,128)(2,1)S(1)}, u32[]{:S(2)}, u32[]{:S(2)}) collective-permute-start(bf16[1,1,1536]{2,1,0:T(2,128)(2,1)S(1)} %get-tuple-element.7), channel_id=1, source_target_pairs={{0,1},{1,2},{2,3},{3,4},{4,5},{5,6},{6,7},{7,8},{8,9},{9,10},{10,1... | collective-permute-start | bytes 9224 | tf_op jit(solution)/shard_map/ppermute | solution.py:12
  95.2 6.2 %copy-start.1 = (bf16[384,1536]{1,0:T(8,128)(2,1)S(1)}, bf16[384,1536]{1,0:T(8,128)(2,1)}, u32[]{:S(2)}) copy-start(bf16[384,1536]{1,0:T(8,128)(2,1)} %param.7) | copy-start | bytes 3538948
  101.4 5.8 %copy-start.3 = (f32[1024]{0:T(1024)S(1)}, f32[1024]{0:T(1024)}, u32[]{:S(2)}) copy-start(f32[1024]{0:T(1024)} %param.11) | copy-start | bytes 12292
  120.1 2.5 %collective-permute-start.4 = (bf16[384,1024]{1,0:T(8,128)(2,1)}, bf16[384,1024]{1,0:T(8,128)(2,1)S(1)}, u32[]{:S(2)}, u32[]{:S(2)}) collective-permute-start(bf16[384,1024]{1,0:T(8,128)(2,1)} %fusion.33), channel_id=1, source_target_pairs={{0,1},{1,0},{2,3},{3,2},{4,5},{5,4},{6,7},{7,6},{8,9},{9,8},{10,11... | collective-permute-start | bytes 2359304 | tf_op jit(solution)/shard_map/ppermute | solution.py:27
  122.6 18.9 %collective-permute-start.5 = (bf16[384,1024]{1,0:T(8,128)(2,1)S(1)}, bf16[384,1024]{1,0:T(8,128)(2,1)S(1)}, u32[]{:S(2)}, u32[]{:S(2)}) collective-permute-start(bf16[384,1024]{1,0:T(8,128)(2,1)S(1)} %collective-permute-done.4), channel_id=1, source_target_pairs={{0,2},{2,0},{1,3},{3,1},{4,6},{6,4},{5,7},{7,5},{8,10},{10,8},{9,1... | collective-permute-start | bytes 2359304 | tf_op jit(solution)/shard_map/ppermute | solution.py:27
  124.5 24.1 %collective-permute-start.1 = (bf16[1,1,1536]{2,1,0:T(2,128)(2,1)S(1)}, bf16[1,1,1536]{2,1,0:T(2,128)(2,1)S(1)}, u32[]{:S(2)}, u32[]{:S(2)}) collective-permute-start(bf16[1,1,1536]{2,1,0:T(2,128)(2,1)S(1)} %get-tuple-element.6), channel_id=1, source_target_pairs={{1,0},{2,1},{3,2},{4,3},{5,4},{6,5},{7,6},{8,7},{9,8},{10,9},{11,1... | collective-permute-start | bytes 9224 | tf_op jit(solution)/shard_map/ppermute | solution.py:15
  127.0 21.7 %copy-start.2 = (bf16[384,1536]{1,0:T(8,128)(2,1)S(1)}, bf16[384,1536]{1,0:T(8,128)(2,1)}, u32[]{:S(2)}) copy-start(bf16[384,1536]{1,0:T(8,128)(2,1)} %param.6) | copy-start | bytes 3538948
  127.0 34.8 %collective-permute-start = (bf16[1,1,1536]{2,1,0:T(2,128)(2,1)S(1)}, bf16[1,1,1536]{2,1,0:T(2,128)(2,1)S(1)}, u32[]{:S(2)}, u32[]{:S(2)}) collective-permute-start(bf16[1,1,1536]{2,1,0:T(2,128)(2,1)S(1)} %get-tuple-element.5), channel_id=1, source_target_pairs={{0,1},{1,2},{2,3},{3,4},{4,5},{5,6},{6,7},{7,8},{8,9},{9,10},{10,1... | collective-permute-start | bytes 9224 | tf_op jit(solution)/shard_map/ppermute | solution.py:12
  141.5 18.1 %collective-permute-start.6 = (bf16[384,1024]{1,0:T(8,128)(2,1)S(1)}, bf16[384,1024]{1,0:T(8,128)(2,1)}, u32[]{:S(2)}, u32[]{:S(2)}) collective-permute-start(bf16[384,1024]{1,0:T(8,128)(2,1)S(1)} %collective-permute-done.5), channel_id=1, source_target_pairs={{0,4},{4,0},{1,5},{5,1},{2,6},{6,2},{3,7},{7,3},{8,12},{12,8},{9,1... | collective-permute-start | bytes 2359304 | tf_op jit(solution)/shard_map/ppermute | solution.py:27
  159.6 18.9 %collective-permute-start.7 = (bf16[384,1024]{1,0:T(8,128)(2,1)}, bf16[384,1024]{1,0:T(8,128)(2,1)}, u32[]{:S(2)}, u32[]{:S(2)}) collective-permute-start(bf16[384,1024]{1,0:T(8,128)(2,1)} %collective-permute-done.6), channel_id=1, source_target_pairs={{0,8},{8,0},{1,9},{9,1},{2,10},{10,2},{3,11},{11,3},{4,12},{12,4},... | collective-permute-start | bytes 2359304 | tf_op jit(solution)/shard_map/ppermute | solution.py:27
Sparse Core Ops, SparseCore 0:
  9.2 86.0 all-gather.2
where the time goes:
time: 203 us; the launch traced here: 200 us
  waiting for transfers between devices  102 us (50%)
  matrix products  49.5 us (24%)
  starting transfers between devices  17.5 us (9%)
  local copies, waits for them, and re-layouts  13.7 us (7%)
  between operations  13.5 us (7%)
  other arithmetic  3.24 us (2%)
    all_gather x1, waiting for transfers between devices, convolve(): taps = lax.all_gather(kernel, 'seq', axis=1, tiled=True)  79.2 us
    dot_general x2, matrix products, run_strands(): jnp.einsum('kbc,ct->kbt', hidden, head_weight, preferred_element_type=jnp...  25.7 us
    dot_general x4, matrix products, convolve(): jnp.dot(padded[0, tap:tap + count], taps[tap], preferred_element_type=jnp...  23.8 us
    ppermute x4, waiting for transfers between devices, partner(): return lax.ppermute(block, axis, route)  22.4 us
    rev x1, local copies, waits for them, and re-layouts, per_device(): reverse_tracks = reverse_tracks[::-1]  11.9 us
    ppermute x2, starting transfers between devices, with_halo(): lax.ppermute(lax.slice_in_dim(block, 0, width, axis=dim), axis, backward)  7.59 us
    ppermute x2, starting transfers between devices, with_halo(): lax.ppermute(lax.slice_in_dim(block, block.shape[dim] - width, None, axis...  5.17 us
    ppermute x4, starting transfers between devices, partner(): return lax.ppermute(block, axis, route)  4.75 us
  transfers between devices with their start and end apart: 9, of which 5 were waited for; matrix products, arithmetic and copies ran while one was open for 20% of the time, Pallas kernels for 0%

commit v1 on v0

v1 whole, which is shorter than its diff:
```python
import functools

import jax
import jax.numpy as jnp
from jax import lax
from jax.experimental import pallas as pl
from jax.experimental.pallas import tpu as pltpu
from jax.sharding import Mesh
from jax.sharding import PartitionSpec as P

AXES = ("y_hi", "z", "x", "y_lo", "core")
SEQ = ("x", "y_lo", "core")
XN, YN, CN = 4, 4, 2
CHUNKS = (512, 512, 512)
VMEM_LIMIT = 56 * 1024 * 1024
EDGE = 16
INV_SQRT2 = 0.7071067811865476


def core_swap(value):
    return lax.ppermute(value, "core", [(0, 1), (1, 0)])


def x_shift(value):
    route = []
    for x in range(XN):
        route += [(x * 2, (x + 1) % XN * 2), (x * 2 + 1, (x - 1) % XN * 2 + 1)]
    return lax.ppermute(value, ("x", "core"), route)


def y_shift(value):
    route = []
    for y in range(YN):
        route += [(y * 2, (y + 1) % YN * 2), (y * 2 + 1, (y - 1) % YN * 2 + 1)]
    return lax.ppermute(value, ("y_hi", "y_lo", "core"), route)


def prepare_kernel(forward_ref, reverse_ref, low_ref, high_ref, out_ref):
    rows = forward_ref.shape[0]
    out_ref[0, :rows, :] = forward_ref[...]
    row = lax.broadcasted_iota(jnp.int32, (rows, rows), 0)
    column = lax.broadcasted_iota(jnp.int32, (rows, rows), 1)
    flip = jnp.where(row + column == rows - 1, 1.0, 0.0).astype(jnp.bfloat16)
    out_ref[1, :rows, :] = jnp.dot(
        flip, reverse_ref[...], preferred_element_type=jnp.float32
    ).astype(jnp.bfloat16)
    width = forward_ref.shape[1]
    edge = lax.broadcasted_iota(jnp.int32, (EDGE, width), 0)
    low = low_ref[...].astype(jnp.float32)
    high = high_ref[...].astype(jnp.float32)
    for strand, after, before in ((0, high[0:1], low[0:1]), (1, low[1:2], high[1:2])):
        tile = jnp.where(edge == 0, after, jnp.where(edge == EDGE - 1, before, 0.0))
        out_ref[strand, rows:, :] = tile.astype(jnp.bfloat16)


def prepare(forward_embed, reverse_embed, low, high):
    rows, width = forward_embed.shape
    return pl.pallas_call(
        prepare_kernel,
        out_shape=jax.ShapeDtypeStruct((2, rows + EDGE, width), jnp.bfloat16),
        compiler_params=pltpu.CompilerParams(vmem_limit_bytes=VMEM_LIMIT),
        cost_estimate=pl.CostEstimate(
            flops=2 * rows * rows * width, bytes_accessed=8 * rows * width, transcendentals=0
        ),
        name="prepare",
    )(forward_embed, reverse_embed, low, high)


def chunk_kernel(strands, start, size, blocks, first, last, *refs):
    place_ref, refs = refs[0], refs[1:]
    sources, refs = refs[: len(blocks)], refs[len(blocks) :]
    x_hbm, bias_ref, head_hbm, head_bias_ref = refs[:4]
    refs = refs[4:]
    if not first:
        prev_hbm, refs = refs[0], refs[1:]
    out_ref, refs = refs[0], refs[1:]
    w_ref, x_ref, head_ref, before_ref, here_ref, after_ref, h_ref = refs[:7]
    refs = refs[7:]
    if not first:
        prev_ref, refs = refs[0], refs[1:]
    w_sem, x_sem, head_sem, prev_sem = refs
    channels = w_ref.shape[1]
    part = channels // 16
    rows = x_ref.shape[1] - EDGE

    x_copies = []
    for slot, strand in enumerate(strands):
        copy = pltpu.make_async_copy(x_hbm.at[strand], x_ref.at[slot], x_sem.at[slot])
        copy.start()
        x_copies.append(copy)
    w_copies = []
    for tap in range(3):
        group = []
        number = 0
        for source, (count, whole) in zip(sources, blocks):
            for index in range(count):
                place = pl.multiple_of(place_ref[number] * part, part)
                piece = source.at[index, tap] if count > 1 else source.at[tap]
                if whole:
                    piece = piece.at[:, pl.ds(start, size)]
                copy = pltpu.make_async_copy(
                    piece, w_ref.at[tap, pl.ds(place, part), :], w_sem.at[tap, number]
                )
                copy.start()
                group.append(copy)
                number += 1
        w_copies.append(group)
    head_copy = pltpu.make_async_copy(head_hbm.at[pl.ds(start, size), :], head_ref, head_sem)
    head_copy.start()
    prev_copies = []
    if not first:
        for slot, strand in enumerate(strands):
            copy = pltpu.make_async_copy(prev_hbm.at[strand], prev_ref.at[slot], prev_sem.at[slot])
            copy.start()
            prev_copies.append(copy)

    bias = bias_ref[...]
    for slot, strand in enumerate(strands):
        x_copies[slot].wait()
        order = (0, 1, 2) if strand == 0 else (2, 1, 0)
        for target, tap in zip((before_ref, here_ref, after_ref), order):
            if slot == 0:
                for copy in w_copies[tap]:
                    copy.wait()
            value = jnp.dot(x_ref[slot], w_ref[tap], preferred_element_type=jnp.float32)
            target[pl.ds(8, rows + EDGE), :] = value
        before_ref[pl.ds(7, 1), :] = before_ref[pl.ds(8 + rows + EDGE - 1, 1), :]
        acc = (
            before_ref[pl.ds(7, rows), :]
            + here_ref[pl.ds(8, rows), :]
            + after_ref[pl.ds(9, rows), :]
            + bias
        )
        hidden = 0.5 * acc * (1.0 + lax.erf(acc * INV_SQRT2))
        h_ref[slot] = hidden.astype(jnp.bfloat16)
        if slot == 0:
            head_copy.wait()
        logits = jnp.dot(h_ref[slot], head_ref[...], preferred_element_type=jnp.float32)
        if not first:
            prev_copies[slot].wait()
            logits = logits + prev_ref[slot]
        if last:
            logits = logits + head_bias_ref[...]
            tracks = jnp.maximum(logits, 0.0) + jnp.log1p(jnp.exp(-jnp.abs(logits)))
            out_ref[slot] = tracks.astype(jnp.bfloat16)
        else:
            out_ref[slot] = logits


def run_chunk(strands, start, size, blocks, place, sources, x, bias, head, head_bias, prev, last):
    rows, channels = x.shape[1] - EDGE, x.shape[2]
    tracks = head.shape[1]
    first = prev is None
    count = len(strands)
    held = pl.BlockSpec(memory_space=pl.ANY)
    inside = pl.BlockSpec(memory_space=pltpu.VMEM)
    scratch = [
        pltpu.VMEM((3, channels, size), jnp.bfloat16),
        pltpu.VMEM((count, rows + EDGE, channels), jnp.bfloat16),
        pltpu.VMEM((size, tracks), jnp.bfloat16),
        pltpu.VMEM((rows + EDGE + 16, size), jnp.float32),
        pltpu.VMEM((rows + EDGE + 16, size), jnp.float32),
        pltpu.VMEM((rows + EDGE + 16, size), jnp.float32),
        pltpu.VMEM((count, rows, size), jnp.bfloat16),
    ]
    if not first:
        scratch.append(pltpu.VMEM((count, rows, tracks), jnp.float32))
    scratch += [
        pltpu.SemaphoreType.DMA((3, 16)),
        pltpu.SemaphoreType.DMA((count,)),
        pltpu.SemaphoreType.DMA,
        pltpu.SemaphoreType.DMA((count,)),
    ]
    operands = [place, *sources, x, bias[:, start : start + size], head, head_bias[None]]
    specs = (
        [pl.BlockSpec(memory_space=pltpu.SMEM)]
        + [held] * len(sources)
        + [held, inside, held, inside]
    )
    if not first:
        operands.append(prev)
        specs.append(held)
    return pl.pallas_call(
        functools.partial(chunk_kernel, strands, start, size, blocks, first, last),
        out_shape=jax.ShapeDtypeStruct(
            (count, rows, tracks), jnp.bfloat16 if last else jnp.float32
        ),
        in_specs=specs,
        out_specs=inside,
        scratch_shapes=scratch,
        compiler_params=pltpu.CompilerParams(vmem_limit_bytes=VMEM_LIMIT),
        cost_estimate=pl.CostEstimate(
            flops=2 * count * rows * size * (3 * channels + tracks),
            bytes_accessed=6 * channels * size + 4 * count * rows * tracks,
            transcendentals=count * rows * size,
        ),
        name="chunk_last" if last else "chunk",
    )(*operands)


def per_device(forward_embed, reverse_embed, conv_weight, conv_bias, head_weight, head_bias):
    own = conv_weight[0]
    channels = own.shape[2]
    x, y, core = lax.axis_index("x"), lax.axis_index("y_lo"), lax.axis_index("core")

    sibling = core_swap(own)
    starts = [sum(CHUNKS[:i]) for i in range(len(CHUNKS))]
    pairs = [
        jnp.stack([own[:, :, s : s + n], sibling[:, :, s : s + n]])
        for s, n in zip(starts, CHUNKS)
    ]
    across = y_shift(own)

    ends = lax.axis_size("x") * lax.axis_size("y_lo") * lax.axis_size("core")
    up = [(i, i + 1) for i in range(ends - 1)]
    down = [(b, a) for a, b in up]
    low = lax.ppermute(jnp.stack([forward_embed[-1], reverse_embed[-1]]), SEQ, up)
    high = lax.ppermute(jnp.stack([forward_embed[0], reverse_embed[0]]), SEQ, down)
    strands = prepare(forward_embed, reverse_embed, low, high)

    across_other = core_swap(across)

    def seq(x_of, y_of, core_of):
        return (x_of % XN) * 4 + y_of * 2 + core_of

    step = 1 - 2 * core
    back, fore, far = x - step + XN, x + step + XN, x + 2
    other, over = 1 - core, 1 - y
    place = jnp.stack(
        [
            seq(x, y, core), seq(x, y, other),
            seq(x, over, core), seq(x, over, other),
            seq(back, y, core), seq(back, y, other),
            seq(fore, y, other), seq(fore, y, core),
            seq(far, y, core), seq(far, y, other),
            seq(back, over, core), seq(back, over, other),
            seq(fore, over, other), seq(fore, over, core),
            seq(far, over, core), seq(far, over, other),
        ]
    ).astype(jnp.int32)
    blocks = (
        (2, False), (1, True), (1, True), (2, False), (2, False), (1, False), (1, False),
        (2, False), (2, False), (1, False), (1, False),
    )

    logits = None
    for number, (start, size) in enumerate(zip(starts, CHUNKS)):
        pair = pairs[number]
        near = x_shift(pair)
        distant = x_shift(near[0])
        near_over = y_shift(near)
        distant_over = y_shift(distant)
        moved = [near, distant, near_over, distant_over]
        near_2, distant_2, near_over_2, distant_over_2 = [core_swap(value) for value in moved]
        sources = [
            pair, across, across_other, near, near_2, distant, distant_2,
            near_over, near_over_2, distant_over, distant_over_2,
        ]
        call = functools.partial(
            run_chunk, start=start, size=size, blocks=blocks, place=place, sources=sources,
            x=strands, bias=conv_bias, head=head_weight, head_bias=head_bias, prev=logits,
        )
        if number < len(CHUNKS) - 1:
            logits = call((0, 1), last=False)
        else:
            reverse_tracks = call((1,), last=True)[0]
            forward_tracks = call((0,), last=True)[0]
    mirror = [(i, ends - 1 - i) for i in range(ends)]
    mirrored = lax.ppermute(reverse_tracks, SEQ, mirror)
    mean = 0.5 * (forward_tracks.astype(jnp.float32) + mirrored.astype(jnp.float32))
    return mean.astype(jnp.bfloat16)


def solution(mesh):
    fine = Mesh(mesh.devices.reshape(2, 8, XN, 2, CN), AXES)
    return jax.shard_map(
        per_device,
        mesh=fine,
        in_specs=(
            P(AXES, None),
            P(AXES, None),
            P(None, None, SEQ, None),
            P(),
            P(),
            P(),
        ),
        out_specs=P(AXES, None),
        check_vma=False,
    )
```

time: 203 us -> 135 us (0.67); the launches traced: 200 us -> 134 us
  waiting for transfers between devices: 102 us -> 40.8 us
  matrix products: 49.5 us -> 0 us
  Pallas kernels: 0 us -> 46.1 us
  starting transfers between devices: 17.5 us -> 36 us
  between operations: 13.5 us -> 0.42 us
  local copies, waits for them, and re-layouts: 13.7 us -> 8.26 us
    all_gather x1 -> x0, waiting for transfers between devices: 79.2 us -> none  [convolve(): taps = lax.all_gather(kernel, 'seq', axis=1, tiled=True)]
    dot_general x6 -> x0, matrix products: 49.5 us -> none  [the longest x2 25.7 us: run_strands(): jnp.einsum('kbc,ct->kbt', hidden, head_weight, preferred_element_type=jnp...]
    pallas_call x0 -> x5, Pallas kernels: none -> 46.1 us  [the longest x4 42.2 us: run_chunk(): pl.pallas_call(functools.partial(chunk_kernel, strands, start, size, bloc...]
    ppermute x8 -> x30, starting transfers between devices: 17.5 us -> 36 us  [the longest x14 16.1 us: core_swap(): return lax.ppermute(value, 'core', [(0, 1), (1, 0)])]
    ppermute x8 -> x30, waiting for transfers between devices: 22.4 us -> 40.8 us  [the longest x7 21.1 us: y_shift(): return lax.ppermute(value, ('y_hi', 'y_lo', 'core'), route)]
    rev x1 -> x0, local copies, waits for them, and re-layouts: 11.9 us -> none  [per_device(): reverse_tracks = reverse_tracks[::-1]]
    unnamed x8 -> x54, local copies, waits for them, and re-layouts: 0.02 us -> 2.95 us
  transfers between devices with their start and end apart: 9 -> 30, of which waited for: 5 -> 9; matrix products, arithmetic and copies ran while one was open for 20% -> 4% of each run, Pallas kernels for 0% -> 28%
where the time goes in v1:
time: 135 us; the launch traced here: 134 us
  Pallas kernels  46.1 us (34%)
  waiting for transfers between devices  40.8 us (30%)
  starting transfers between devices  36 us (27%)
  local copies, waits for them, and re-layouts  8.26 us (6%)
  other arithmetic  2.5 us (2%)
    pallas_call x4, Pallas kernels, run_chunk(): pl.pallas_call(functools.partial(chunk_kernel, strands, start, size, bloc...  42.2 us
    ppermute x7, waiting for transfers between devices, y_shift(): return lax.ppermute(value, ('y_hi', 'y_lo', 'core'), route)  21.1 us
    ppermute x14, starting transfers between devices, core_swap(): return lax.ppermute(value, 'core', [(0, 1), (1, 0)])  16.1 us
    ppermute x1, waiting for transfers between devices, per_device(): mirrored = lax.ppermute(reverse_tracks, SEQ, mirror)  12.2 us
    ppermute x6, starting transfers between devices, x_shift(): return lax.ppermute(value, ('x', 'core'), route)  10.9 us
    ppermute x6, waiting for transfers between devices, x_shift(): return lax.ppermute(value, ('x', 'core'), route)  7.43 us
    ppermute x7, starting transfers between devices, y_shift(): return lax.ppermute(value, ('y_hi', 'y_lo', 'core'), route)  4.53 us
    pallas_call x1, Pallas kernels, prepare(): pl.pallas_call(prepare_kernel, out_shape=jax.ShapeDtypeStruct((2, rows +...  3.96 us
  transfers between devices with their start and end apart: 30, of which 9 were waited for; matrix products, arithmetic and copies ran while one was open for 4% of the time, Pallas kernels for 28%

profile of v1, /device:TPU:1, one launch (start us, length us, event | category | flops | bytes accessed | tf_op | source)
XLA Modules:
  0.0 134.1 jit_solution(2222359832773813077)
XLA Ops:
  0.0 3.2 %collective-permute-start = (bf16[3,96,1536]{2,1,0:T(8,128)(2,1)}, bf16[3,96,1536]{2,1,0:T(8,128)(2,1)S(1)}, u32[]{:S(2)}, u32[]{:S(2)}) collective-permute-start(bf16[3,96,1536]{2,1,0:T(8,128)(2,1)} %bitcast.40), channel_id=1, source_target_pairs={{0,1},{1,0},{2,3},{3,2},{4,5},{5,4},{6,7},{7,6},{8,9},{9,8},{10,11... | collective-permute-start | bytes 2654216 | tf_op jit(solution)/shard_map/ppermute | solution.py:21
  3.2 1.0 collective-permute-start.1
  4.2 0.8 fusion.2
  5.1 1.2 slice_bitcast_fusion.2
  6.4 2.6 %collective-permute-start.21 = (bf16[2,3,96,512]{3,2,1,0:T(8,128)(2,1)S(1)}, bf16[2,3,96,512]{3,2,1,0:T(8,128)(2,1)}, u32[]{:S(2)}, u32[]{:S(2)}) collective-permute-start(bf16[2,3,96,512]{3,2,1,0:T(8,128)(2,1)S(1)} %pad_maximum_fusion.2.refs_1_), channel_id=1, source_target_pairs={{0,4},{1,13},{4,8},{5,1},{8,12},{9,5},{12,0},{13,9},{2,6},{3,15},{... | collective-permute-start | bytes 1769480 | tf_op jit(solution)/shard_map/ppermute | solution.py:28
  9.0 1.9 %collective-permute-start.11 = (bf16[2,1536]{1,0:T(2,128)(2,1)S(1)}, bf16[2,1536]{1,0:T(2,128)(2,1)S(1)}, u32[]{:S(2)}, u32[]{:S(2)}) collective-permute-start(bf16[2,1536]{1,0:T(2,128)(2,1)S(1)} %pad_maximum_fusion.3), channel_id=1, source_target_pairs={{0,1},{1,2},{2,3},{3,4},{4,5},{5,6},{6,7},{7,8},{8,9},{9,10},{10,1... | collective-permute-start | bytes 18440 | tf_op jit(solution)/shard_map/ppermute | solution.py:217
  11.0 0.6 collective-permute-start.13
  11.7 1.3 collective-permute-start.3
  13.0 2.7 %collective-permute-done.1.refs_2_ = bf16[3,96,1536]{2,1,0:T(8,128)(2,1)S(1)} collective-permute-done((bf16[3,96,1536]{2,1,0:T(8,128)(2,1)}, bf16[3,96,1536]{2,1,0:T(8,128)(2,1)S(1)}, u32[]{:S(2)}, u32[]{:S(2)}) %collective-permute-start.1) | collective-permute-done | bytes 884768 | tf_op jit(solution)/shard_map/ppermute | solution.py:35
  15.7 2.0 %collective-permute-start.2 = (bf16[3,96,1536]{2,1,0:T(8,128)(2,1)S(1)}, bf16[3,96,1536]{2,1,0:T(8,128)(2,1)S(1)}, u32[]{:S(2)}, u32[]{:S(2)}) collective-permute-start(bf16[3,96,1536]{2,1,0:T(8,128)(2,1)S(1)} %collective-permute-done.1.refs_2_), channel_id=1, source_target_pairs={{0,1},{1,0},{2,3},{3,2},{4,5},{5,4},{6,7},{7,6},{8,9},{9,8},{10,11... | collective-permute-start | bytes 2654216 | tf_op jit(solution)/shard_map/ppermute | solution.py:21
  17.7 1.9 %collective-permute-start.12 = (bf16[2,1536]{1,0:T(2,128)(2,1)S(1)}, bf16[2,1536]{1,0:T(2,128)(2,1)S(1)}, u32[]{:S(2)}, u32[]{:S(2)}) collective-permute-start(bf16[2,1536]{1,0:T(2,128)(2,1)S(1)} %pad_maximum_fusion.4), channel_id=1, source_target_pairs={{1,0},{2,1},{3,2},{4,3},{5,4},{6,5},{7,6},{8,7},{9,8},{10,9},{11,1... | collective-permute-start | bytes 18440 | tf_op jit(solution)/shard_map/ppermute | solution.py:218
  19.7 1.0 slice_bitcast_fusion
  20.7 1.5 %collective-permute-done.13.refs_4_ = bf16[2,3,96,512]{3,2,1,0:T(8,128)(2,1)} collective-permute-done((bf16[2,3,96,512]{3,2,1,0:T(8,128)(2,1)S(1)}, bf16[2,3,96,512]{3,2,1,0:T(8,128)(2,1)}, u32[]{:S(2)}, u32[]{:S(2)}) %collective-permute-start.13) | collective-permute-done | bytes 589856 | tf_op jit(solution)/shard_map/ppermute | solution.py:28
  22.2 3.2 %collective-permute-start.23 = (bf16[3,96,512]{2,1,0:T(8,128)(2,1)S(1)}, bf16[3,96,512]{2,1,0:T(8,128)(2,1)S(1)}, u32[]{:S(2)}, u32[]{:S(2)}) collective-permute-start(bf16[3,96,512]{2,1,0:T(8,128)(2,1)S(1)} %slice_bitcast_fusion), channel_id=1, source_target_pairs={{0,4},{1,13},{4,8},{5,1},{8,12},{9,5},{12,0},{13,9},{2,6},{3,15},{... | collective-permute-start | bytes 884744 | tf_op jit(solution)/shard_map/ppermute | solution.py:28
  25.4 1.0 slice_bitcast_fusion.3
  26.4 2.1 %collective-permute-done.3.refs_4_ = bf16[2,3,96,512]{3,2,1,0:T(8,128)(2,1)S(1)} collective-permute-done((bf16[2,3,96,512]{3,2,1,0:T(8,128)(2,1)S(1)}, bf16[2,3,96,512]{3,2,1,0:T(8,128)(2,1)S(1)}, u32[]{:S(2)}, u32[]{:S(2)}) %collective-permute-start.3) | collective-permute-done | bytes 589856 | tf_op jit(solution)/shard_map/ppermute | solution.py:28
  28.5 3.1 %collective-permute-start.15 = (bf16[3,96,512]{2,1,0:T(8,128)(2,1)S(1)}, bf16[3,96,512]{2,1,0:T(8,128)(2,1)S(1)}, u32[]{:S(2)}, u32[]{:S(2)}) collective-permute-start(bf16[3,96,512]{2,1,0:T(8,128)(2,1)S(1)} %slice_bitcast_fusion.3), channel_id=1, source_target_pairs={{0,4},{1,13},{4,8},{5,1},{8,12},{9,5},{12,0},{13,9},{2,6},{3,15},{... | collective-permute-start | bytes 884744 | tf_op jit(solution)/shard_map/ppermute | solution.py:28
  31.7 0.5 collective-permute-start.25
  32.5 1.4 %collective-permute-start.24 = (bf16[3,96,512]{2,1,0:T(8,128)(2,1)S(1)}, bf16[3,96,512]{2,1,0:T(8,128)(2,1)S(1)}, u32[]{:S(2)}, u32[]{:S(2)}) collective-permute-start(bf16[3,96,512]{2,1,0:T(8,128)(2,1)S(1)} %collective-permute-done.23.refs_6_), channel_id=1, source_target_pairs={{0,1},{1,0},{2,3},{3,2},{4,5},{5,4},{6,7},{7,6},{8,9},{9,8},{10,11... | collective-permute-start | bytes 884744 | tf_op jit(solution)/shard_map/ppermute | solution.py:21
  33.9 1.4 %collective-permute-done.15.refs_6_ = bf16[3,96,512]{2,1,0:T(8,128)(2,1)S(1)} collective-permute-done((bf16[3,96,512]{2,1,0:T(8,128)(2,1)S(1)}, bf16[3,96,512]{2,1,0:T(8,128)(2,1)S(1)}, u32[]{:S(2)}, u32[]{:S(2)}) %collective-permute-start.15) | collective-permute-done | bytes 294944 | tf_op jit(solution)/shard_map/ppermute | solution.py:28
  35.3 0.7 collective-permute-start.19
  36.0 2.4 %collective-permute-done.5.refs_6_ = bf16[3,96,512]{2,1,0:T(8,128)(2,1)S(1)} collective-permute-done((bf16[3,96,512]{2,1,0:T(8,128)(2,1)S(1)}, bf16[3,96,512]{2,1,0:T(8,128)(2,1)S(1)}, u32[]{:S(2)}, u32[]{:S(2)}) %collective-permute-start.5) | collective-permute-done | bytes 294944 | tf_op jit(solution)/shard_map/ppermute | solution.py:28
  38.4 2.5 %collective-permute-start.16 = (bf16[3,96,512]{2,1,0:T(8,128)(2,1)S(1)}, bf16[3,96,512]{2,1,0:T(8,128)(2,1)S(1)}, u32[]{:S(2)}, u32[]{:S(2)}) collective-permute-start(bf16[3,96,512]{2,1,0:T(8,128)(2,1)S(1)} %collective-permute-done.15.refs_6_), channel_id=1, source_target_pairs={{0,1},{1,0},{2,3},{3,2},{4,5},{5,4},{6,7},{7,6},{8,9},{9,8},{10,11... | collective-permute-start | bytes 884744 | tf_op jit(solution)/shard_map/ppermute | solution.py:21
  40.9 3.4 %collective-permute-done.27.refs_10_ = bf16[3,96,512]{2,1,0:T(8,128)(2,1)} collective-permute-done((bf16[3,96,512]{2,1,0:T(8,128)(2,1)S(1)}, bf16[3,96,512]{2,1,0:T(8,128)(2,1)}, u32[]{:S(2)}, u32[]{:S(2)}) %collective-permute-start.27) | collective-permute-done | bytes 294944 | tf_op jit(solution)/shard_map/ppermute | solution.py:35
  44.3 1.2 collective-permute-start.22
  45.6 0.6 collective-permute-start.17
  46.3 1.1 collective-permute-done.19.refs_10_
  47.4 1.4 %collective-permute-start.7 = (bf16[2,3,96,512]{3,2,1,0:T(8,128)(2,1)S(1)}, bf16[2,3,96,512]{3,2,1,0:T(8,128)(2,1)S(1)}, u32[]{:S(2)}, u32[]{:S(2)}) collective-permute-start(bf16[2,3,96,512]{3,2,1,0:T(8,128)(2,1)S(1)} %collective-permute-done.3.refs_4_), channel_id=1, source_target_pairs={{0,2},{1,131},{2,128},{3,1},{128,130},{129,3},{130,0},{131,129},{4... | collective-permute-start | bytes 1769480 | tf_op jit(solution)/shard_map/ppermute | solution.py:35
  48.9 1.5 %collective-permute-start.26 = (bf16[2,3,96,512]{3,2,1,0:T(8,128)(2,1)}, bf16[2,3,96,512]{3,2,1,0:T(8,128)(2,1)}, u32[]{:S(2)}, u32[]{:S(2)}) collective-permute-start(bf16[2,3,96,512]{3,2,1,0:T(8,128)(2,1)} %collective-permute-done.25.refs_8_), channel_id=1, source_target_pairs={{0,1},{1,0},{2,3},{3,2},{4,5},{5,4},{6,7},{7,6},{8,9},{9,8},{10,11... | collective-permute-start | bytes 1769480 | tf_op jit(solution)/shard_map/ppermute | solution.py:21
  50.4 13.9 %collective-permute-done.9.refs_10_ = bf16[3,96,512]{2,1,0:T(8,128)(2,1)S(1)} collective-permute-done((bf16[3,96,512]{2,1,0:T(8,128)(2,1)S(1)}, bf16[3,96,512]{2,1,0:T(8,128)(2,1)S(1)}, u32[]{:S(2)}, u32[]{:S(2)}) %collective-permute-start.9) | collective-permute-done | bytes 294944 | tf_op jit(solution)/shard_map/ppermute | solution.py:35
  64.3 0.7 copy-done.10
  65.0 2.1 %collective-permute-start.28 = (bf16[3,96,512]{2,1,0:T(8,128)(2,1)}, bf16[3,96,512]{2,1,0:T(8,128)(2,1)}, u32[]{:S(2)}, u32[]{:S(2)}) collective-permute-start(bf16[3,96,512]{2,1,0:T(8,128)(2,1)} %collective-permute-done.27.refs_10_), channel_id=1, source_target_pairs={{0,1},{1,0},{2,3},{3,2},{4,5},{5,4},{6,7},{7,6},{8,9},{9,8},{10,11... | collective-permute-start | bytes 884744 | tf_op jit(solution)/shard_map/ppermute | solution.py:21
  67.3 0.6 stack.100.refs_0_
  67.9 0.5 collective-permute-start.18
  68.4 0.6 fusion.4
  69.0 4.0 %prepare.1.refs_12_ = bf16[2,400,1536]{2,1,0:T(8,128)(2,1)} custom-call(bf16[384,1536]{1,0:T(8,128)(2,1)} %forward_ref.1, bf16[384,1536]{1,0:T(8,128)(2,1)} %reverse_ref.1, bf16[2,1536]{1,0:T(2,128)(2,1)} %copy-done.23, bf16[2,1536]{1,0:T(2,128)(2,1)} %copy-done.24), custom_call_target="tpu_custom_call" | custom-call | flops 452984832 | bytes 4718592 | tf_op jit(solution)/shard_map/prepare/pallas_call | solution.py:58
  73.2 0.4 collective-permute-start.20
  73.7 11.9 %chunk.2.refs_16_ = f32[2,384,1024]{2,1,0:T(8,128)} custom-call(s32[16]{0:T(128)} %stack.100.refs_0_, bf16[2,3,96,512]{3,2,1,0:T(8,128)(2,1)} %copy-done.16, bf16[3,96,1536]{2,1,0:T(8,128)(2,1)} %copy-done, bf16[3,96,1536]{2,1,0:T(8,128)(2,1)} %copy-done.1, bf16[2,3,96,512]{3,2,1,0:T(8,128)(2,1)} %collective-permute-done.21.refs_4_, ...), custom_call_target="tpu_custom_call" | custom-call | flops 4429185024 | bytes 7864320 | tf_op jit(solution)/shard_map/chunk/pallas_call | solution.py:183
  85.7 0.5 collective-permute-start.6
  86.1 0.4 collective-permute-start.10
  86.9 0.5 copy-done.15
  87.4 12.1 %chunk.3.refs_16_ = f32[2,384,1024]{2,1,0:T(8,128)} custom-call(s32[16]{0:T(128)} %stack.100.refs_0_, bf16[2,3,96,512]{3,2,1,0:T(8,128)(2,1)} %copy-done.7, bf16[3,96,1536]{2,1,0:T(8,128)(2,1)} %copy-done, bf16[3,96,1536]{2,1,0:T(8,128)(2,1)} %copy-done.1, bf16[2,3,96,512]{3,2,1,0:T(8,128)(2,1)} %collective-permute-done.13.refs_4_, ...), custom_call_target="tpu_custom_call" | custom-call | flops 4429185024 | bytes 7864320 | tf_op jit(solution)/shard_map/chunk/pallas_call | solution.py:183
  99.6 0.6 copy-done.12
  100.8 9.1 %chunk_last.3 = bf16[1,384,1024]{2,1,0:T(8,128)(2,1)} custom-call(s32[16]{0:T(128)} %stack.100.refs_0_, bf16[2,3,96,512]{3,2,1,0:T(8,128)(2,1)} %copy-done.2, bf16[3,96,1536]{2,1,0:T(8,128)(2,1)} %copy-done, bf16[3,96,1536]{2,1,0:T(8,128)(2,1)} %copy-done.1, bf16[2,3,96,512]{3,2,1,0:T(8,128)(2,1)} %copy-done.3, bf16[2,3,96,512]{3,2,1,0:T(8,128)(2,1)} %copy-done.5, ...), custom_call_target="tpu_custom_call" | custom-call | flops 2214592512 | bytes 6291456 | tf_op jit(solution)/shard_map/chunk_last/pallas_call | solution.py:183
  109.9 0.6 collective-permute-start.29
  110.5 9.1 %chunk_last.2 = bf16[1,384,1024]{2,1,0:T(8,128)(2,1)} custom-call(s32[16]{0:T(128)} %stack.100.refs_0_, bf16[2,3,96,512]{3,2,1,0:T(8,128)(2,1)} %copy-done.2, bf16[3,96,1536]{2,1,0:T(8,128)(2,1)} %copy-done, bf16[3,96,1536]{2,1,0:T(8,128)(2,1)} %copy-done.1, bf16[2,3,96,512]{3,2,1,0:T(8,128)(2,1)} %copy-done.3, bf16[2,3,96,512]{3,2,1,0:T(8,128)(2,1)} %copy-done.5, ...), custom_call_target="tpu_custom_call" | custom-call | flops 2214592512 | bytes 6291456 | tf_op jit(solution)/shard_map/chunk_last/pallas_call | solution.py:183
  119.6 12.2 %collective-permute-done.29 = bf16[384,1024]{1,0:T(8,128)(2,1)S(1)} collective-permute-done((bf16[384,1024]{1,0:T(8,128)(2,1)}, bf16[384,1024]{1,0:T(8,128)(2,1)S(1)}, u32[]{:S(2)}, u32[]{:S(2)}) %collective-permute-start.29) | collective-permute-done | bytes 786464 | tf_op jit(solution)/shard_map/ppermute | solution.py:269
  131.8 2.3 %fusion.1 = bf16[384,1024]{1,0:T(8,128)(2,1)} fusion(bf16[384,1024]{1,0:T(8,128)(2,1)S(1)} %collective-permute-done.29, bf16[1,384,1024]{2,1,0:T(8,128)(2,1)} %chunk_last.2), kind=kLoop, calls=%fused_computation.2 | loop fusion | flops 1966080 | bytes 2359296 | tf_op jit(solution)/shard_map/convert_element_type | solution.py:271
  (85 shorter events, 2.1 us)
Async XLA Ops:
  0.0 6.3 %collective-permute-start = (bf16[3,96,1536]{2,1,0:T(8,128)(2,1)}, bf16[3,96,1536]{2,1,0:T(8,128)(2,1)S(1)}, u32[]{:S(2)}, u32[]{:S(2)}) collective-permute-start(bf16[3,96,1536]{2,1,0:T(8,128)(2,1)} %bitcast.40), channel_id=1, source_target_pairs={{0,1},{1,0},{2,3},{3,2},{4,5},{5,4},{6,7},{7,6},{8,9},{9,8},{10,11... | collective-permute-start | bytes 2654216 | tf_op jit(solution)/shard_map/ppermute | solution.py:21
  3.2 12.5 %collective-permute-start.1 = (bf16[3,96,1536]{2,1,0:T(8,128)(2,1)}, bf16[3,96,1536]{2,1,0:T(8,128)(2,1)S(1)}, u32[]{:S(2)}, u32[]{:S(2)}) collective-permute-start(bf16[3,96,1536]{2,1,0:T(8,128)(2,1)} %bitcast.41), channel_id=1, source_target_pairs={{0,2},{1,131},{2,128},{3,1},{128,130},{129,3},{130,0},{131,129},{4... | collective-permute-start | bytes 2654216 | tf_op jit(solution)/shard_map/ppermute | solution.py:35
  6.4 19.9 %copy-start.16 = (bf16[2,3,96,512]{3,2,1,0:T(8,128)(2,1)}, bf16[2,3,96,512]{3,2,1,0:T(8,128)(2,1)S(1)}, u32[]{:S(2)}) copy-start(bf16[2,3,96,512]{3,2,1,0:T(8,128)(2,1)S(1)} %pad_maximum_fusion.2.refs_1_) | copy-start | bytes 1769476
  6.4 11.3 %collective-permute-start.21 = (bf16[2,3,96,512]{3,2,1,0:T(8,128)(2,1)S(1)}, bf16[2,3,96,512]{3,2,1,0:T(8,128)(2,1)}, u32[]{:S(2)}, u32[]{:S(2)}) collective-permute-start(bf16[2,3,96,512]{3,2,1,0:T(8,128)(2,1)S(1)} %pad_maximum_fusion.2.refs_1_), channel_id=1, source_target_pairs={{0,4},{1,13},{4,8},{5,1},{8,12},{9,5},{12,0},{13,9},{2,6},{3,15},{... | collective-permute-start | bytes 1769480 | tf_op jit(solution)/shard_map/ppermute | solution.py:28
  9.0 22.6 %collective-permute-start.11 = (bf16[2,1536]{1,0:T(2,128)(2,1)S(1)}, bf16[2,1536]{1,0:T(2,128)(2,1)S(1)}, u32[]{:S(2)}, u32[]{:S(2)}) collective-permute-start(bf16[2,1536]{1,0:T(2,128)(2,1)S(1)} %pad_maximum_fusion.3), channel_id=1, source_target_pairs={{0,1},{1,2},{2,3},{3,4},{4,5},{5,6},{6,7},{7,8},{8,9},{9,10},{10,1... | collective-permute-start | bytes 18440 | tf_op jit(solution)/shard_map/ppermute | solution.py:217
  11.0 35.2 %copy-start.7 = (bf16[2,3,96,512]{3,2,1,0:T(8,128)(2,1)}, bf16[2,3,96,512]{3,2,1,0:T(8,128)(2,1)S(1)}, u32[]{:S(2)}) copy-start(bf16[2,3,96,512]{3,2,1,0:T(8,128)(2,1)S(1)} %pad_maximum_fusion.1.refs_1_) | copy-start | bytes 1769476
  11.0 11.1 %collective-permute-start.13 = (bf16[2,3,96,512]{3,2,1,0:T(8,128)(2,1)S(1)}, bf16[2,3,96,512]{3,2,1,0:T(8,128)(2,1)}, u32[]{:S(2)}, u32[]{:S(2)}) collective-permute-start(bf16[2,3,96,512]{3,2,1,0:T(8,128)(2,1)S(1)} %pad_maximum_fusion.1.refs_1_), channel_id=1, source_target_pairs={{0,4},{1,13},{4,8},{5,1},{8,12},{9,5},{12,0},{13,9},{2,6},{3,15},{... | collective-permute-start | bytes 1769480 | tf_op jit(solution)/shard_map/ppermute | solution.py:28
  11.7 56.7 %copy-start.22 = (f32[1,1536]{1,0:T(1,128)S(1)}, f32[1,1536]{1,0:T(1,128)}, u32[]{:S(2)}) copy-start(f32[1,1536]{1,0:T(1,128)} %param.9) | copy-start | bytes 18436
  11.7 61.2 %copy-start.2 = (bf16[2,3,96,512]{3,2,1,0:T(8,128)(2,1)}, bf16[2,3,96,512]{3,2,1,0:T(8,128)(2,1)S(1)}, u32[]{:S(2)}) copy-start(bf16[2,3,96,512]{3,2,1,0:T(8,128)(2,1)S(1)} %pad_maximum_fusion.refs_1_) | copy-start | bytes 1769476
  11.7 16.7 %collective-permute-start.3 = (bf16[2,3,96,512]{3,2,1,0:T(8,128)(2,1)S(1)}, bf16[2,3,96,512]{3,2,1,0:T(8,128)(2,1)S(1)}, u32[]{:S(2)}, u32[]{:S(2)}) collective-permute-start(bf16[2,3,96,512]{3,2,1,0:T(8,128)(2,1)S(1)} %pad_maximum_fusion.refs_1_), channel_id=1, source_target_pairs={{0,4},{1,13},{4,8},{5,1},{8,12},{9,5},{12,0},{13,9},{2,6},{3,15},{... | collective-permute-start | bytes 1769480 | tf_op jit(solution)/shard_map/ppermute | solution.py:28
  15.7 57.2 %copy-start = (bf16[3,96,1536]{2,1,0:T(8,128)(2,1)}, bf16[3,96,1536]{2,1,0:T(8,128)(2,1)S(1)}, u32[]{:S(2)}) copy-start(bf16[3,96,1536]{2,1,0:T(8,128)(2,1)S(1)} %collective-permute-done.1.refs_2_) | copy-start | bytes 2654212
  15.7 16.8 %collective-permute-start.2 = (bf16[3,96,1536]{2,1,0:T(8,128)(2,1)S(1)}, bf16[3,96,1536]{2,1,0:T(8,128)(2,1)S(1)}, u32[]{:S(2)}, u32[]{:S(2)}) collective-permute-start(bf16[3,96,1536]{2,1,0:T(8,128)(2,1)S(1)} %collective-permute-done.1.refs_2_), channel_id=1, source_target_pairs={{0,1},{1,0},{2,3},{3,2},{4,5},{5,4},{6,7},{7,6},{8,9},{9,8},{10,11... | collective-permute-start | bytes 2654216 | tf_op jit(solution)/shard_map/ppermute | solution.py:21
  17.7 14.0 %collective-permute-start.12 = (bf16[2,1536]{1,0:T(2,128)(2,1)S(1)}, bf16[2,1536]{1,0:T(2,128)(2,1)S(1)}, u32[]{:S(2)}, u32[]{:S(2)}) collective-permute-start(bf16[2,1536]{1,0:T(2,128)(2,1)S(1)} %pad_maximum_fusion.4), channel_id=1, source_target_pairs={{1,0},{2,1},{3,2},{4,3},{5,4},{6,5},{7,6},{8,7},{9,8},{10,9},{11,1... | collective-permute-start | bytes 18440 | tf_op jit(solution)/shard_map/ppermute | solution.py:218
  22.2 10.1 %collective-permute-start.23 = (bf16[3,96,512]{2,1,0:T(8,128)(2,1)S(1)}, bf16[3,96,512]{2,1,0:T(8,128)(2,1)S(1)}, u32[]{:S(2)}, u32[]{:S(2)}) collective-permute-start(bf16[3,96,512]{2,1,0:T(8,128)(2,1)S(1)} %slice_bitcast_fusion), channel_id=1, source_target_pairs={{0,4},{1,13},{4,8},{5,1},{8,12},{9,5},{12,0},{13,9},{2,6},{3,15},{... | collective-permute-start | bytes 884744 | tf_op jit(solution)/shard_map/ppermute | solution.py:28
  28.5 44.5 %copy-start.3 = (bf16[2,3,96,512]{3,2,1,0:T(8,128)(2,1)}, bf16[2,3,96,512]{3,2,1,0:T(8,128)(2,1)S(1)}, u32[]{:S(2)}) copy-start(bf16[2,3,96,512]{3,2,1,0:T(8,128)(2,1)S(1)} %collective-permute-done.3.refs_4_) | copy-start | bytes 1769476
  28.5 6.8 %collective-permute-start.15 = (bf16[3,96,512]{2,1,0:T(8,128)(2,1)S(1)}, bf16[3,96,512]{2,1,0:T(8,128)(2,1)S(1)}, u32[]{:S(2)}, u32[]{:S(2)}) collective-permute-start(bf16[3,96,512]{2,1,0:T(8,128)(2,1)S(1)} %slice_bitcast_fusion.3), channel_id=1, source_target_pairs={{0,4},{1,13},{4,8},{5,1},{8,12},{9,5},{12,0},{13,9},{2,6},{3,15},{... | collective-permute-start | bytes 884744 | tf_op jit(solution)/shard_map/ppermute | solution.py:28
  31.6 37.4 %copy-start.23 = (bf16[2,1536]{1,0:T(2,128)(2,1)}, bf16[2,1536]{1,0:T(2,128)(2,1)S(1)}, u32[]{:S(2)}) copy-start(bf16[2,1536]{1,0:T(2,128)(2,1)S(1)} %collective-permute-done.11.low_ref) | copy-start | bytes 18436
  31.6 6.8 %collective-permute-start.5 = (bf16[3,96,512]{2,1,0:T(8,128)(2,1)S(1)}, bf16[3,96,512]{2,1,0:T(8,128)(2,1)S(1)}, u32[]{:S(2)}, u32[]{:S(2)}) collective-permute-start(bf16[3,96,512]{2,1,0:T(8,128)(2,1)S(1)} %slice_bitcast_fusion.6), channel_id=1, source_target_pairs={{0,4},{1,13},{4,8},{5,1},{8,12},{9,5},{12,0},{13,9},{2,6},{3,15},{... | collective-permute-start | bytes 884744 | tf_op jit(solution)/shard_map/ppermute | solution.py:28
  31.7 14.4 %copy-start.24 = (bf16[2,1536]{1,0:T(2,128)(2,1)}, bf16[2,1536]{1,0:T(2,128)(2,1)S(1)}, u32[]{:S(2)}) copy-start(bf16[2,1536]{1,0:T(2,128)(2,1)S(1)} %collective-permute-done.12.high_ref) | copy-start | bytes 18436
  31.7 17.1 %collective-permute-start.25 = (bf16[2,3,96,512]{3,2,1,0:T(8,128)(2,1)}, bf16[2,3,96,512]{3,2,1,0:T(8,128)(2,1)}, u32[]{:S(2)}, u32[]{:S(2)}) collective-permute-start(bf16[2,3,96,512]{3,2,1,0:T(8,128)(2,1)} %collective-permute-done.21.refs_4_), channel_id=1, source_target_pairs={{0,2},{1,131},{2,128},{3,1},{128,130},{129,3},{130,0},{131,129},{4... | collective-permute-start | bytes 1769480 | tf_op jit(solution)/shard_map/ppermute | solution.py:35
  32.3 34.9 %copy-start.25 = (bf16[3,96,512]{2,1,0:T(8,128)(2,1)}, bf16[3,96,512]{2,1,0:T(8,128)(2,1)S(1)}, u32[]{:S(2)}) copy-start(bf16[3,96,512]{2,1,0:T(8,128)(2,1)S(1)} %collective-permute-done.23.refs_6_) | copy-start | bytes 884740
  32.3 12.0 %collective-permute-start.27 = (bf16[3,96,512]{2,1,0:T(8,128)(2,1)S(1)}, bf16[3,96,512]{2,1,0:T(8,128)(2,1)}, u32[]{:S(2)}, u32[]{:S(2)}) collective-permute-start(bf16[3,96,512]{2,1,0:T(8,128)(2,1)S(1)} %collective-permute-done.23.refs_6_), channel_id=1, source_target_pairs={{0,2},{1,131},{2,128},{3,1},{128,130},{129,3},{130,0},{131,129},{4... | collective-permute-start | bytes 884744 | tf_op jit(solution)/shard_map/ppermute | solution.py:35
  32.5 40.5 %copy-start.1 = (bf16[3,96,1536]{2,1,0:T(8,128)(2,1)}, bf16[3,96,1536]{2,1,0:T(8,128)(2,1)S(1)}, u32[]{:S(2)}) copy-start(bf16[3,96,1536]{2,1,0:T(8,128)(2,1)S(1)} %collective-permute-done.2.refs_3_) | copy-start | bytes 2654212
  32.5 13.1 %collective-permute-start.24 = (bf16[3,96,512]{2,1,0:T(8,128)(2,1)S(1)}, bf16[3,96,512]{2,1,0:T(8,128)(2,1)S(1)}, u32[]{:S(2)}, u32[]{:S(2)}) collective-permute-start(bf16[3,96,512]{2,1,0:T(8,128)(2,1)S(1)} %collective-permute-done.23.refs_6_), channel_id=1, source_target_pairs={{0,1},{1,0},{2,3},{3,2},{4,5},{5,4},{6,7},{7,6},{8,9},{9,8},{10,11... | collective-permute-start | bytes 884744 | tf_op jit(solution)/shard_map/ppermute | solution.py:21
  35.3 31.9 %copy-start.17 = (bf16[3,96,512]{2,1,0:T(8,128)(2,1)}, bf16[3,96,512]{2,1,0:T(8,128)(2,1)S(1)}, u32[]{:S(2)}) copy-start(bf16[3,96,512]{2,1,0:T(8,128)(2,1)S(1)} %collective-permute-done.15.refs_6_) | copy-start | bytes 884740
  35.3 12.1 %collective-permute-start.19 = (bf16[3,96,512]{2,1,0:T(8,128)(2,1)S(1)}, bf16[3,96,512]{2,1,0:T(8,128)(2,1)S(1)}, u32[]{:S(2)}, u32[]{:S(2)}) collective-permute-start(bf16[3,96,512]{2,1,0:T(8,128)(2,1)S(1)} %collective-permute-done.15.refs_6_), channel_id=1, source_target_pairs={{0,2},{1,131},{2,128},{3,1},{128,130},{129,3},{130,0},{131,129},{4... | collective-permute-start | bytes 884744 | tf_op jit(solution)/shard_map/ppermute | solution.py:35
  38.4 10.4 %copy-start.8 = (bf16[3,96,512]{2,1,0:T(8,128)(2,1)}, bf16[3,96,512]{2,1,0:T(8,128)(2,1)S(1)}, u32[]{:S(2)}) copy-start(bf16[3,96,512]{2,1,0:T(8,128)(2,1)S(1)} %collective-permute-done.5.refs_6_) | copy-start | bytes 884740
  38.4 10.3 %collective-permute-start.16 = (bf16[3,96,512]{2,1,0:T(8,128)(2,1)S(1)}, bf16[3,96,512]{2,1,0:T(8,128)(2,1)S(1)}, u32[]{:S(2)}, u32[]{:S(2)}) collective-permute-start(bf16[3,96,512]{2,1,0:T(8,128)(2,1)S(1)} %collective-permute-done.15.refs_6_), channel_id=1, source_target_pairs={{0,1},{1,0},{2,3},{3,2},{4,5},{5,4},{6,7},{7,6},{8,9},{9,8},{10,11... | collective-permute-start | bytes 884744 | tf_op jit(solution)/shard_map/ppermute | solution.py:21
  44.3 23.6 %collective-permute-start.22 = (bf16[2,3,96,512]{3,2,1,0:T(8,128)(2,1)}, bf16[2,3,96,512]{3,2,1,0:T(8,128)(2,1)}, u32[]{:S(2)}, u32[]{:S(2)}) collective-permute-start(bf16[2,3,96,512]{3,2,1,0:T(8,128)(2,1)} %collective-permute-done.21.refs_4_), channel_id=1, source_target_pairs={{0,1},{1,0},{2,3},{3,2},{4,5},{5,4},{6,7},{7,6},{8,9},{9,8},{10,11... | collective-permute-start | bytes 1769480 | tf_op jit(solution)/shard_map/ppermute | solution.py:21
  45.6 22.3 %collective-permute-start.17 = (bf16[2,3,96,512]{3,2,1,0:T(8,128)(2,1)}, bf16[2,3,96,512]{3,2,1,0:T(8,128)(2,1)}, u32[]{:S(2)}, u32[]{:S(2)}) collective-permute-start(bf16[2,3,96,512]{3,2,1,0:T(8,128)(2,1)} %collective-permute-done.13.refs_4_), channel_id=1, source_target_pairs={{0,2},{1,131},{2,128},{3,1},{128,130},{129,3},{130,0},{131,129},{4... | collective-permute-start | bytes 1769480 | tf_op jit(solution)/shard_map/ppermute | solution.py:35
  47.4 19.8 %copy-start.18 = (bf16[3,96,512]{2,1,0:T(8,128)(2,1)}, bf16[3,96,512]{2,1,0:T(8,128)(2,1)S(1)}, u32[]{:S(2)}) copy-start(bf16[3,96,512]{2,1,0:T(8,128)(2,1)S(1)} %collective-permute-done.19.refs_10_) | copy-start | bytes 884740
  47.4 25.6 %collective-permute-start.7 = (bf16[2,3,96,512]{3,2,1,0:T(8,128)(2,1)S(1)}, bf16[2,3,96,512]{3,2,1,0:T(8,128)(2,1)S(1)}, u32[]{:S(2)}, u32[]{:S(2)}) collective-permute-start(bf16[2,3,96,512]{3,2,1,0:T(8,128)(2,1)S(1)} %collective-permute-done.3.refs_4_), channel_id=1, source_target_pairs={{0,2},{1,131},{2,128},{3,1},{128,130},{129,3},{130,0},{131,129},{4... | collective-permute-start | bytes 1769480 | tf_op jit(solution)/shard_map/ppermute | solution.py:35
  48.8 18.4 %copy-start.20 = (bf16[3,96,512]{2,1,0:T(8,128)(2,1)}, bf16[3,96,512]{2,1,0:T(8,128)(2,1)S(1)}, u32[]{:S(2)}) copy-start(bf16[3,96,512]{2,1,0:T(8,128)(2,1)S(1)} %collective-permute-done.16.refs_7_) | copy-start | bytes 884740
  48.8 15.5 %collective-permute-start.9 = (bf16[3,96,512]{2,1,0:T(8,128)(2,1)S(1)}, bf16[3,96,512]{2,1,0:T(8,128)(2,1)S(1)}, u32[]{:S(2)}, u32[]{:S(2)}) collective-permute-start(bf16[3,96,512]{2,1,0:T(8,128)(2,1)S(1)} %collective-permute-done.5.refs_6_), channel_id=1, source_target_pairs={{0,2},{1,131},{2,128},{3,1},{128,130},{129,3},{130,0},{131,129},{4... | collective-permute-start | bytes 884744 | tf_op jit(solution)/shard_map/ppermute | solution.py:35
  48.9 24.7 %collective-permute-start.26 = (bf16[2,3,96,512]{3,2,1,0:T(8,128)(2,1)}, bf16[2,3,96,512]{3,2,1,0:T(8,128)(2,1)}, u32[]{:S(2)}, u32[]{:S(2)}) collective-permute-start(bf16[2,3,96,512]{3,2,1,0:T(8,128)(2,1)} %collective-permute-done.25.refs_8_), channel_id=1, source_target_pairs={{0,1},{1,0},{2,3},{3,2},{4,5},{5,4},{6,7},{7,6},{8,9},{9,8},{10,11... | collective-permute-start | bytes 1769480 | tf_op jit(solution)/shard_map/ppermute | solution.py:21
  65.0 8.2 %collective-permute-start.28 = (bf16[3,96,512]{2,1,0:T(8,128)(2,1)}, bf16[3,96,512]{2,1,0:T(8,128)(2,1)}, u32[]{:S(2)}, u32[]{:S(2)}) collective-permute-start(bf16[3,96,512]{2,1,0:T(8,128)(2,1)} %collective-permute-done.27.refs_10_), channel_id=1, source_target_pairs={{0,1},{1,0},{2,3},{3,2},{4,5},{5,4},{6,7},{7,6},{8,9},{9,8},{10,11... | collective-permute-start | bytes 884744 | tf_op jit(solution)/shard_map/ppermute | solution.py:21
  67.9 17.7 %collective-permute-start.14 = (bf16[2,3,96,512]{3,2,1,0:T(8,128)(2,1)}, bf16[2,3,96,512]{3,2,1,0:T(8,128)(2,1)S(1)}, u32[]{:S(2)}, u32[]{:S(2)}) collective-permute-start(bf16[2,3,96,512]{3,2,1,0:T(8,128)(2,1)} %collective-permute-done.13.refs_4_), channel_id=1, source_target_pairs={{0,1},{1,0},{2,3},{3,2},{4,5},{5,4},{6,7},{7,6},{8,9},{9,8},{10,11... | collective-permute-start | bytes 1769480 | tf_op jit(solution)/shard_map/ppermute | solution.py:21
  67.9 18.7 %collective-permute-start.18 = (bf16[2,3,96,512]{3,2,1,0:T(8,128)(2,1)}, bf16[2,3,96,512]{3,2,1,0:T(8,128)(2,1)S(1)}, u32[]{:S(2)}, u32[]{:S(2)}) collective-permute-start(bf16[2,3,96,512]{3,2,1,0:T(8,128)(2,1)} %collective-permute-done.17.refs_8_), channel_id=1, source_target_pairs={{0,1},{1,0},{2,3},{3,2},{4,5},{5,4},{6,7},{7,6},{8,9},{9,8},{10,11... | collective-permute-start | bytes 1769480 | tf_op jit(solution)/shard_map/ppermute | solution.py:21
  69.0 4.2 %copy-start.19 = (bf16[3,96,512]{2,1,0:T(8,128)(2,1)S(1)}, bf16[3,96,512]{2,1,0:T(8,128)(2,1)}, u32[]{:S(2)}) copy-start(bf16[3,96,512]{2,1,0:T(8,128)(2,1)} %copy-done.18) | copy-start | bytes 884740
  73.0 12.6 %copy-start.4 = (bf16[2,3,96,512]{3,2,1,0:T(8,128)(2,1)}, bf16[2,3,96,512]{3,2,1,0:T(8,128)(2,1)S(1)}, u32[]{:S(2)}) copy-start(bf16[2,3,96,512]{3,2,1,0:T(8,128)(2,1)S(1)} %collective-permute-done.7.refs_8_) | copy-start | bytes 1769476
  73.0 26.6 %collective-permute-start.4 = (bf16[2,3,96,512]{3,2,1,0:T(8,128)(2,1)S(1)}, bf16[2,3,96,512]{3,2,1,0:T(8,128)(2,1)S(1)}, u32[]{:S(2)}, u32[]{:S(2)}) collective-permute-start(bf16[2,3,96,512]{3,2,1,0:T(8,128)(2,1)S(1)} %collective-permute-done.3.refs_4_), channel_id=1, source_target_pairs={{0,1},{1,0},{2,3},{3,2},{4,5},{5,4},{6,7},{7,6},{8,9},{9,8},{10,11... | collective-permute-start | bytes 1769480 | tf_op jit(solution)/shard_map/ppermute | solution.py:21
  73.2 13.0 %collective-permute-start.20 = (bf16[3,96,512]{2,1,0:T(8,128)(2,1)S(1)}, bf16[3,96,512]{2,1,0:T(8,128)(2,1)S(1)}, u32[]{:S(2)}, u32[]{:S(2)}) collective-permute-start(bf16[3,96,512]{2,1,0:T(8,128)(2,1)S(1)} %copy-done.19), channel_id=1, source_target_pairs={{0,1},{1,0},{2,3},{3,2},{4,5},{5,4},{6,7},{7,6},{8,9},{9,8},{10,11... | collective-permute-start | bytes 884744 | tf_op jit(solution)/shard_map/ppermute | solution.py:21
  73.6 26.0 %collective-permute-start.8 = (bf16[2,3,96,512]{3,2,1,0:T(8,128)(2,1)S(1)}, bf16[2,3,96,512]{3,2,1,0:T(8,128)(2,1)S(1)}, u32[]{:S(2)}, u32[]{:S(2)}) collective-permute-start(bf16[2,3,96,512]{3,2,1,0:T(8,128)(2,1)S(1)} %collective-permute-done.7.refs_8_), channel_id=1, source_target_pairs={{0,1},{1,0},{2,3},{3,2},{4,5},{5,4},{6,7},{7,6},{8,9},{9,8},{10,11... | collective-permute-start | bytes 1769480 | tf_op jit(solution)/shard_map/ppermute | solution.py:21
  73.7 11.9 %copy-start.9 = (bf16[3,96,512]{2,1,0:T(8,128)(2,1)S(1)}, bf16[3,96,512]{2,1,0:T(8,128)(2,1)}, u32[]{:S(2)}) copy-start(bf16[3,96,512]{2,1,0:T(8,128)(2,1)} %copy-done.8) | copy-start | bytes 884740
  73.7 12.4 %copy-start.11 = (bf16[3,96,512]{2,1,0:T(8,128)(2,1)S(1)}, bf16[3,96,512]{2,1,0:T(8,128)(2,1)}, u32[]{:S(2)}) copy-start(bf16[3,96,512]{2,1,0:T(8,128)(2,1)} %copy-done.10) | copy-start | bytes 884740
  85.7 13.9 %collective-permute-start.6 = (bf16[3,96,512]{2,1,0:T(8,128)(2,1)S(1)}, bf16[3,96,512]{2,1,0:T(8,128)(2,1)S(1)}, u32[]{:S(2)}, u32[]{:S(2)}) collective-permute-start(bf16[3,96,512]{2,1,0:T(8,128)(2,1)S(1)} %copy-done.9), channel_id=1, source_target_pairs={{0,1},{1,0},{2,3},{3,2},{4,5},{5,4},{6,7},{7,6},{8,9},{9,8},{10,11... | collective-permute-start | bytes 884744 | tf_op jit(solution)/shard_map/ppermute | solution.py:21
  86.1 13.4 %collective-permute-start.10 = (bf16[3,96,512]{2,1,0:T(8,128)(2,1)S(1)}, bf16[3,96,512]{2,1,0:T(8,128)(2,1)S(1)}, u32[]{:S(2)}, u32[]{:S(2)}) collective-permute-start(bf16[3,96,512]{2,1,0:T(8,128)(2,1)S(1)} %copy-done.11), channel_id=1, source_target_pairs={{0,1},{1,0},{2,3},{3,2},{4,5},{5,4},{6,7},{7,6},{8,9},{9,8},{10,11... | collective-permute-start | bytes 884744 | tf_op jit(solution)/shard_map/ppermute | solution.py:21
  109.9 22.0 %collective-permute-start.29 = (bf16[384,1024]{1,0:T(8,128)(2,1)}, bf16[384,1024]{1,0:T(8,128)(2,1)S(1)}, u32[]{:S(2)}, u32[]{:S(2)}) collective-permute-start(bf16[384,1024]{1,0:T(8,128)(2,1)} %bitcast.43), channel_id=1, source_target_pairs={{0,15},{1,14},{2,13},{3,12},{4,11},{5,10},{6,9},{7,8},{8,7},{9,6},... | collective-permute-start | bytes 2359304 | tf_op jit(solution)/shard_map/ppermute | solution.py:269
  (9 other events, 7.7 us)

commit v2 on v0

v2 whole, which is shorter than its diff:
```python
import functools

import jax
import jax.numpy as jnp
from jax import lax
from jax.experimental import pallas as pl
from jax.experimental.pallas import tpu as pltpu
from jax.sharding import Mesh
from jax.sharding import PartitionSpec as P

AXES = ("y_hi", "z", "x", "y_lo", "core")
SEQ = ("x", "y_lo", "core")
XN, YN, CN = 4, 4, 2
VMEM_LIMIT = 48 * 1024 * 1024
EDGE = 16
TILE = 256
PARTS = (8, 6, 2)
INV_SQRT2 = 0.7071067811865476


def core_swap(value):
    return lax.ppermute(value, "core", [(0, 1), (1, 0)])


def x_shift(value):
    route = []
    for x in range(XN):
        route += [(x * 2, (x + 1) % XN * 2), (x * 2 + 1, (x - 1) % XN * 2 + 1)]
    return lax.ppermute(value, ("x", "core"), route)


def y_shift(value):
    route = []
    for y in range(YN):
        route += [(y * 2, (y + 1) % YN * 2), (y * 2 + 1, (y - 1) % YN * 2 + 1)]
    return lax.ppermute(value, ("y_hi", "y_lo", "core"), route)


def fence(*values):
    return pl.pallas_call(
        lambda *refs: None,
        out_shape=[jax.ShapeDtypeStruct(v.shape, v.dtype) for v in values],
        in_specs=[pl.BlockSpec(memory_space=pl.ANY)] * len(values),
        out_specs=[pl.BlockSpec(memory_space=pl.ANY)] * len(values),
        input_output_aliases={i: i for i in range(len(values))},
        name="fence",
    )(*values)


def prepare_kernel(place_ref, forward_ref, reverse_ref, low_ref, high_ref, *refs):
    out_refs, full_ref = refs[:3], refs[3]
    rows, width = forward_ref.shape
    part = width // 16
    full_ref[0, :rows, :] = forward_ref[...]
    row = lax.broadcasted_iota(jnp.int32, (rows, rows), 0)
    column = lax.broadcasted_iota(jnp.int32, (rows, rows), 1)
    flip = jnp.where(row + column == rows - 1, 1.0, 0.0).astype(jnp.bfloat16)
    full_ref[1, :rows, :] = jnp.dot(
        flip, reverse_ref[...], preferred_element_type=jnp.float32
    ).astype(jnp.bfloat16)
    edge = lax.broadcasted_iota(jnp.int32, (EDGE, width), 0)
    low = low_ref[...].astype(jnp.float32)
    high = high_ref[...].astype(jnp.float32)
    for strand, after, before in ((0, high[0:1], low[0:1]), (1, low[1:2], high[1:2])):
        tile = jnp.where(edge == 0, after, jnp.where(edge == EDGE - 1, before, 0.0))
        full_ref[strand, rows:, :] = tile.astype(jnp.bfloat16)
    begin = 0
    for out_ref, count in zip(out_refs, PARTS):
        size = count * part
        lane = lax.broadcasted_iota(jnp.int32, (1, size), 1)
        wanted = jnp.zeros((1, size), jnp.int32)
        for block in range(count):
            inside = (lane >= block * part) & (lane < (block + 1) * part)
            wanted = jnp.where(inside, lane + (place_ref[begin + block] - block) * part, wanted)
        source = lax.broadcasted_iota(jnp.int32, (width, size), 0)
        move = jnp.where(source == wanted, 1.0, 0.0).astype(jnp.bfloat16)
        for strand in range(2):
            out_ref[strand] = jnp.dot(
                full_ref[strand], move, preferred_element_type=jnp.float32
            ).astype(jnp.bfloat16)
        begin += count


def prepare(place, forward_embed, reverse_embed, low, high):
    rows, width = forward_embed.shape
    part = width // 16
    inside = pl.BlockSpec(memory_space=pltpu.VMEM)
    return pl.pallas_call(
        prepare_kernel,
        out_shape=[
            jax.ShapeDtypeStruct((2, rows + EDGE, count * part), jnp.bfloat16) for count in PARTS
        ],
        in_specs=[pl.BlockSpec(memory_space=pltpu.SMEM)] + [inside] * 4,
        out_specs=[inside] * 3,
        scratch_shapes=[pltpu.VMEM((2, rows + EDGE, width), jnp.bfloat16)],
        compiler_params=pltpu.CompilerParams(vmem_limit_bytes=VMEM_LIMIT),
        cost_estimate=pl.CostEstimate(
            flops=4 * rows * width * width, bytes_accessed=8 * rows * width, transcendentals=0
        ),
        name="prepare",
    )(place, forward_embed, reverse_embed, low, high)


def convolve(x_ref, slot, flipped, blocks, taps):
    rows = x_ref.shape[1] - EDGE
    order = (2, 1, 0) if flipped else (0, 1, 2)
    for target, tap in zip(taps, order):
        weight = jnp.concatenate([block[tap] for block in blocks], axis=0)
        target[pl.ds(8, rows + EDGE), :] = jnp.dot(
            x_ref[slot], weight, preferred_element_type=jnp.float32
        )
    before, here, after = taps
    before[pl.ds(7, 1), :] = before[pl.ds(8 + rows + EDGE - 1, 1), :]
    return before[pl.ds(7, rows), :] + here[pl.ds(8, rows), :] + after[pl.ds(9, rows), :]


def partial_kernel(count, first, x_ref, *refs):
    blocks, refs = refs[:count], refs[count:]
    if not first:
        prev_ref, refs = refs[0], refs[1:]
    out_ref, taps = refs[0], refs[1:]
    for strand in range(2):
        acc = convolve(x_ref, strand, strand == 1, blocks, taps)
        if not first:
            acc = acc + prev_ref[strand]
        out_ref[strand] = acc


def partial_sum(x, sources, prev):
    rows, depth = x.shape[1] - EDGE, x.shape[2]
    part, channels = sources[0].shape[1:]
    acc_spec = pl.BlockSpec((2, rows, TILE), lambda n: (0, 0, n))
    operands, specs = [x, *sources], [pl.BlockSpec((2, rows + EDGE, depth), lambda n: (0, 0, 0))]
    specs += [pl.BlockSpec((3, part, TILE), lambda n: (0, 0, n))] * len(sources)
    if prev is not None:
        operands.append(prev)
        specs.append(acc_spec)
    return pl.pallas_call(
        functools.partial(partial_kernel, len(sources), prev is None),
        out_shape=jax.ShapeDtypeStruct((2, rows, channels), jnp.float32),
        grid=(channels // TILE,),
        in_specs=specs,
        out_specs=acc_spec,
        scratch_shapes=[pltpu.VMEM((rows + EDGE + 16, TILE), jnp.float32)] * 3,
        compiler_params=pltpu.CompilerParams(vmem_limit_bytes=VMEM_LIMIT),
        cost_estimate=pl.CostEstimate(
            flops=12 * rows * depth * channels,
            bytes_accessed=6 * depth * channels + 8 * rows * channels,
            transcendentals=0,
        ),
        name="partial_sum",
    )(*operands)


def finish_kernel(count, flipped, x_ref, *refs):
    blocks, refs = refs[:count], refs[count:]
    prev_ref, bias_ref, head_ref, head_bias_ref, out_ref, logits_ref = refs[:6]
    taps = refs[6:]
    step = pl.program_id(0)
    acc = convolve(x_ref, 0, flipped, blocks, taps) + prev_ref[0] + bias_ref[...]
    hidden = (0.5 * acc * (1.0 + lax.erf(acc * INV_SQRT2))).astype(jnp.bfloat16)
    value = jnp.dot(hidden, head_ref[...], preferred_element_type=jnp.float32)

    @pl.when(step == 0)
    def _():
        logits_ref[...] = value

    @pl.when(step > 0)
    def _():
        logits_ref[...] += value

    @pl.when(step == pl.num_programs(0) - 1)
    def _():
        logits = logits_ref[...] + head_bias_ref[...]
        tracks = jnp.maximum(logits, 0.0) + jnp.log1p(jnp.exp(-jnp.abs(logits)))
        out_ref[...] = tracks.astype(jnp.bfloat16)


def finish(strand, x, sources, prev, bias, head, head_bias):
    rows, depth = x.shape[1] - EDGE, x.shape[2]
    part, channels = sources[0].shape[1:]
    tracks = head.shape[1]
    return pl.pallas_call(
        functools.partial(finish_kernel, len(sources), strand == 1),
        out_shape=jax.ShapeDtypeStruct((rows, tracks), jnp.bfloat16),
        grid=(channels // TILE,),
        in_specs=[pl.BlockSpec((1, rows + EDGE, depth), lambda n: (strand, 0, 0))]
        + [pl.BlockSpec((3, part, TILE), lambda n: (0, 0, n))] * len(sources)
        + [
            pl.BlockSpec((1, rows, TILE), lambda n: (strand, 0, n)),
            pl.BlockSpec((1, TILE), lambda n: (0, n)),
            pl.BlockSpec((TILE, tracks), lambda n: (n, 0)),
            pl.BlockSpec((1, tracks), lambda n: (0, 0)),
        ],
        out_specs=pl.BlockSpec((rows, tracks), lambda n: (0, 0)),
        scratch_shapes=[pltpu.VMEM((rows, tracks), jnp.float32)]
        + [pltpu.VMEM((rows + EDGE + 16, TILE), jnp.float32)] * 3,
        compiler_params=pltpu.CompilerParams(vmem_limit_bytes=VMEM_LIMIT),
        cost_estimate=pl.CostEstimate(
            flops=2 * rows * channels * (3 * depth + tracks),
            bytes_accessed=6 * depth * channels + 2 * channels * tracks,
            transcendentals=rows * channels,
        ),
        name="finish",
    )(x, *sources, prev, bias, head, head_bias[None])


def per_device(forward_embed, reverse_embed, conv_weight, conv_bias, head_weight, head_bias):
    own = conv_weight[0]
    x, y, core = lax.axis_index("x"), lax.axis_index("y_lo"), lax.axis_index("core")
    ends = XN * 2 * CN

    def seq(x_of, y_of, core_of):
        return (x_of % XN) * 4 + y_of * 2 + core_of

    step = 1 - 2 * core
    back, fore, far = x - step + XN, x + step + XN, x + 2
    other, over = 1 - core, 1 - y
    place = jnp.stack(
        [
            seq(x, y, core), seq(x, y, other), seq(x, over, core), seq(x, over, other),
            seq(back, y, core), seq(fore, y, other), seq(back, over, core), seq(fore, over, other),
            seq(far, y, core), seq(far, y, other), seq(back, y, other), seq(fore, y, core),
            seq(far, over, core), seq(far, over, other),
            seq(back, over, other), seq(fore, over, core),
        ]
    ).astype(jnp.int32)

    across = y_shift(own)
    near = x_shift(own)
    sibling = core_swap(own)
    up = [(i, i + 1) for i in range(ends - 1)]
    down = [(b, a) for a, b in up]
    low = lax.ppermute(jnp.stack([forward_embed[-1], reverse_embed[-1]]), SEQ, up)
    high = lax.ppermute(jnp.stack([forward_embed[0], reverse_embed[0]]), SEQ, down)
    x_1, x_2, x_3 = prepare(place, forward_embed, reverse_embed, low, high)
    near, across, sibling, x_1 = fence(near, across, sibling, x_1)

    distant = x_shift(near)
    near_over = y_shift(near)
    across_b = core_swap(across)
    near_b = core_swap(near)
    distant, near_over, sibling, across_b, near_b = fence(
        distant, near_over, sibling, across_b, near_b
    )

    second = x_shift(sibling)
    distant_over = y_shift(distant)
    near_over_b = core_swap(near_over)
    distant_b = core_swap(distant)
    acc = partial_sum(
        x_1, [own, sibling, across, across_b, near, near_b, near_over, near_over_b], None
    )
    second, distant_over, distant_b, acc = fence(second, distant_over, distant_b, acc)

    second_over = y_shift(second)
    second_b = core_swap(second)
    distant_over_b = core_swap(distant_over)
    acc = partial_sum(
        x_2, [distant, distant_b, second, second_b, distant_over, distant_over_b], acc
    )
    second_over, acc = fence(second_over, acc)
    second_over_b = core_swap(second_over)

    last = [second_over, second_over_b]
    reverse_tracks = finish(1, x_3, last, acc, conv_bias, head_weight, head_bias)
    forward_tracks = finish(0, x_3, last, acc, conv_bias, head_weight, head_bias)
    mirrored = lax.ppermute(reverse_tracks, SEQ, [(i, ends - 1 - i) for i in range(ends)])
    mean = 0.5 * (forward_tracks.astype(jnp.float32) + mirrored.astype(jnp.float32))
    return mean.astype(jnp.bfloat16)


def solution(mesh):
    fine = Mesh(mesh.devices.reshape(2, 8, XN, 2, CN), AXES)
    return jax.shard_map(
        per_device,
        mesh=fine,
        in_specs=(
            P(AXES, None),
            P(AXES, None),
            P(None, None, SEQ, None),
            P(),
            P(),
            P(),
        ),
        out_specs=P(AXES, None),
        check_vma=False,
    )
```

time: 203 us -> 120 us (0.59); the launches traced: 200 us -> 119 us
  waiting for transfers between devices: 102 us -> 30.3 us
  matrix products: 49.5 us -> 0 us
  Pallas kernels: 0 us -> 43 us
  between operations: 13.5 us -> 0.26 us
  local copies, waits for them, and re-layouts: 13.7 us -> 21.6 us
  starting transfers between devices: 17.5 us -> 22.4 us
    all_gather x1 -> x0, waiting for transfers between devices: 79.2 us -> none  [convolve(): taps = lax.all_gather(kernel, 'seq', axis=1, tiled=True)]
    dot_general x6 -> x0, matrix products: 49.5 us -> none  [the longest x2 25.7 us: run_strands(): jnp.einsum('kbc,ct->kbt', hidden, head_weight, preferred_element_type=jnp...]
    pallas_call x0 -> x9, Pallas kernels: none -> 43 us  [the longest x2 20.6 us: partial_sum(): pl.pallas_call(functools.partial(partial_kernel, len(sources), prev is No...]
    unnamed x8 -> x54, local copies, waits for them, and re-layouts: 0.02 us -> 20.7 us
    rev x1 -> x0, local copies, waits for them, and re-layouts: 11.9 us -> none  [per_device(): reverse_tracks = reverse_tracks[::-1]]
    ppermute x8 -> x18, waiting for transfers between devices: 22.4 us -> 30.3 us  [the longest x1 10.6 us: per_device(): lax.ppermute(reverse_tracks, SEQ, [(i, ends - 1 - i) for i in range(ends)])]
    ppermute x8 -> x18, starting transfers between devices: 17.5 us -> 22.4 us  [the longest x4 6.63 us: y_shift(): return lax.ppermute(value, ('y_hi', 'y_lo', 'core'), route)]
  transfers between devices with their start and end apart: 9 -> 18, of which waited for: 5 -> 9; matrix products, arithmetic and copies ran while one was open for 20% -> 1% of each run, Pallas kernels for 0% -> 29%
where the time goes in v2:
time: 120 us; the launch traced here: 119 us
  Pallas kernels  43 us (36%)
  waiting for transfers between devices  30.3 us (25%)
  starting transfers between devices  22.4 us (19%)
  local copies, waits for them, and re-layouts  21.6 us (18%)
  other arithmetic  1.22 us (1%)
    unnamed x54, local copies, waits for them, and re-layouts  20.7 us
    pallas_call x2, Pallas kernels, partial_sum(): pl.pallas_call(functools.partial(partial_kernel, len(sources), prev is No...  20.6 us
    pallas_call x2, Pallas kernels, finish(): pl.pallas_call(functools.partial(finish_kernel, len(sources), strand == 1...  16.3 us
    ppermute x1, waiting for transfers between devices, per_device(): lax.ppermute(reverse_tracks, SEQ, [(i, ends - 1 - i) for i in range(ends)])  10.6 us
    ppermute x4, waiting for transfers between devices, y_shift(): return lax.ppermute(value, ('y_hi', 'y_lo', 'core'), route)  9.25 us
    ppermute x4, starting transfers between devices, y_shift(): return lax.ppermute(value, ('y_hi', 'y_lo', 'core'), route)  6.63 us
    pallas_call x1, Pallas kernels, prepare(): pl.pallas_call(prepare_kernel, out_shape=[jax.ShapeDtypeStruct((2, rows +...  6.14 us
    ppermute x8, starting transfers between devices, core_swap(): return lax.ppermute(value, 'core', [(0, 1), (1, 0)])  6.04 us
  transfers between devices with their start and end apart: 18, of which 9 were waited for; matrix products, arithmetic and copies ran while one was open for 1% of the time, Pallas kernels for 29%

profile of v2, /device:TPU:1, one launch (start us, length us, event | category | flops | bytes accessed | tf_op | source)
XLA Modules:
  0.0 118.8 jit_solution(16998745751565552524)
XLA Ops:
  0.0 3.2 %collective-permute-start.4 = (bf16[3,96,1536]{2,1,0:T(8,128)(2,1)}, bf16[3,96,1536]{2,1,0:T(8,128)(2,1)S(1)}, u32[]{:S(2)}, u32[]{:S(2)}) collective-permute-start(bf16[3,96,1536]{2,1,0:T(8,128)(2,1)} %bitcast.20), channel_id=1, source_target_pairs={{0,1},{1,0},{2,3},{3,2},{4,5},{5,4},{6,7},{7,6},{8,9},{9,8},{10,11... | collective-permute-start | bytes 2654216 | tf_op jit(solution)/shard_map/ppermute | solution.py:22
  3.2 1.0 collective-permute-start.3
  4.2 2.5 %collective-permute-start.2 = (bf16[3,96,1536]{2,1,0:T(8,128)(2,1)}, bf16[3,96,1536]{2,1,0:T(8,128)(2,1)S(1)}, u32[]{:S(2)}, u32[]{:S(2)}) collective-permute-start(bf16[3,96,1536]{2,1,0:T(8,128)(2,1)} %bitcast.22), channel_id=1, source_target_pairs={{0,4},{1,13},{4,8},{5,1},{8,12},{9,5},{12,0},{13,9},{2,6},{3,15},{... | collective-permute-start | bytes 2654216 | tf_op jit(solution)/shard_map/ppermute | solution.py:29
  6.7 0.8 fusion
  7.6 1.9 %collective-permute-start = (bf16[2,1536]{1,0:T(2,128)(2,1)S(1)}, bf16[2,1536]{1,0:T(2,128)(2,1)S(1)}, u32[]{:S(2)}, u32[]{:S(2)}) collective-permute-start(bf16[2,1536]{1,0:T(2,128)(2,1)S(1)} %pad_maximum_fusion), channel_id=1, source_target_pairs={{0,1},{1,2},{2,3},{3,4},{4,5},{5,6},{6,7},{7,8},{8,9},{9,10},{10,1... | collective-permute-start | bytes 18440 | tf_op jit(solution)/shard_map/ppermute | solution.py:234
  9.5 2.4 %collective-permute-start.1 = (bf16[2,1536]{1,0:T(2,128)(2,1)S(1)}, bf16[2,1536]{1,0:T(2,128)(2,1)S(1)}, u32[]{:S(2)}, u32[]{:S(2)}) collective-permute-start(bf16[2,1536]{1,0:T(2,128)(2,1)S(1)} %pad_maximum_fusion.1), channel_id=1, source_target_pairs={{1,0},{2,1},{3,2},{4,3},{5,4},{6,5},{7,6},{8,7},{9,8},{10,9},{11,1... | collective-permute-start | bytes 18440 | tf_op jit(solution)/shard_map/ppermute | solution.py:235
  12.1 2.8 %collective-permute-done.1.high_ref = bf16[2,1536]{1,0:T(2,128)(2,1)S(1)} collective-permute-done((bf16[2,1536]{1,0:T(2,128)(2,1)S(1)}, bf16[2,1536]{1,0:T(2,128)(2,1)S(1)}, u32[]{:S(2)}, u32[]{:S(2)}) %collective-permute-start.1) | collective-permute-done | bytes 6176 | tf_op jit(solution)/shard_map/ppermute | solution.py:235
  14.9 1.3 %copy-done.23 = bf16[384,1536]{1,0:T(8,128)(2,1)S(1)} copy-done((bf16[384,1536]{1,0:T(8,128)(2,1)S(1)}, bf16[384,1536]{1,0:T(8,128)(2,1)}, u32[]{:S(2)}) %copy-start.23) | copy-done | bytes 1179672
  16.2 1.3 %copy-done.24 = bf16[384,1536]{1,0:T(8,128)(2,1)S(1)} copy-done((bf16[384,1536]{1,0:T(8,128)(2,1)S(1)}, bf16[384,1536]{1,0:T(8,128)(2,1)}, u32[]{:S(2)}) %copy-start.24) | copy-done | bytes 1179672
  17.4 6.1 %prepare.1 = (bf16[2,400,768]{2,1,0:T(8,128)(2,1)S(1)}, bf16[2,400,576]{2,1,0:T(8,128)(2,1)S(1)}, bf16[2,400,192]{2,1,0:T(8,128)(2,1)S(1)}) custom-call(s32[16]{0:T(128)S(1)} %stack.73.place_ref, bf16[384,1536]{1,0:T(8,128)(2,1)S(1)} %copy-done.23, bf16[384,1536]{1,0:T(8,128)(2,1)S(1)} %copy-done.24, bf16[2,1536]{1,0:T(2,128)(2,1)S(1)} %collective-permute-done.low_ref, ...), custom_call_target="tpu_custom_call" | custom-call | flops 3623878656 | bytes 4718592 | tf_op jit(solution)/shard_map/prepare/pallas_call | solution.py:88
  23.6 0.7 copy-done.9
  24.3 1.1 copy-done.11
  25.4 1.0 copy-done.12
  26.4 0.9 copy-done.7
  27.9 0.5 collective-permute-start.8
  28.4 2.3 %collective-permute-start.6 = (bf16[3,96,1536]{2,1,0:T(8,128)(2,1)}, bf16[3,96,1536]{2,1,0:T(8,128)(2,1)}, u32[]{:S(2)}, u32[]{:S(2)}) collective-permute-start(bf16[3,96,1536]{2,1,0:T(8,128)(2,1)} %get-tuple-element.25.refs_4_), channel_id=1, source_target_pairs={{0,2},{1,131},{2,128},{3,1},{128,130},{129,3},{130,0},{131,129},{4... | collective-permute-start | bytes 2654216 | tf_op jit(solution)/shard_map/ppermute | solution.py:36
  30.7 1.0 collective-permute-done.8.refs_4_
  31.8 9.2 %collective-permute-done.6.refs_1_ = bf16[3,96,1536]{2,1,0:T(8,128)(2,1)} collective-permute-done((bf16[3,96,1536]{2,1,0:T(8,128)(2,1)}, bf16[3,96,1536]{2,1,0:T(8,128)(2,1)}, u32[]{:S(2)}, u32[]{:S(2)}) %collective-permute-start.6) | collective-permute-done | bytes 884768 | tf_op jit(solution)/shard_map/ppermute | solution.py:36
  41.0 2.2 %collective-permute-done.5.refs_0_ = bf16[3,96,1536]{2,1,0:T(8,128)(2,1)} collective-permute-done((bf16[3,96,1536]{2,1,0:T(8,128)(2,1)}, bf16[3,96,1536]{2,1,0:T(8,128)(2,1)}, u32[]{:S(2)}, u32[]{:S(2)}) %collective-permute-start.5) | collective-permute-done | bytes 884768 | tf_op jit(solution)/shard_map/ppermute | solution.py:29
  43.3 1.1 collective-permute-start.12
  44.6 1.6 %collective-permute-start.10 = (bf16[3,96,1536]{2,1,0:T(8,128)(2,1)}, bf16[3,96,1536]{2,1,0:T(8,128)(2,1)S(1)}, u32[]{:S(2)}, u32[]{:S(2)}) collective-permute-start(bf16[3,96,1536]{2,1,0:T(8,128)(2,1)} %get-tuple-element.29.refs_0_), channel_id=1, source_target_pairs={{0,2},{1,131},{2,128},{3,1},{128,130},{129,3},{130,0},{131,129},{4... | collective-permute-start | bytes 2654216 | tf_op jit(solution)/shard_map/ppermute | solution.py:36
  46.2 0.4 collective-permute-done.12.refs_7_
  46.6 1.0 copy-done.26
  47.6 1.2 copy-done.8
  48.8 1.2 copy-done.16
  49.9 1.2 copy-done.18
  51.1 1.2 copy-done.20
  52.3 1.2 copy-done.25
  53.4 10.1 %partial_sum.2.refs_3_ = f32[2,384,1536]{2,1,0:T(8,128)} custom-call(bf16[2,400,768]{2,1,0:T(8,128)(2,1)} %get-tuple-element.30.x_ref, bf16[3,96,1536]{2,1,0:T(8,128)(2,1)S(1)} %bitcast.23, bf16[3,96,1536]{2,1,0:T(8,128)(2,1)S(1)} %copy-done.8, bf16[3,96,1536]{2,1,0:T(8,128)(2,1)S(1)} %copy-done.14, bf16[3,96,1536]{2,1,0:T(8,128)(2,1)S(1)} %copy-done.18, ...), custom_call_target="tpu_custom_call" | custom-call | flops 5435817984 | bytes 11796480 | tf_op jit(solution)/shard_map/partial_sum/pallas_call | solution.py:138
  63.6 0.9 copy-done.1
  64.8 0.9 copy-done.5
  65.7 0.4 collective-permute-start.15
  66.2 1.7 %collective-permute-start.13 = (bf16[3,96,1536]{2,1,0:T(8,128)(2,1)}, bf16[3,96,1536]{2,1,0:T(8,128)(2,1)}, u32[]{:S(2)}, u32[]{:S(2)}) collective-permute-start(bf16[3,96,1536]{2,1,0:T(8,128)(2,1)} %get-tuple-element.34.refs_2_), channel_id=1, source_target_pairs={{0,2},{1,131},{2,128},{3,1},{128,130},{129,3},{130,0},{131,129},{4... | collective-permute-start | bytes 2654216 | tf_op jit(solution)/shard_map/ppermute | solution.py:36
  67.9 0.5 collective-permute-done.15.refs_5_
  68.4 1.3 %collective-permute-done.14.refs_3_ = bf16[3,96,1536]{2,1,0:T(8,128)(2,1)S(1)} collective-permute-done((bf16[3,96,1536]{2,1,0:T(8,128)(2,1)}, bf16[3,96,1536]{2,1,0:T(8,128)(2,1)S(1)}, u32[]{:S(2)}, u32[]{:S(2)}) %collective-permute-start.14) | collective-permute-done | bytes 884768 | tf_op jit(solution)/shard_map/ppermute | solution.py:22
  69.6 1.2 copy-done.2
  70.8 1.2 copy-done.4
  72.0 1.2 copy-done.6
  73.1 10.5 %partial_sum.3.refs_1_ = f32[2,384,1536]{2,1,0:T(8,128)} custom-call(bf16[2,400,576]{2,1,0:T(8,128)(2,1)} %copy-done.12, bf16[3,96,1536]{2,1,0:T(8,128)(2,1)} %get-tuple-element.29.refs_0_, bf16[3,96,1536]{2,1,0:T(8,128)(2,1)S(1)} %copy-done.4, bf16[3,96,1536]{2,1,0:T(8,128)(2,1)S(1)} %copy-done.2, bf16[3,96,1536]{2,1,0:T(8,128)(2,1)S(1)} %collective-permute-done.14.refs_3_, ...), custom_call_target="tpu_custom_call" | custom-call | flops 4076863488 | bytes 10027008 | tf_op jit(solution)/shard_map/partial_sum/pallas_call | solution.py:138
  83.6 0.5 collective-permute-start.16
  84.1 2.3 %collective-permute-done.16.refs_1_ = bf16[3,96,1536]{2,1,0:T(8,128)(2,1)S(1)} collective-permute-done((bf16[3,96,1536]{2,1,0:T(8,128)(2,1)}, bf16[3,96,1536]{2,1,0:T(8,128)(2,1)S(1)}, u32[]{:S(2)}, u32[]{:S(2)}) %collective-permute-start.16) | collective-permute-done | bytes 884768 | tf_op jit(solution)/shard_map/ppermute | solution.py:22
  86.4 0.7 copy-done.21
  87.1 0.7 copy-done.22
  87.7 8.2 %finish.3 = bf16[384,1024]{1,0:T(8,128)(2,1)S(1)} custom-call(bf16[2,400,192]{2,1,0:T(8,128)(2,1)S(1)} %copy-done.10, bf16[3,96,1536]{2,1,0:T(8,128)(2,1)} %get-tuple-element.39.refs_0_, bf16[3,96,1536]{2,1,0:T(8,128)(2,1)S(1)} %collective-permute-done.16.refs_1_, f32[2,384,1536]{2,1,0:T(8,128)} %get-tuple-element.40.refs_2_, f32[1,1536]{1,0:T(1,128)S(1)} %copy-done.21, ...), custom_call_target="tpu_custom_call" | custom-call | flops 1887436800 | bytes 4915200 | tf_op jit(solution)/shard_map/finish/pallas_call | solution.py:183
  95.9 2.9 %collective-permute-start.17 = (bf16[384,1024]{1,0:T(8,128)(2,1)S(1)}, bf16[384,1024]{1,0:T(8,128)(2,1)S(1)}, u32[]{:S(2)}, u32[]{:S(2)}) collective-permute-start(bf16[384,1024]{1,0:T(8,128)(2,1)S(1)} %finish.3), channel_id=1, source_target_pairs={{0,15},{1,14},{2,13},{3,12},{4,11},{5,10},{6,9},{7,8},{8,7},{9,6},... | collective-permute-start | bytes 2359304 | tf_op jit(solution)/shard_map/ppermute | solution.py:268
  98.8 8.2 %finish.2 = bf16[384,1024]{1,0:T(8,128)(2,1)S(1)} custom-call(bf16[2,400,192]{2,1,0:T(8,128)(2,1)S(1)} %copy-done.10, bf16[3,96,1536]{2,1,0:T(8,128)(2,1)} %get-tuple-element.39.refs_0_, bf16[3,96,1536]{2,1,0:T(8,128)(2,1)S(1)} %collective-permute-done.16.refs_1_, f32[2,384,1536]{2,1,0:T(8,128)} %get-tuple-element.40.refs_2_, f32[1,1536]{1,0:T(1,128)S(1)} %copy-done.21, ...), custom_call_target="tpu_custom_call" | custom-call | flops 1887436800 | bytes 4915200 | tf_op jit(solution)/shard_map/finish/pallas_call | solution.py:183
  107.0 10.6 %collective-permute-done.17 = bf16[384,1024]{1,0:T(8,128)(2,1)S(1)} collective-permute-done((bf16[384,1024]{1,0:T(8,128)(2,1)S(1)}, bf16[384,1024]{1,0:T(8,128)(2,1)S(1)}, u32[]{:S(2)}, u32[]{:S(2)}) %collective-permute-start.17) | collective-permute-done | bytes 786464 | tf_op jit(solution)/shard_map/ppermute | solution.py:268
  117.6 1.2 multiply_convert_fusion
  (56 shorter events, 1.4 us)
Async XLA Ops:
  0.0 26.4 %collective-permute-start.4 = (bf16[3,96,1536]{2,1,0:T(8,128)(2,1)}, bf16[3,96,1536]{2,1,0:T(8,128)(2,1)S(1)}, u32[]{:S(2)}, u32[]{:S(2)}) collective-permute-start(bf16[3,96,1536]{2,1,0:T(8,128)(2,1)} %bitcast.20), channel_id=1, source_target_pairs={{0,1},{1,0},{2,3},{3,2},{4,5},{5,4},{6,7},{7,6},{8,9},{9,8},{10,11... | collective-permute-start | bytes 2654216 | tf_op jit(solution)/shard_map/ppermute | solution.py:22
  3.2 23.1 %collective-permute-start.3 = (bf16[3,96,1536]{2,1,0:T(8,128)(2,1)}, bf16[3,96,1536]{2,1,0:T(8,128)(2,1)S(1)}, u32[]{:S(2)}, u32[]{:S(2)}) collective-permute-start(bf16[3,96,1536]{2,1,0:T(8,128)(2,1)} %bitcast.21), channel_id=1, source_target_pairs={{0,2},{1,131},{2,128},{3,1},{128,130},{129,3},{130,0},{131,129},{4... | collective-permute-start | bytes 2654216 | tf_op jit(solution)/shard_map/ppermute | solution.py:36
  4.2 22.1 %collective-permute-start.2 = (bf16[3,96,1536]{2,1,0:T(8,128)(2,1)}, bf16[3,96,1536]{2,1,0:T(8,128)(2,1)S(1)}, u32[]{:S(2)}, u32[]{:S(2)}) collective-permute-start(bf16[3,96,1536]{2,1,0:T(8,128)(2,1)} %bitcast.22), channel_id=1, source_target_pairs={{0,4},{1,13},{4,8},{5,1},{8,12},{9,5},{12,0},{13,9},{2,6},{3,15},{... | collective-permute-start | bytes 2654216 | tf_op jit(solution)/shard_map/ppermute | solution.py:29
  7.6 4.5 %collective-permute-start = (bf16[2,1536]{1,0:T(2,128)(2,1)S(1)}, bf16[2,1536]{1,0:T(2,128)(2,1)S(1)}, u32[]{:S(2)}, u32[]{:S(2)}) collective-permute-start(bf16[2,1536]{1,0:T(2,128)(2,1)S(1)} %pad_maximum_fusion), channel_id=1, source_target_pairs={{0,1},{1,2},{2,3},{3,4},{4,5},{5,6},{6,7},{7,8},{8,9},{9,10},{10,1... | collective-permute-start | bytes 18440 | tf_op jit(solution)/shard_map/ppermute | solution.py:234
  9.5 5.4 %collective-permute-start.1 = (bf16[2,1536]{1,0:T(2,128)(2,1)S(1)}, bf16[2,1536]{1,0:T(2,128)(2,1)S(1)}, u32[]{:S(2)}, u32[]{:S(2)}) collective-permute-start(bf16[2,1536]{1,0:T(2,128)(2,1)S(1)} %pad_maximum_fusion.1), channel_id=1, source_target_pairs={{1,0},{2,1},{3,2},{4,3},{5,4},{6,5},{7,6},{8,7},{9,8},{10,9},{11,1... | collective-permute-start | bytes 18440 | tf_op jit(solution)/shard_map/ppermute | solution.py:235
  14.9 1.3 %copy-start.23 = (bf16[384,1536]{1,0:T(8,128)(2,1)S(1)}, bf16[384,1536]{1,0:T(8,128)(2,1)}, u32[]{:S(2)}) copy-start(bf16[384,1536]{1,0:T(8,128)(2,1)} %forward_ref.1) | copy-start | bytes 3538948
  16.2 1.3 %copy-start.24 = (bf16[384,1536]{1,0:T(8,128)(2,1)S(1)}, bf16[384,1536]{1,0:T(8,128)(2,1)}, u32[]{:S(2)}) copy-start(bf16[384,1536]{1,0:T(8,128)(2,1)} %reverse_ref.1) | copy-start | bytes 3538948
  23.6 0.8 copy-start.9
  24.3 1.1 copy-start.11
  25.4 1.0 copy-start.12
  26.4 0.9 copy-start.7
  26.4 1.2 %copy-start.13 = (bf16[3,96,1536]{2,1,0:T(8,128)(2,1)}, bf16[3,96,1536]{2,1,0:T(8,128)(2,1)S(1)}, u32[]{:S(2)}) copy-start(bf16[3,96,1536]{2,1,0:T(8,128)(2,1)S(1)} %collective-permute-done.3.refs_1_) | copy-start | bytes 2654212
  26.4 1.5 %copy-start.15 = (bf16[3,96,1536]{2,1,0:T(8,128)(2,1)}, bf16[3,96,1536]{2,1,0:T(8,128)(2,1)S(1)}, u32[]{:S(2)}) copy-start(bf16[3,96,1536]{2,1,0:T(8,128)(2,1)S(1)} %collective-permute-done.2.refs_0_) | copy-start | bytes 2654212
  27.9 2.8 %collective-permute-start.7 = (bf16[3,96,1536]{2,1,0:T(8,128)(2,1)}, bf16[3,96,1536]{2,1,0:T(8,128)(2,1)S(1)}, u32[]{:S(2)}, u32[]{:S(2)}) collective-permute-start(bf16[3,96,1536]{2,1,0:T(8,128)(2,1)} %get-tuple-element.27.refs_2_), channel_id=1, source_target_pairs={{0,1},{1,0},{2,3},{3,2},{4,5},{5,4},{6,7},{7,6},{8,9},{9,8},{10,11... | collective-permute-start | bytes 2654216 | tf_op jit(solution)/shard_map/ppermute | solution.py:22
  27.9 3.9 %collective-permute-start.8 = (bf16[3,96,1536]{2,1,0:T(8,128)(2,1)}, bf16[3,96,1536]{2,1,0:T(8,128)(2,1)S(1)}, u32[]{:S(2)}, u32[]{:S(2)}) collective-permute-start(bf16[3,96,1536]{2,1,0:T(8,128)(2,1)} %get-tuple-element.25.refs_4_), channel_id=1, source_target_pairs={{0,1},{1,0},{2,3},{3,2},{4,5},{5,4},{6,7},{7,6},{8,9},{9,8},{10,11... | collective-permute-start | bytes 2654216 | tf_op jit(solution)/shard_map/ppermute | solution.py:22
  28.4 12.6 %collective-permute-start.6 = (bf16[3,96,1536]{2,1,0:T(8,128)(2,1)}, bf16[3,96,1536]{2,1,0:T(8,128)(2,1)}, u32[]{:S(2)}, u32[]{:S(2)}) collective-permute-start(bf16[3,96,1536]{2,1,0:T(8,128)(2,1)} %get-tuple-element.25.refs_4_), channel_id=1, source_target_pairs={{0,2},{1,131},{2,128},{3,1},{128,130},{129,3},{130,0},{131,129},{4... | collective-permute-start | bytes 2654216 | tf_op jit(solution)/shard_map/ppermute | solution.py:36
  30.7 12.5 %collective-permute-start.5 = (bf16[3,96,1536]{2,1,0:T(8,128)(2,1)}, bf16[3,96,1536]{2,1,0:T(8,128)(2,1)}, u32[]{:S(2)}, u32[]{:S(2)}) collective-permute-start(bf16[3,96,1536]{2,1,0:T(8,128)(2,1)} %get-tuple-element.25.refs_4_), channel_id=1, source_target_pairs={{0,4},{1,13},{4,8},{5,1},{8,12},{9,5},{12,0},{13,9},{2,6},{3,15},{... | collective-permute-start | bytes 2654216 | tf_op jit(solution)/shard_map/ppermute | solution.py:29
  30.7 12.5 %copy-start.17 = (bf16[3,96,1536]{2,1,0:T(8,128)(2,1)}, bf16[3,96,1536]{2,1,0:T(8,128)(2,1)S(1)}, u32[]{:S(2)}) copy-start(bf16[3,96,1536]{2,1,0:T(8,128)(2,1)S(1)} %collective-permute-done.7.refs_3_) | copy-start | bytes 2654212
  31.8 11.5 %copy-start.19 = (bf16[3,96,1536]{2,1,0:T(8,128)(2,1)}, bf16[3,96,1536]{2,1,0:T(8,128)(2,1)S(1)}, u32[]{:S(2)}) copy-start(bf16[3,96,1536]{2,1,0:T(8,128)(2,1)S(1)} %collective-permute-done.8.refs_4_) | copy-start | bytes 2654212
  43.2 4.4 %copy-start.14 = (bf16[3,96,1536]{2,1,0:T(8,128)(2,1)S(1)}, bf16[3,96,1536]{2,1,0:T(8,128)(2,1)}, u32[]{:S(2)}) copy-start(bf16[3,96,1536]{2,1,0:T(8,128)(2,1)} %get-tuple-element.27.refs_2_) | copy-start | bytes 2654212
  43.3 3.4 %collective-permute-start.12 = (bf16[3,96,1536]{2,1,0:T(8,128)(2,1)}, bf16[3,96,1536]{2,1,0:T(8,128)(2,1)S(1)}, u32[]{:S(2)}, u32[]{:S(2)}) collective-permute-start(bf16[3,96,1536]{2,1,0:T(8,128)(2,1)} %get-tuple-element.33.refs_6_), channel_id=1, source_target_pairs={{0,1},{1,0},{2,3},{3,2},{4,5},{5,4},{6,7},{7,6},{8,9},{9,8},{10,11... | collective-permute-start | bytes 2654216 | tf_op jit(solution)/shard_map/ppermute | solution.py:22
  44.4 19.2 %collective-permute-start.9 = (bf16[3,96,1536]{2,1,0:T(8,128)(2,1)}, bf16[3,96,1536]{2,1,0:T(8,128)(2,1)S(1)}, u32[]{:S(2)}, u32[]{:S(2)}) collective-permute-start(bf16[3,96,1536]{2,1,0:T(8,128)(2,1)} %get-tuple-element.28.refs_1_), channel_id=1, source_target_pairs={{0,4},{1,13},{4,8},{5,1},{8,12},{9,5},{12,0},{13,9},{2,6},{3,15},{... | collective-permute-start | bytes 2654216 | tf_op jit(solution)/shard_map/ppermute | solution.py:29
  44.4 19.2 %collective-permute-start.11 = (bf16[3,96,1536]{2,1,0:T(8,128)(2,1)}, bf16[3,96,1536]{2,1,0:T(8,128)(2,1)S(1)}, u32[]{:S(2)}, u32[]{:S(2)}) collective-permute-start(bf16[3,96,1536]{2,1,0:T(8,128)(2,1)} %get-tuple-element.29.refs_0_), channel_id=1, source_target_pairs={{0,1},{1,0},{2,3},{3,2},{4,5},{5,4},{6,7},{7,6},{8,9},{9,8},{10,11... | collective-permute-start | bytes 2654216 | tf_op jit(solution)/shard_map/ppermute | solution.py:22
  44.6 19.0 %collective-permute-start.10 = (bf16[3,96,1536]{2,1,0:T(8,128)(2,1)}, bf16[3,96,1536]{2,1,0:T(8,128)(2,1)S(1)}, u32[]{:S(2)}, u32[]{:S(2)}) collective-permute-start(bf16[3,96,1536]{2,1,0:T(8,128)(2,1)} %get-tuple-element.29.refs_0_), channel_id=1, source_target_pairs={{0,2},{1,131},{2,128},{3,1},{128,130},{129,3},{130,0},{131,129},{4... | collective-permute-start | bytes 2654216 | tf_op jit(solution)/shard_map/ppermute | solution.py:36
  46.6 1.0 copy-start.26
  47.6 1.2 copy-start.8
  48.8 1.2 copy-start.16
  49.9 1.2 copy-start.18
  51.1 1.2 copy-start.20
  52.3 1.2 copy-start.25
  63.5 1.0 copy-start.1
  63.5 1.2 %copy-start.3 = (bf16[3,96,1536]{2,1,0:T(8,128)(2,1)}, bf16[3,96,1536]{2,1,0:T(8,128)(2,1)S(1)}, u32[]{:S(2)}) copy-start(bf16[3,96,1536]{2,1,0:T(8,128)(2,1)S(1)} %collective-permute-done.11.refs_2_) | copy-start | bytes 2654212
  64.8 0.9 copy-start.5
  65.7 2.6 %collective-permute-start.15 = (bf16[3,96,1536]{2,1,0:T(8,128)(2,1)}, bf16[3,96,1536]{2,1,0:T(8,128)(2,1)S(1)}, u32[]{:S(2)}, u32[]{:S(2)}) collective-permute-start(bf16[3,96,1536]{2,1,0:T(8,128)(2,1)} %get-tuple-element.37.refs_4_), channel_id=1, source_target_pairs={{0,1},{1,0},{2,3},{3,2},{4,5},{5,4},{6,7},{7,6},{8,9},{9,8},{10,11... | collective-permute-start | bytes 2654216 | tf_op jit(solution)/shard_map/ppermute | solution.py:22
  66.1 3.5 %collective-permute-start.14 = (bf16[3,96,1536]{2,1,0:T(8,128)(2,1)}, bf16[3,96,1536]{2,1,0:T(8,128)(2,1)S(1)}, u32[]{:S(2)}, u32[]{:S(2)}) collective-permute-start(bf16[3,96,1536]{2,1,0:T(8,128)(2,1)} %get-tuple-element.34.refs_2_), channel_id=1, source_target_pairs={{0,1},{1,0},{2,3},{3,2},{4,5},{5,4},{6,7},{7,6},{8,9},{9,8},{10,11... | collective-permute-start | bytes 2654216 | tf_op jit(solution)/shard_map/ppermute | solution.py:22
  66.2 17.4 %collective-permute-start.13 = (bf16[3,96,1536]{2,1,0:T(8,128)(2,1)}, bf16[3,96,1536]{2,1,0:T(8,128)(2,1)}, u32[]{:S(2)}, u32[]{:S(2)}) collective-permute-start(bf16[3,96,1536]{2,1,0:T(8,128)(2,1)} %get-tuple-element.34.refs_2_), channel_id=1, source_target_pairs={{0,2},{1,131},{2,128},{3,1},{128,130},{129,3},{130,0},{131,129},{4... | collective-permute-start | bytes 2654216 | tf_op jit(solution)/shard_map/ppermute | solution.py:36
  69.6 1.2 copy-start.2
  70.8 1.2 copy-start.4
  72.0 1.2 copy-start.6
  83.6 2.7 %copy-start = (bf16[1536,1024]{1,0:T(8,128)(2,1)S(1)}, bf16[1536,1024]{1,0:T(8,128)(2,1)}, u32[]{:S(2)}) copy-start(bf16[1536,1024]{1,0:T(8,128)(2,1)} %refs_4_.3) | copy-start | bytes 9437188
  83.6 2.7 %copy-start.10 = (bf16[2,400,192]{2,1,0:T(8,128)(2,1)S(1)}, bf16[2,400,192]{2,1,0:T(8,128)(2,1)}, u32[]{:S(2)}) copy-start(bf16[2,400,192]{2,1,0:T(8,128)(2,1)} %copy-done.9) | copy-start | bytes 921604
  83.6 2.7 %collective-permute-start.16 = (bf16[3,96,1536]{2,1,0:T(8,128)(2,1)}, bf16[3,96,1536]{2,1,0:T(8,128)(2,1)S(1)}, u32[]{:S(2)}, u32[]{:S(2)}) collective-permute-start(bf16[3,96,1536]{2,1,0:T(8,128)(2,1)} %get-tuple-element.39.refs_0_), channel_id=1, source_target_pairs={{0,1},{1,0},{2,3},{3,2},{4,5},{5,4},{6,7},{7,6},{8,9},{9,8},{10,11... | collective-permute-start | bytes 2654216 | tf_op jit(solution)/shard_map/ppermute | solution.py:22
  86.4 0.7 copy-start.21
  87.1 0.7 copy-start.22
  95.9 21.7 %collective-permute-start.17 = (bf16[384,1024]{1,0:T(8,128)(2,1)S(1)}, bf16[384,1024]{1,0:T(8,128)(2,1)S(1)}, u32[]{:S(2)}, u32[]{:S(2)}) collective-permute-start(bf16[384,1024]{1,0:T(8,128)(2,1)S(1)} %finish.3), channel_id=1, source_target_pairs={{0,15},{1,14},{2,13},{3,12},{4,11},{5,10},{6,9},{7,8},{8,7},{9,6},... | collective-permute-start | bytes 2359304 | tf_op jit(solution)/shard_map/ppermute | solution.py:268

commit v3 on v2

v3 whole, which is shorter than its diff:
```python
import functools

import jax
import jax.numpy as jnp
from jax import lax
from jax.experimental import pallas as pl
from jax.experimental.pallas import tpu as pltpu
from jax.sharding import Mesh
from jax.sharding import PartitionSpec as P

AXES = ("y_hi", "z", "x", "y_lo", "core")
SEQ = ("x", "y_lo", "core")
XN, YN, CN = 4, 4, 2
VMEM_LIMIT = 24 * 1024 * 1024
EDGE = 16
TILE = 512
PARTS = (8, 6, 2)
ROWS = 128
TOKEN = jax.ShapeDtypeStruct((8, 128), jnp.float32)
INV_SQRT2 = 0.7071067811865476


def core_swap(value):
    return lax.ppermute(value, "core", [(0, 1), (1, 0)])


def x_shift(value):
    route = []
    for x in range(XN):
        route += [(x * 2, (x + 1) % XN * 2), (x * 2 + 1, (x - 1) % XN * 2 + 1)]
    return lax.ppermute(value, ("x", "core"), route)


def y_shift(value):
    route = []
    for y in range(YN):
        route += [(y * 2, (y + 1) % YN * 2), (y * 2 + 1, (y - 1) % YN * 2 + 1)]
    return lax.ppermute(value, ("y_hi", "y_lo", "core"), route)


def fence_kernel(count, *refs):
    for source, target in zip(refs[:count], refs[-count:]):
        target[...] = source[...]


def fence(token, *values):
    inside = pl.BlockSpec(memory_space=pltpu.VMEM)
    operands = values if token is None else (*values, token)
    return pl.pallas_call(
        functools.partial(fence_kernel, len(values)),
        out_shape=[jax.ShapeDtypeStruct(v.shape, v.dtype) for v in values],
        in_specs=[inside] * len(operands),
        out_specs=[inside] * len(values),
        input_output_aliases={i: i for i in range(len(values))},
        compiler_params=pltpu.CompilerParams(vmem_limit_bytes=8 * 1024 * 1024),
        name="fence",
    )(*operands)


def prepare_kernel(place_ref, forward_ref, reverse_ref, low_ref, high_ref, *refs):
    out_refs, (token_ref, full_ref, reverse_vmem, sem) = refs[:3], refs[3:]
    token_ref[...] = jnp.zeros_like(token_ref)
    rows, width = forward_ref.shape
    part = width // 16
    forward_copy = pltpu.make_async_copy(forward_ref, full_ref.at[0, pl.ds(0, rows), :], sem.at[0])
    forward_copy.start()
    reverse_copy = pltpu.make_async_copy(reverse_ref, reverse_vmem, sem.at[1])
    reverse_copy.start()
    row = lax.broadcasted_iota(jnp.int32, (rows, rows), 0)
    column = lax.broadcasted_iota(jnp.int32, (rows, rows), 1)
    flip = jnp.where(row + column == rows - 1, 1.0, 0.0).astype(jnp.bfloat16)
    reverse_copy.wait()
    full_ref[1, :rows, :] = jnp.dot(
        flip, reverse_vmem[...], preferred_element_type=jnp.float32
    ).astype(jnp.bfloat16)
    edge = lax.broadcasted_iota(jnp.int32, (EDGE, width), 0)
    low = low_ref[...].astype(jnp.float32)
    high = high_ref[...].astype(jnp.float32)
    for strand, after, before in ((0, high[0:1], low[0:1]), (1, low[1:2], high[1:2])):
        tile = jnp.where(edge == 0, after, jnp.where(edge == EDGE - 1, before, 0.0))
        full_ref[strand, rows:, :] = tile.astype(jnp.bfloat16)
    forward_copy.wait()
    begin = 0
    for out_ref, count in zip(out_refs, PARTS):
        size = count * part
        lane = lax.broadcasted_iota(jnp.int32, (1, size), 1)
        wanted = jnp.zeros((1, size), jnp.int32)
        for block in range(count):
            inside = (lane >= block * part) & (lane < (block + 1) * part)
            wanted = jnp.where(inside, lane + (place_ref[begin + block] - block) * part, wanted)
        source = lax.broadcasted_iota(jnp.int32, (width, size), 0)
        move = jnp.where(source == wanted, 1.0, 0.0).astype(jnp.bfloat16)
        for strand in range(2):
            out_ref[strand] = jnp.dot(
                full_ref[strand], move, preferred_element_type=jnp.float32
            ).astype(jnp.bfloat16)
        begin += count


def prepare(place, forward_embed, reverse_embed, low, high):
    rows, width = forward_embed.shape
    part = width // 16
    inside = pl.BlockSpec(memory_space=pltpu.VMEM)
    return pl.pallas_call(
        prepare_kernel,
        out_shape=[
            jax.ShapeDtypeStruct((2, rows + EDGE, count * part), jnp.bfloat16) for count in PARTS
        ]
        + [TOKEN],
        in_specs=[pl.BlockSpec(memory_space=pltpu.SMEM)]
        + [pl.BlockSpec(memory_space=pltpu.HBM)] * 2
        + [inside] * 2,
        out_specs=[inside] * 4,
        scratch_shapes=[
            pltpu.VMEM((2, rows + EDGE, width), jnp.bfloat16),
            pltpu.VMEM((rows, width), jnp.bfloat16),
            pltpu.SemaphoreType.DMA((2,)),
        ],
        compiler_params=pltpu.CompilerParams(vmem_limit_bytes=VMEM_LIMIT),
        cost_estimate=pl.CostEstimate(
            flops=4 * rows * width * width, bytes_accessed=8 * rows * width, transcendentals=0
        ),
        name="prepare",
    )(place, forward_embed, reverse_embed, low, high)


def convolve(x, flipped, blocks, columns):
    rows = x.shape[0] - EDGE
    total = None
    for tap in range(3):
        weight = jnp.concatenate([block[tap, :, columns] for block in blocks], axis=0)
        value = jnp.dot(x, weight, preferred_element_type=jnp.float32)
        shift = tap - 1 if flipped else 1 - tap
        if shift:
            value = pltpu.roll(value, shift % (rows + EDGE), 0)
        value = value[:rows]
        total = value if total is None else total + value
    return total


def partial_kernel(count, first, x_ref, *refs):
    blocks, refs = refs[:count], refs[count:]
    out_ref, token_ref = refs[-2:]
    token_ref[...] = jnp.zeros_like(token_ref)
    channels = out_ref.shape[2]
    for start in range(0, channels, TILE):
        columns = pl.ds(start, TILE)
        for strand in range(2):
            acc = convolve(x_ref[strand], strand == 1, blocks, columns)
            if not first:
                acc = acc + refs[0][strand, :, columns]
            out_ref[strand, :, columns] = acc


def partial_sum(x, sources, prev):
    rows, depth = x.shape[1] - EDGE, x.shape[2]
    channels = sources[0].shape[2]
    operands = [x, *sources] + ([] if prev is None else [prev])
    inside = pl.BlockSpec(memory_space=pltpu.VMEM)
    return pl.pallas_call(
        functools.partial(partial_kernel, len(sources), prev is None),
        out_shape=[jax.ShapeDtypeStruct((2, rows, channels), jnp.float32), TOKEN],
        in_specs=[inside] * len(operands),
        out_specs=[inside] * 2,
        input_output_aliases={} if prev is None else {len(operands) - 1: 0},
        compiler_params=pltpu.CompilerParams(vmem_limit_bytes=VMEM_LIMIT),
        cost_estimate=pl.CostEstimate(
            flops=12 * rows * depth * channels,
            bytes_accessed=6 * depth * channels,
            transcendentals=0,
        ),
        name="partial_sum",
    )(*operands)


def finish_kernel(strand, groups, x_ref, *refs):
    count = sum(groups)
    sources, refs = refs[:count], refs[count:]
    prev_ref, bias_ref, head_ref, head_bias_ref, out_ref, hidden_ref = refs
    rows = out_ref.shape[0]
    start = 0
    for count in groups:
        blocks, sources = sources[:count], sources[count:]
        width = blocks[0].shape[2]
        here = pl.ds(start, width)
        acc = convolve(x_ref[strand], strand == 1, blocks, pl.ds(0, width))
        acc = acc + prev_ref[strand, :, here] + bias_ref[:, here]
        hidden = 0.5 * acc * (1.0 + lax.erf(acc * INV_SQRT2))
        hidden_ref[:, here] = hidden.astype(jnp.bfloat16)
        start += width
    for row in range(0, rows, ROWS):
        logits = jnp.dot(
            hidden_ref[pl.ds(row, ROWS), :], head_ref[...], preferred_element_type=jnp.float32
        )
        logits = logits + head_bias_ref[...]
        tracks = jnp.maximum(logits, 0.0) + jnp.log1p(jnp.exp(-jnp.abs(logits)))
        out_ref[pl.ds(row, ROWS), :] = tracks.astype(jnp.bfloat16)


def finish(strand, x, groups, prev, bias, head, head_bias):
    rows, depth = x.shape[1] - EDGE, x.shape[2]
    channels, tracks = head.shape
    sources = [value for group in groups for value in group]
    inside = pl.BlockSpec(memory_space=pltpu.VMEM)
    return pl.pallas_call(
        functools.partial(finish_kernel, strand, tuple(len(group) for group in groups)),
        out_shape=jax.ShapeDtypeStruct((rows, tracks), jnp.bfloat16),
        in_specs=[inside] * (len(sources) + 5),
        out_specs=inside,
        scratch_shapes=[pltpu.VMEM((rows, channels), jnp.bfloat16)],
        compiler_params=pltpu.CompilerParams(vmem_limit_bytes=VMEM_LIMIT),
        cost_estimate=pl.CostEstimate(
            flops=2 * rows * channels * (3 * depth + tracks),
            bytes_accessed=6 * depth * channels + 2 * channels * tracks,
            transcendentals=rows * channels,
        ),
        name="finish",
    )(x, *sources, prev, bias, head, head_bias[None])


def per_device(forward_embed, reverse_embed, conv_weight, conv_bias, head_weight, head_bias):
    own = conv_weight[0]
    x, y, core = lax.axis_index("x"), lax.axis_index("y_lo"), lax.axis_index("core")
    ends = XN * 2 * CN

    def seq(x_of, y_of, core_of):
        return (x_of % XN) * 4 + y_of * 2 + core_of

    step = 1 - 2 * core
    back, fore, far = x - step + XN, x + step + XN, x + 2
    other, over = 1 - core, 1 - y
    place = jnp.stack(
        [
            seq(x, y, core), seq(x, y, other), seq(x, over, core), seq(x, over, other),
            seq(back, y, core), seq(fore, y, other), seq(back, over, core), seq(fore, over, other),
            seq(far, y, core), seq(far, y, other), seq(back, y, other), seq(fore, y, core),
            seq(far, over, core), seq(far, over, other),
            seq(back, over, other), seq(fore, over, core),
        ]
    ).astype(jnp.int32)

    near = x_shift(own)
    across = y_shift(own)
    sibling = core_swap(own)
    up = [(i, i + 1) for i in range(ends - 1)]
    down = [(b, a) for a, b in up]
    low = lax.ppermute(jnp.stack([forward_embed[-1], reverse_embed[-1]]), SEQ, up)
    high = lax.ppermute(jnp.stack([forward_embed[0], reverse_embed[0]]), SEQ, down)
    near, across, low, high = fence(None, near, across, low, high)

    distant = x_shift(near)
    near_over = y_shift(near)
    across_b = core_swap(across)
    near_b = core_swap(near)
    x_1, x_2, x_3, token = prepare(place, forward_embed, reverse_embed, low, high)
    distant, near_over, sibling = fence(token, distant, near_over, sibling)

    second = x_shift(sibling)
    distant_over = y_shift(distant)
    near_over_b = core_swap(near_over)
    distant_b = core_swap(distant)
    half = own.shape[2] // 2
    across_half = across_b[:, :, :half]
    acc, token = partial_sum(
        x_1, [own, sibling, across, across_b, near, near_b, near_over, near_over_b], None
    )
    second, distant_over, across_half = fence(token, second, distant_over, across_half)

    over_low = x_shift(across_half)
    over_high = y_shift(second[:, :, half:])
    second_b = core_swap(second)
    distant_over_b = core_swap(distant_over)
    acc, token = partial_sum(
        x_2, [distant, distant_b, second, second_b, distant_over, distant_over_b], acc
    )
    over_low, over_high = fence(token, over_low, over_high)

    last = [[over_low, core_swap(over_low)], [over_high, core_swap(over_high)]]
    reverse_tracks = finish(1, x_3, last, acc, conv_bias, head_weight, head_bias)
    forward_tracks = finish(0, x_3, last, acc, conv_bias, head_weight, head_bias)
    mirrored = lax.ppermute(reverse_tracks, SEQ, [(i, ends - 1 - i) for i in range(ends)])
    mean = 0.5 * (forward_tracks.astype(jnp.float32) + mirrored.astype(jnp.float32))
    return mean.astype(jnp.bfloat16)


def solution(mesh):
    fine = Mesh(mesh.devices.reshape(2, 8, XN, 2, CN), AXES)
    return jax.shard_map(
        per_device,
        mesh=fine,
        in_specs=(
            P(AXES, None),
            P(AXES, None),
            P(None, None, SEQ, None),
            P(),
            P(),
            P(),
        ),
        out_specs=P(AXES, None),
        check_vma=False,
    )
```

time: 120 us -> 91.9 us (0.77)
  local copies, waits for them, and re-layouts: 21.6 us -> 4.69 us
  Pallas kernels: 43 us -> 31.3 us
  starting transfers between devices: 22.4 us -> 24.7 us
    unnamed x54 -> x14, local copies, waits for them, and re-layouts: 20.7 us -> 3.18 us
    pallas_call x2, Pallas kernels: 20.6 us -> 14 us  [partial_sum(): pl.pallas_call(functools.partial(partial_kernel, len(sources), prev is No...]
    ppermute x1, waiting for transfers between devices: 10.6 us -> 16.6 us  [per_device(): lax.ppermute(reverse_tracks, SEQ, [(i, ends - 1 - i) for i in range(ends)])]
    pallas_call x6, Pallas kernels: 16.3 us -> 10.4 us  [the longest x2 7.6 us: finish(): pl.pallas_call(functools.partial(finish_kernel, strand, tuple((len(group)...]
    ppermute x3 -> x4, starting transfers between devices: 2.49 us -> 7.82 us  [x_shift(): return lax.ppermute(value, ('x', 'core'), route)]
    ppermute x4, waiting for transfers between devices: 9.25 us -> 3.93 us  [y_shift(): return lax.ppermute(value, ('y_hi', 'y_lo', 'core'), route)]
    ppermute x8 -> x9, waiting for transfers between devices: 5.47 us -> 3.26 us  [core_swap(): return lax.ppermute(value, 'core', [(0, 1), (1, 0)])]
    ppermute x1, starting transfers between devices: 2.93 us -> 1.6 us  [per_device(): lax.ppermute(reverse_tracks, SEQ, [(i, ends - 1 - i) for i in range(ends)])]
  transfers between devices with their start and end apart: 18 -> 20, of which waited for: 9 -> 9; matrix products, arithmetic and copies ran while one was open for 1% -> 2% of each run, Pallas kernels for 29% -> 30%
where the time goes in v3:
time: 91.9 us; the launch traced here: 91.6 us
  Pallas kernels  31.3 us (34%)
  waiting for transfers between devices  29.5 us (32%)
  starting transfers between devices  24.7 us (27%)
  local copies, waits for them, and re-layouts  4.69 us (5%)
  other arithmetic  1.22 us (1%)
    ppermute x1, waiting for transfers between devices, per_device(): lax.ppermute(reverse_tracks, SEQ, [(i, ends - 1 - i) for i in range(ends)])  16.6 us
    pallas_call x2, Pallas kernels, partial_sum(): pl.pallas_call(functools.partial(partial_kernel, len(sources), prev is No...  14 us
    ppermute x4, starting transfers between devices, x_shift(): return lax.ppermute(value, ('x', 'core'), route)  7.82 us
    pallas_call x2, Pallas kernels, finish(): pl.pallas_call(functools.partial(finish_kernel, strand, tuple((len(group)...  7.6 us
    pallas_call x1, Pallas kernels, prepare(): pl.pallas_call(prepare_kernel, out_shape=[jax.ShapeDtypeStruct((2, rows +...  6.83 us
    ppermute x4, starting transfers between devices, y_shift(): return lax.ppermute(value, ('y_hi', 'y_lo', 'core'), route)  5.91 us
    ppermute x9, starting transfers between devices, core_swap(): return lax.ppermute(value, 'core', [(0, 1), (1, 0)])  5.06 us
    ppermute x4, waiting for transfers between devices, y_shift(): return lax.ppermute(value, ('y_hi', 'y_lo', 'core'), route)  3.93 us
  transfers between devices with their start and end apart: 20, of which 9 were waited for; matrix products, arithmetic and copies ran while one was open for 2% of the time, Pallas kernels for 30%

profile of v3, /device:TPU:1, one launch (start us, length us, event | category | flops | bytes accessed | tf_op | source)
XLA Modules:
  0.0 91.6 jit_solution(9256673519021529718)
XLA Ops:
  0.0 3.3 %collective-permute-start = (bf16[3,96,1536]{2,1,0:T(8,128)(2,1)}, bf16[3,96,1536]{2,1,0:T(8,128)(2,1)S(1)}, u32[]{:S(2)}, u32[]{:S(2)}) collective-permute-start(bf16[3,96,1536]{2,1,0:T(8,128)(2,1)} %bitcast.20), channel_id=1, source_target_pairs={{0,4},{1,13},{4,8},{5,1},{8,12},{9,5},{12,0},{13,9},{2,6},{3,15},{... | collective-permute-start | bytes 2654216 | tf_op jit(solution)/shard_map/ppermute | solution.py:31
  3.3 2.7 %collective-permute-start.1 = (bf16[3,96,1536]{2,1,0:T(8,128)(2,1)}, bf16[3,96,1536]{2,1,0:T(8,128)(2,1)S(1)}, u32[]{:S(2)}, u32[]{:S(2)}) collective-permute-start(bf16[3,96,1536]{2,1,0:T(8,128)(2,1)} %bitcast.21), channel_id=1, source_target_pairs={{0,2},{1,131},{2,128},{3,1},{128,130},{129,3},{130,0},{131,129},{4... | collective-permute-start | bytes 2654216 | tf_op jit(solution)/shard_map/ppermute | solution.py:38
  6.0 0.8 fusion
  6.9 1.9 %collective-permute-start.2 = (bf16[2,1536]{1,0:T(2,128)(2,1)S(1)}, bf16[2,1536]{1,0:T(2,128)(2,1)S(1)}, u32[]{:S(2)}, u32[]{:S(2)}) collective-permute-start(bf16[2,1536]{1,0:T(2,128)(2,1)S(1)} %pad_maximum_fusion), channel_id=1, source_target_pairs={{0,1},{1,2},{2,3},{3,4},{4,5},{5,6},{6,7},{7,8},{8,9},{9,10},{10,1... | collective-permute-start | bytes 18440 | tf_op jit(solution)/shard_map/ppermute | solution.py:247
  8.8 2.4 %collective-permute-start.3 = (bf16[2,1536]{1,0:T(2,128)(2,1)S(1)}, bf16[2,1536]{1,0:T(2,128)(2,1)S(1)}, u32[]{:S(2)}, u32[]{:S(2)}) collective-permute-start(bf16[2,1536]{1,0:T(2,128)(2,1)S(1)} %pad_maximum_fusion.1), channel_id=1, source_target_pairs={{1,0},{2,1},{3,2},{4,3},{5,4},{6,5},{7,6},{8,7},{9,8},{10,9},{11,1... | collective-permute-start | bytes 18440 | tf_op jit(solution)/shard_map/ppermute | solution.py:248
  11.3 0.1 collective-permute-start.6
  11.4 0.0 collective-permute-done.2.refs_2_
  11.4 2.8 %collective-permute-done.3.refs_3_ = bf16[2,1536]{1,0:T(2,128)(2,1)S(1)} collective-permute-done((bf16[2,1536]{1,0:T(2,128)(2,1)S(1)}, bf16[2,1536]{1,0:T(2,128)(2,1)S(1)}, u32[]{:S(2)}, u32[]{:S(2)}) %collective-permute-start.3) | collective-permute-done | bytes 6176 | tf_op jit(solution)/shard_map/ppermute | solution.py:248
  14.2 0.0 collective-permute-done.refs_0_
  14.2 2.1 %collective-permute-done.1.refs_1_ = bf16[3,96,1536]{2,1,0:T(8,128)(2,1)S(1)} collective-permute-done((bf16[3,96,1536]{2,1,0:T(8,128)(2,1)}, bf16[3,96,1536]{2,1,0:T(8,128)(2,1)S(1)}, u32[]{:S(2)}, u32[]{:S(2)}) %collective-permute-start.1) | collective-permute-done | bytes 884768 | tf_op jit(solution)/shard_map/ppermute | solution.py:38
  16.3 0.2 fence.4
  16.6 0.7 collective-permute-start.4
  17.2 3.0 %collective-permute-start.5 = (bf16[3,96,1536]{2,1,0:T(8,128)(2,1)S(1)}, bf16[3,96,1536]{2,1,0:T(8,128)(2,1)}, u32[]{:S(2)}, u32[]{:S(2)}) collective-permute-start(bf16[3,96,1536]{2,1,0:T(8,128)(2,1)S(1)} %get-tuple-element.28.refs_4_), channel_id=1, source_target_pairs={{0,2},{1,131},{2,128},{3,1},{128,130},{129,3},{130,0},{131,129},{4... | collective-permute-start | bytes 2654216 | tf_op jit(solution)/shard_map/ppermute | solution.py:38
  20.2 0.6 stack.73.place_ref
  20.8 0.5 collective-permute-start.9
  21.4 0.6 copy-done.3
  22.0 1.3 %copy-done.4 = bf16[384,1536]{1,0:T(8,128)(2,1)S(1)} copy-done((bf16[384,1536]{1,0:T(8,128)(2,1)S(1)}, bf16[384,1536]{1,0:T(8,128)(2,1)}, u32[]{:S(2)}) %copy-start.4) | copy-done | bytes 1179672
  23.3 1.3 %copy-done.5 = bf16[384,1536]{1,0:T(8,128)(2,1)S(1)} copy-done((bf16[384,1536]{1,0:T(8,128)(2,1)S(1)}, bf16[384,1536]{1,0:T(8,128)(2,1)}, u32[]{:S(2)}) %copy-start.5) | copy-done | bytes 1179672
  24.5 6.8 %prepare.1 = (bf16[2,400,768]{2,1,0:T(8,128)(2,1)S(1)}, bf16[2,400,576]{2,1,0:T(8,128)(2,1)S(1)}, bf16[2,400,192]{2,1,0:T(8,128)(2,1)S(1)}, f32[8,128]{1,0:T(8,128)S(1)}) custom-call(s32[16]{0:T(128)S(1)} %copy-done.3, bf16[384,1536]{1,0:T(8,128)(2,1)S(1)} %copy-done.4, bf16[384,1536]{1,0:T(8,128)(2,1)S(1)} %copy-done.5, ...), custom_call_target="tpu_custom_call" | custom-call | flops 3623878656 | bytes 4718592 | tf_op jit(solution)/shard_map/prepare/pallas_call | solution.py:104
  31.4 0.0 collective-permute-done.4.refs_0_
  31.4 0.0 collective-permute-done.5.refs_1_
  31.4 0.0 copy-start.6
  31.4 2.2 %fence.5 = (bf16[3,96,1536]{2,1,0:T(8,128)(2,1)S(1)}, bf16[3,96,1536]{2,1,0:T(8,128)(2,1)}, bf16[3,96,1536]{2,1,0:T(8,128)(2,1)S(1)}) custom-call(bf16[3,96,1536]{2,1,0:T(8,128)(2,1)S(1)} %collective-permute-done.4.refs_0_, bf16[3,96,1536]{2,1,0:T(8,128)(2,1)} %collective-permute-done.5.refs_1_, ...), custom_call_target="tpu_custom_call", output_to_operand_aliasing={{0}: (0, {}), {1}: (1, {}), {2}: (2, {})} | custom-call | tf_op jit(solution)/shard_map/fence/pallas_call | solution.py:49
  33.6 2.2 %collective-permute-start.11 = (bf16[3,96,1536]{2,1,0:T(8,128)(2,1)}, bf16[3,96,1536]{2,1,0:T(8,128)(2,1)S(1)}, u32[]{:S(2)}, u32[]{:S(2)}) collective-permute-start(bf16[3,96,1536]{2,1,0:T(8,128)(2,1)} %get-tuple-element.34.refs_6_), channel_id=1, source_target_pairs={{0,1},{1,0},{2,3},{3,2},{4,5},{5,4},{6,7},{7,6},{8,9},{9,8},{10,11... | collective-permute-start | bytes 2654216 | tf_op jit(solution)/shard_map/ppermute | solution.py:24
  35.8 1.8 %collective-permute-start.7 = (bf16[3,96,1536]{2,1,0:T(8,128)(2,1)S(1)}, bf16[3,96,1536]{2,1,0:T(8,128)(2,1)S(1)}, u32[]{:S(2)}, u32[]{:S(2)}) collective-permute-start(bf16[3,96,1536]{2,1,0:T(8,128)(2,1)S(1)} %get-tuple-element.30.refs_1_), channel_id=1, source_target_pairs={{0,4},{1,13},{4,8},{5,1},{8,12},{9,5},{12,0},{13,9},{2,6},{3,15},{... | collective-permute-start | bytes 2654216 | tf_op jit(solution)/shard_map/ppermute | solution.py:31
  37.6 0.1 collective-permute-start.8
  37.8 0.0 collective-permute-start.14
  37.8 0.3 collective-permute-done.11.refs_7_
  38.1 7.1 %partial_sum.2 = (f32[2,384,1536]{2,1,0:T(8,128)S(1)}, f32[8,128]{1,0:T(8,128)S(1)}) custom-call(bf16[2,400,768]{2,1,0:T(8,128)(2,1)S(1)} %get-tuple-element.33.x_ref, bf16[3,96,1536]{2,1,0:T(8,128)(2,1)S(1)} %bitcast.23, bf16[3,96,1536]{2,1,0:T(8,128)(2,1)S(1)} %get-tuple-element.30.refs_1_, bf16[3,96,1536]{2,1,0:T(8,128)(2,1)S(1)} %get-tuple-element.32.refs_2_, ...), custom_call_target="tpu_custom_call" | custom-call | flops 5435817984 | bytes 7077888 | tf_op jit(solution)/shard_map/partial_sum/pallas_call | solution.py:160
  45.2 2.8 %collective-permute-done.7.refs_0_ = bf16[3,96,1536]{2,1,0:T(8,128)(2,1)S(1)} collective-permute-done((bf16[3,96,1536]{2,1,0:T(8,128)(2,1)S(1)}, bf16[3,96,1536]{2,1,0:T(8,128)(2,1)S(1)}, u32[]{:S(2)}, u32[]{:S(2)}) %collective-permute-start.7) | collective-permute-done | bytes 884768 | tf_op jit(solution)/shard_map/ppermute | solution.py:31
  48.0 1.8 %collective-permute-done.8.refs_1_ = bf16[3,96,1536]{2,1,0:T(8,128)(2,1)S(1)} collective-permute-done((bf16[3,96,1536]{2,1,0:T(8,128)(2,1)S(1)}, bf16[3,96,1536]{2,1,0:T(8,128)(2,1)S(1)}, u32[]{:S(2)}, u32[]{:S(2)}) %collective-permute-start.8) | collective-permute-done | bytes 884768 | tf_op jit(solution)/shard_map/ppermute | solution.py:38
  49.8 0.3 fence.6
  50.1 1.6 %collective-permute-start.15 = (bf16[3,96,1536]{2,1,0:T(8,128)(2,1)S(1)}, bf16[3,96,1536]{2,1,0:T(8,128)(2,1)S(1)}, u32[]{:S(2)}, u32[]{:S(2)}) collective-permute-start(bf16[3,96,1536]{2,1,0:T(8,128)(2,1)S(1)} %get-tuple-element.37.refs_2_), channel_id=1, source_target_pairs={{0,1},{1,0},{2,3},{3,2},{4,5},{5,4},{6,7},{7,6},{8,9},{9,8},{10,11... | collective-permute-start | bytes 2654216 | tf_op jit(solution)/shard_map/ppermute | solution.py:24
  51.6 0.1 collective-permute-start.16
  51.8 0.1 collective-permute-start.13
  51.9 2.1 %collective-permute-start.12 = (bf16[3,96,768]{2,1,0:T(8,128)(2,1)S(1)}, bf16[3,96,768]{2,1,0:T(8,128)(2,1)S(1)}, u32[]{:S(2)}, u32[]{:S(2)}) collective-permute-start(bf16[3,96,768]{2,1,0:T(8,128)(2,1)S(1)} %get-tuple-element.36), channel_id=1, source_target_pairs={{0,4},{1,13},{4,8},{5,1},{8,12},{9,5},{12,0},{13,9},{2,6},{3,15},{... | collective-permute-start | bytes 1327112 | tf_op jit(solution)/shard_map/ppermute | solution.py:31
  53.9 1.0 %collective-permute-done.16.refs_5_ = bf16[3,96,1536]{2,1,0:T(8,128)(2,1)S(1)} collective-permute-done((bf16[3,96,1536]{2,1,0:T(8,128)(2,1)S(1)}, bf16[3,96,1536]{2,1,0:T(8,128)(2,1)S(1)}, u32[]{:S(2)}, u32[]{:S(2)}) %collective-permute-start.16) | collective-permute-done | bytes 884768 | tf_op jit(solution)/shard_map/ppermute | solution.py:24
  55.0 6.9 %partial_sum.3 = (f32[2,384,1536]{2,1,0:T(8,128)S(1)}, f32[8,128]{1,0:T(8,128)S(1)}) custom-call(bf16[2,400,576]{2,1,0:T(8,128)(2,1)S(1)} %get-tuple-element.38.x_ref, bf16[3,96,1536]{2,1,0:T(8,128)(2,1)S(1)} %get-tuple-element.31.refs_0_, bf16[3,96,1536]{2,1,0:T(8,128)(2,1)S(1)} %collective-permute-done.14.refs_1_, ...), custom_call_target="tpu_custom_call", output_to_operand_aliasing={{0}: (7, {})} | custom-call | flops 4076863488 | bytes 5308416 | tf_op jit(solution)/shard_map/partial_sum/pallas_call | solution.py:160
  61.9 0.1 fence.7
  62.0 0.5 collective-permute-start.17
  62.5 0.1 collective-permute-start.18
  62.6 1.3 %collective-permute-done.17.refs_1_ = bf16[3,96,768]{2,1,0:T(8,128)(2,1)S(1)} collective-permute-done((bf16[3,96,768]{2,1,0:T(8,128)(2,1)S(1)}, bf16[3,96,768]{2,1,0:T(8,128)(2,1)S(1)}, u32[]{:S(2)}, u32[]{:S(2)}) %collective-permute-start.17) | collective-permute-done | bytes 442400 | tf_op jit(solution)/shard_map/ppermute | solution.py:24
  63.9 0.6 collective-permute-done.18.refs_3_
  64.6 3.8 %finish.3 = bf16[384,1024]{1,0:T(8,128)(2,1)S(1)} custom-call(bf16[2,400,192]{2,1,0:T(8,128)(2,1)S(1)} %get-tuple-element.27.x_ref, bf16[3,96,768]{2,1,0:T(8,128)(2,1)S(1)} %get-tuple-element.42.refs_0_, bf16[3,96,768]{2,1,0:T(8,128)(2,1)S(1)} %collective-permute-done.17.refs_1_, bf16[3,96,768]{2,1,0:T(8,128)(2,1)S(1)} %get-tuple-element.43.refs_2_, ...), custom_call_target="tpu_custom_call" | custom-call | flops 1887436800 | bytes 4915200 | tf_op jit(solution)/shard_map/finish/pallas_call | solution.py:205
  68.4 1.6 %collective-permute-start.19 = (bf16[384,1024]{1,0:T(8,128)(2,1)S(1)}, bf16[384,1024]{1,0:T(8,128)(2,1)S(1)}, u32[]{:S(2)}, u32[]{:S(2)}) collective-permute-start(bf16[384,1024]{1,0:T(8,128)(2,1)S(1)} %finish.3), channel_id=1, source_target_pairs={{0,15},{1,14},{2,13},{3,12},{4,11},{5,10},{6,9},{7,8},{8,7},{9,6},... | collective-permute-start | bytes 2359304 | tf_op jit(solution)/shard_map/ppermute | solution.py:281
  70.0 3.8 %finish.2 = bf16[384,1024]{1,0:T(8,128)(2,1)S(1)} custom-call(bf16[2,400,192]{2,1,0:T(8,128)(2,1)S(1)} %get-tuple-element.27.x_ref, bf16[3,96,768]{2,1,0:T(8,128)(2,1)S(1)} %get-tuple-element.42.refs_0_, bf16[3,96,768]{2,1,0:T(8,128)(2,1)S(1)} %collective-permute-done.17.refs_1_, bf16[3,96,768]{2,1,0:T(8,128)(2,1)S(1)} %get-tuple-element.43.refs_2_, ...), custom_call_target="tpu_custom_call" | custom-call | flops 1887436800 | bytes 4915200 | tf_op jit(solution)/shard_map/finish/pallas_call | solution.py:205
  73.8 16.6 %collective-permute-done.19 = bf16[384,1024]{1,0:T(8,128)(2,1)S(1)} collective-permute-done((bf16[384,1024]{1,0:T(8,128)(2,1)S(1)}, bf16[384,1024]{1,0:T(8,128)(2,1)S(1)}, u32[]{:S(2)}, u32[]{:S(2)}) %collective-permute-start.19) | collective-permute-done | bytes 786464 | tf_op jit(solution)/shard_map/ppermute | solution.py:281
  90.4 1.2 %multiply_convert_fusion = bf16[384,1024]{1,0:T(8,128)(2,1)} fusion(bf16[384,1024]{1,0:T(8,128)(2,1)S(1)} %collective-permute-done.19, bf16[384,1024]{1,0:T(8,128)(2,1)S(1)} %finish.2), kind=kLoop, calls=%fused_computation | loop fusion | flops 1966080 | bytes 2359296 | tf_op jit(solution)/shard_map/convert_element_type | solution.py:283
  (22 shorter events, 0.1 us)
Async XLA Ops:
  0.0 14.2 %collective-permute-start = (bf16[3,96,1536]{2,1,0:T(8,128)(2,1)}, bf16[3,96,1536]{2,1,0:T(8,128)(2,1)S(1)}, u32[]{:S(2)}, u32[]{:S(2)}) collective-permute-start(bf16[3,96,1536]{2,1,0:T(8,128)(2,1)} %bitcast.20), channel_id=1, source_target_pairs={{0,4},{1,13},{4,8},{5,1},{8,12},{9,5},{12,0},{13,9},{2,6},{3,15},{... | collective-permute-start | bytes 2654216 | tf_op jit(solution)/shard_map/ppermute | solution.py:31
  3.3 13.0 %collective-permute-start.1 = (bf16[3,96,1536]{2,1,0:T(8,128)(2,1)}, bf16[3,96,1536]{2,1,0:T(8,128)(2,1)S(1)}, u32[]{:S(2)}, u32[]{:S(2)}) collective-permute-start(bf16[3,96,1536]{2,1,0:T(8,128)(2,1)} %bitcast.21), channel_id=1, source_target_pairs={{0,2},{1,131},{2,128},{3,1},{128,130},{129,3},{130,0},{131,129},{4... | collective-permute-start | bytes 2654216 | tf_op jit(solution)/shard_map/ppermute | solution.py:38
  6.9 4.5 %collective-permute-start.2 = (bf16[2,1536]{1,0:T(2,128)(2,1)S(1)}, bf16[2,1536]{1,0:T(2,128)(2,1)S(1)}, u32[]{:S(2)}, u32[]{:S(2)}) collective-permute-start(bf16[2,1536]{1,0:T(2,128)(2,1)S(1)} %pad_maximum_fusion), channel_id=1, source_target_pairs={{0,1},{1,2},{2,3},{3,4},{4,5},{5,6},{6,7},{7,8},{8,9},{9,10},{10,1... | collective-permute-start | bytes 18440 | tf_op jit(solution)/shard_map/ppermute | solution.py:247
  8.8 5.4 %collective-permute-start.3 = (bf16[2,1536]{1,0:T(2,128)(2,1)S(1)}, bf16[2,1536]{1,0:T(2,128)(2,1)S(1)}, u32[]{:S(2)}, u32[]{:S(2)}) collective-permute-start(bf16[2,1536]{1,0:T(2,128)(2,1)S(1)} %pad_maximum_fusion.1), channel_id=1, source_target_pairs={{1,0},{2,1},{3,2},{4,3},{5,4},{6,5},{7,6},{8,7},{9,8},{10,9},{11,1... | collective-permute-start | bytes 18440 | tf_op jit(solution)/shard_map/ppermute | solution.py:248
  11.3 20.1 %collective-permute-start.6 = (bf16[3,96,1536]{2,1,0:T(8,128)(2,1)}, bf16[3,96,1536]{2,1,0:T(8,128)(2,1)S(1)}, u32[]{:S(2)}, u32[]{:S(2)}) collective-permute-start(bf16[3,96,1536]{2,1,0:T(8,128)(2,1)} %bitcast.22), channel_id=1, source_target_pairs={{0,1},{1,0},{2,3},{3,2},{4,5},{5,4},{6,7},{7,6},{8,9},{9,8},{10,11... | collective-permute-start | bytes 2654216 | tf_op jit(solution)/shard_map/ppermute | solution.py:24
  16.6 14.8 %collective-permute-start.4 = (bf16[3,96,1536]{2,1,0:T(8,128)(2,1)S(1)}, bf16[3,96,1536]{2,1,0:T(8,128)(2,1)S(1)}, u32[]{:S(2)}, u32[]{:S(2)}) collective-permute-start(bf16[3,96,1536]{2,1,0:T(8,128)(2,1)S(1)} %get-tuple-element.28.refs_4_), channel_id=1, source_target_pairs={{0,4},{1,13},{4,8},{5,1},{8,12},{9,5},{12,0},{13,9},{2,6},{3,15},{... | collective-permute-start | bytes 2654216 | tf_op jit(solution)/shard_map/ppermute | solution.py:31
  17.2 14.2 %collective-permute-start.5 = (bf16[3,96,1536]{2,1,0:T(8,128)(2,1)S(1)}, bf16[3,96,1536]{2,1,0:T(8,128)(2,1)}, u32[]{:S(2)}, u32[]{:S(2)}) collective-permute-start(bf16[3,96,1536]{2,1,0:T(8,128)(2,1)S(1)} %get-tuple-element.28.refs_4_), channel_id=1, source_target_pairs={{0,2},{1,131},{2,128},{3,1},{128,130},{129,3},{130,0},{131,129},{4... | collective-permute-start | bytes 2654216 | tf_op jit(solution)/shard_map/ppermute | solution.py:38
  20.8 17.0 %collective-permute-start.10 = (bf16[3,96,1536]{2,1,0:T(8,128)(2,1)S(1)}, bf16[3,96,1536]{2,1,0:T(8,128)(2,1)S(1)}, u32[]{:S(2)}, u32[]{:S(2)}) collective-permute-start(bf16[3,96,1536]{2,1,0:T(8,128)(2,1)S(1)} %get-tuple-element.28.refs_4_), channel_id=1, source_target_pairs={{0,1},{1,0},{2,3},{3,2},{4,5},{5,4},{6,7},{7,6},{8,9},{9,8},{10,11... | collective-permute-start | bytes 2654216 | tf_op jit(solution)/shard_map/ppermute | solution.py:24
  20.8 16.9 %collective-permute-start.9 = (bf16[3,96,1536]{2,1,0:T(8,128)(2,1)S(1)}, bf16[3,96,1536]{2,1,0:T(8,128)(2,1)S(1)}, u32[]{:S(2)}, u32[]{:S(2)}) collective-permute-start(bf16[3,96,1536]{2,1,0:T(8,128)(2,1)S(1)} %get-tuple-element.32.refs_2_), channel_id=1, source_target_pairs={{0,1},{1,0},{2,3},{3,2},{4,5},{5,4},{6,7},{7,6},{8,9},{9,8},{10,11... | collective-permute-start | bytes 2654216 | tf_op jit(solution)/shard_map/ppermute | solution.py:24
  21.4 0.6 copy-start.3
  22.0 1.3 %copy-start.4 = (bf16[384,1536]{1,0:T(8,128)(2,1)S(1)}, bf16[384,1536]{1,0:T(8,128)(2,1)}, u32[]{:S(2)}) copy-start(bf16[384,1536]{1,0:T(8,128)(2,1)} %forward_ref.1) | copy-start | bytes 3538948
  23.3 1.3 %copy-start.5 = (bf16[384,1536]{1,0:T(8,128)(2,1)S(1)}, bf16[384,1536]{1,0:T(8,128)(2,1)}, u32[]{:S(2)}) copy-start(bf16[384,1536]{1,0:T(8,128)(2,1)} %reverse_ref.1) | copy-start | bytes 3538948
  31.4 6.7 %copy-start.6 = (bf16[1,3,96,1536]{3,2,1,0:T(8,128)(2,1)S(1)}, bf16[1,3,96,1536]{3,2,1,0:T(8,128)(2,1)}, u32[]{:S(2)}) copy-start(bf16[1,3,96,1536]{3,2,1,0:T(8,128)(2,1)} %param.8) | copy-start | bytes 2654212
  33.6 4.5 %collective-permute-start.11 = (bf16[3,96,1536]{2,1,0:T(8,128)(2,1)}, bf16[3,96,1536]{2,1,0:T(8,128)(2,1)S(1)}, u32[]{:S(2)}, u32[]{:S(2)}) collective-permute-start(bf16[3,96,1536]{2,1,0:T(8,128)(2,1)} %get-tuple-element.34.refs_6_), channel_id=1, source_target_pairs={{0,1},{1,0},{2,3},{3,2},{4,5},{5,4},{6,7},{7,6},{8,9},{9,8},{10,11... | collective-permute-start | bytes 2654216 | tf_op jit(solution)/shard_map/ppermute | solution.py:24
  35.8 12.2 %collective-permute-start.7 = (bf16[3,96,1536]{2,1,0:T(8,128)(2,1)S(1)}, bf16[3,96,1536]{2,1,0:T(8,128)(2,1)S(1)}, u32[]{:S(2)}, u32[]{:S(2)}) collective-permute-start(bf16[3,96,1536]{2,1,0:T(8,128)(2,1)S(1)} %get-tuple-element.30.refs_1_), channel_id=1, source_target_pairs={{0,4},{1,13},{4,8},{5,1},{8,12},{9,5},{12,0},{13,9},{2,6},{3,15},{... | collective-permute-start | bytes 2654216 | tf_op jit(solution)/shard_map/ppermute | solution.py:31
  37.6 12.2 %collective-permute-start.8 = (bf16[3,96,1536]{2,1,0:T(8,128)(2,1)S(1)}, bf16[3,96,1536]{2,1,0:T(8,128)(2,1)S(1)}, u32[]{:S(2)}, u32[]{:S(2)}) collective-permute-start(bf16[3,96,1536]{2,1,0:T(8,128)(2,1)S(1)} %get-tuple-element.31.refs_0_), channel_id=1, source_target_pairs={{0,2},{1,131},{2,128},{3,1},{128,130},{129,3},{130,0},{131,129},{4... | collective-permute-start | bytes 2654216 | tf_op jit(solution)/shard_map/ppermute | solution.py:38
  37.8 16.2 %collective-permute-start.14 = (bf16[3,96,1536]{2,1,0:T(8,128)(2,1)S(1)}, bf16[3,96,1536]{2,1,0:T(8,128)(2,1)S(1)}, u32[]{:S(2)}, u32[]{:S(2)}) collective-permute-start(bf16[3,96,1536]{2,1,0:T(8,128)(2,1)S(1)} %get-tuple-element.31.refs_0_), channel_id=1, source_target_pairs={{0,1},{1,0},{2,3},{3,2},{4,5},{5,4},{6,7},{7,6},{8,9},{9,8},{10,11... | collective-permute-start | bytes 2654216 | tf_op jit(solution)/shard_map/ppermute | solution.py:24
  50.1 3.8 %collective-permute-start.15 = (bf16[3,96,1536]{2,1,0:T(8,128)(2,1)S(1)}, bf16[3,96,1536]{2,1,0:T(8,128)(2,1)S(1)}, u32[]{:S(2)}, u32[]{:S(2)}) collective-permute-start(bf16[3,96,1536]{2,1,0:T(8,128)(2,1)S(1)} %get-tuple-element.37.refs_2_), channel_id=1, source_target_pairs={{0,1},{1,0},{2,3},{3,2},{4,5},{5,4},{6,7},{7,6},{8,9},{9,8},{10,11... | collective-permute-start | bytes 2654216 | tf_op jit(solution)/shard_map/ppermute | solution.py:24
  51.6 3.3 %collective-permute-start.16 = (bf16[3,96,1536]{2,1,0:T(8,128)(2,1)S(1)}, bf16[3,96,1536]{2,1,0:T(8,128)(2,1)S(1)}, u32[]{:S(2)}, u32[]{:S(2)}) collective-permute-start(bf16[3,96,1536]{2,1,0:T(8,128)(2,1)S(1)} %get-tuple-element.39.refs_4_), channel_id=1, source_target_pairs={{0,1},{1,0},{2,3},{3,2},{4,5},{5,4},{6,7},{7,6},{8,9},{9,8},{10,11... | collective-permute-start | bytes 2654216 | tf_op jit(solution)/shard_map/ppermute | solution.py:24
  51.8 10.1 %collective-permute-start.13 = (bf16[3,96,768]{2,1,0:T(8,128)(2,1)S(1)}, bf16[3,96,768]{2,1,0:T(8,128)(2,1)S(1)}, u32[]{:S(2)}, u32[]{:S(2)}) collective-permute-start(bf16[3,96,768]{2,1,0:T(8,128)(2,1)S(1)} %slice.23), channel_id=1, source_target_pairs={{0,2},{1,131},{2,128},{3,1},{128,130},{129,3},{130,0},{131,129},{4... | collective-permute-start | bytes 1327112 | tf_op jit(solution)/shard_map/ppermute | solution.py:38
  51.9 10.0 %collective-permute-start.12 = (bf16[3,96,768]{2,1,0:T(8,128)(2,1)S(1)}, bf16[3,96,768]{2,1,0:T(8,128)(2,1)S(1)}, u32[]{:S(2)}, u32[]{:S(2)}) collective-permute-start(bf16[3,96,768]{2,1,0:T(8,128)(2,1)S(1)} %get-tuple-element.36), channel_id=1, source_target_pairs={{0,4},{1,13},{4,8},{5,1},{8,12},{9,5},{12,0},{13,9},{2,6},{3,15},{... | collective-permute-start | bytes 1327112 | tf_op jit(solution)/shard_map/ppermute | solution.py:31
  55.0 9.6 %copy-start = (bf16[1536,1024]{1,0:T(8,128)(2,1)S(1)}, bf16[1536,1024]{1,0:T(8,128)(2,1)}, u32[]{:S(2)}) copy-start(bf16[1536,1024]{1,0:T(8,128)(2,1)} %refs_6_.3) | copy-start | bytes 9437188
  55.0 9.6 %copy-start.1 = (f32[1,1536]{1,0:T(1,128)S(1)}, f32[1,1536]{1,0:T(1,128)}, u32[]{:S(2)}) copy-start(f32[1,1536]{1,0:T(1,128)} %refs_5_.3) | copy-start | bytes 18436
  55.0 9.6 %copy-start.2 = (f32[1024]{0:T(1024)S(1)}, f32[1024]{0:T(1024)}, u32[]{:S(2)}) copy-start(f32[1024]{0:T(1024)} %param.11) | copy-start | bytes 12292
  62.0 1.9 %collective-permute-start.17 = (bf16[3,96,768]{2,1,0:T(8,128)(2,1)S(1)}, bf16[3,96,768]{2,1,0:T(8,128)(2,1)S(1)}, u32[]{:S(2)}, u32[]{:S(2)}) collective-permute-start(bf16[3,96,768]{2,1,0:T(8,128)(2,1)S(1)} %get-tuple-element.42.refs_0_), channel_id=1, source_target_pairs={{0,1},{1,0},{2,3},{3,2},{4,5},{5,4},{6,7},{7,6},{8,9},{9,8},{10,11... | collective-permute-start | bytes 1327112 | tf_op jit(solution)/shard_map/ppermute | solution.py:24
  62.5 2.1 %collective-permute-start.18 = (bf16[3,96,768]{2,1,0:T(8,128)(2,1)S(1)}, bf16[3,96,768]{2,1,0:T(8,128)(2,1)S(1)}, u32[]{:S(2)}, u32[]{:S(2)}) collective-permute-start(bf16[3,96,768]{2,1,0:T(8,128)(2,1)S(1)} %get-tuple-element.43.refs_2_), channel_id=1, source_target_pairs={{0,1},{1,0},{2,3},{3,2},{4,5},{5,4},{6,7},{7,6},{8,9},{9,8},{10,11... | collective-permute-start | bytes 1327112 | tf_op jit(solution)/shard_map/ppermute | solution.py:24
  68.4 22.0 %collective-permute-start.19 = (bf16[384,1024]{1,0:T(8,128)(2,1)S(1)}, bf16[384,1024]{1,0:T(8,128)(2,1)S(1)}, u32[]{:S(2)}, u32[]{:S(2)}) collective-permute-start(bf16[384,1024]{1,0:T(8,128)(2,1)S(1)} %finish.3), channel_id=1, source_target_pairs={{0,15},{1,14},{2,13},{3,12},{4,11},{5,10},{6,9},{7,8},{8,7},{9,6},... | collective-permute-start | bytes 2359304 | tf_op jit(solution)/shard_map/ppermute | solution.py:281

commit v4 on v3

--- a/solution.py
+++ b/solution.py
@@ -14,7 +14,7 @@
 VMEM_LIMIT = 24 * 1024 * 1024
 EDGE = 16
 TILE = 512
-PARTS = (8, 6, 2)
+PARTS = (8, 4, 4)
 ROWS = 128
 TOKEN = jax.ShapeDtypeStruct((8, 128), jnp.float32)
 INV_SQRT2 = 0.7071067811865476
@@ -173,21 +173,16 @@
     )(*operands)
 
 
-def finish_kernel(strand, groups, x_ref, *refs):
-    count = sum(groups)
+def finish_kernel(strand, count, x_ref, *refs):
     sources, refs = refs[:count], refs[count:]
     prev_ref, bias_ref, head_ref, head_bias_ref, out_ref, hidden_ref = refs
     rows = out_ref.shape[0]
-    start = 0
-    for count in groups:
-        blocks, sources = sources[:count], sources[count:]
-        width = blocks[0].shape[2]
-        here = pl.ds(start, width)
-        acc = convolve(x_ref[strand], strand == 1, blocks, pl.ds(0, width))
+    for start in range(0, hidden_ref.shape[1], TILE):
+        here = pl.ds(start, TILE)
+        acc = convolve(x_ref[strand], strand == 1, sources, here)
         acc = acc + prev_ref[strand, :, here] + bias_ref[:, here]
         hidden = 0.5 * acc * (1.0 + lax.erf(acc * INV_SQRT2))
         hidden_ref[:, here] = hidden.astype(jnp.bfloat16)
-        start += width
     for row in range(0, rows, ROWS):
         logits = jnp.dot(
             hidden_ref[pl.ds(row, ROWS), :], head_ref[...], preferred_element_type=jnp.float32
@@ -197,13 +192,12 @@
         out_ref[pl.ds(row, ROWS), :] = tracks.astype(jnp.bfloat16)
 
 
-def finish(strand, x, groups, prev, bias, head, head_bias):
+def finish(strand, x, sources, prev, bias, head, head_bias):
     rows, depth = x.shape[1] - EDGE, x.shape[2]
     channels, tracks = head.shape
-    sources = [value for group in groups for value in group]
-    inside = pl.BlockSpec(memory_space=pltpu.VMEM)
-    return pl.pallas_call(
-        functools.partial(finish_kernel, strand, tuple(len(group) for group in groups)),
+    inside = pl.BlockSpec(memory_space=pltpu.VMEM)
+    return pl.pallas_call(
+        functools.partial(finish_kernel, strand, len(sources)),
         out_shape=jax.ShapeDtypeStruct((rows, tracks), jnp.bfloat16),
         in_specs=[inside] * (len(sources) + 5),
         out_specs=inside,
@@ -234,8 +228,8 @@
             seq(x, y, core), seq(x, y, other), seq(x, over, core), seq(x, over, other),
             seq(back, y, core), seq(fore, y, other), seq(back, over, core), seq(fore, over, other),
             seq(far, y, core), seq(far, y, other), seq(back, y, other), seq(fore, y, core),
+            seq(back, over, other), seq(fore, over, core),
             seq(far, over, core), seq(far, over, other),
-            seq(back, over, other), seq(fore, over, core),
         ]
     ).astype(jnp.int32)
 
@@ -246,36 +240,28 @@
     down = [(b, a) for a, b in up]
     low = lax.ppermute(jnp.stack([forward_embed[-1], reverse_embed[-1]]), SEQ, up)
     high = lax.ppermute(jnp.stack([forward_embed[0], reverse_embed[0]]), SEQ, down)
-    near, across, low, high = fence(None, near, across, low, high)
+    near, across, sibling, low, high = fence(None, near, across, sibling, low, high)
 
     distant = x_shift(near)
     near_over = y_shift(near)
+    second = x_shift(sibling)
     across_b = core_swap(across)
     near_b = core_swap(near)
     x_1, x_2, x_3, token = prepare(place, forward_embed, reverse_embed, low, high)
-    distant, near_over, sibling = fence(token, distant, near_over, sibling)
-
-    second = x_shift(sibling)
+    distant, second, across_b = fence(token, distant, second, across_b)
+
+    second_over = x_shift(across_b)
     distant_over = y_shift(distant)
+    distant_b = core_swap(distant)
+    second_b = core_swap(second)
     near_over_b = core_swap(near_over)
-    distant_b = core_swap(distant)
-    half = own.shape[2] // 2
-    across_half = across_b[:, :, :half]
-    acc, token = partial_sum(
+    acc, _ = partial_sum(
         x_1, [own, sibling, across, across_b, near, near_b, near_over, near_over_b], None
     )
-    second, distant_over, across_half = fence(token, second, distant_over, across_half)
-
-    over_low = x_shift(across_half)
-    over_high = y_shift(second[:, :, half:])
-    second_b = core_swap(second)
-    distant_over_b = core_swap(distant_over)
-    acc, token = partial_sum(
-        x_2, [distant, distant_b, second, second_b, distant_over, distant_over_b], acc
-    )
-    over_low, over_high = fence(token, over_low, over_high)
-
-    last = [[over_low, core_swap(over_low)], [over_high, core_swap(over_high)]]
+    acc, token = partial_sum(x_2, [distant, distant_b, second, second_b], acc)
+    second_over, distant_over = fence(token, second_over, distant_over)
+
+    last = [second_over, core_swap(second_over), distant_over, core_swap(distant_over)]
     reverse_tracks = finish(1, x_3, last, acc, conv_bias, head_weight, head_bias)
     forward_tracks = finish(0, x_3, last, acc, conv_bias, head_weight, head_bias)
     mirrored = lax.ppermute(reverse_tracks, SEQ, [(i, ends - 1 - i) for i in range(ends)])

time: 91.9 us -> 93.9 us (1.022)
  Pallas kernels: 31.3 us -> 32.7 us
  starting transfers between devices: 24.7 us -> 25.8 us
    ppermute x4 -> x3, waiting for transfers between devices: 3.93 us -> 8.14 us  [y_shift(): return lax.ppermute(value, ('y_hi', 'y_lo', 'core'), route)]
    ppermute x1, waiting for transfers between devices: 16.6 us -> 13.3 us  [per_device(): lax.ppermute(reverse_tracks, SEQ, [(i, ends - 1 - i) for i in range(ends)])]
    ppermute x4 -> x3, starting transfers between devices: 5.91 us -> 2.75 us  [y_shift(): return lax.ppermute(value, ('y_hi', 'y_lo', 'core'), route)]
    ppermute x9 -> x8, starting transfers between devices: 5.06 us -> 7.29 us  [core_swap(): return lax.ppermute(value, 'core', [(0, 1), (1, 0)])]
    ppermute x1, starting transfers between devices: 1.6 us -> 3.6 us  [per_device(): lax.ppermute(reverse_tracks, SEQ, [(i, ends - 1 - i) for i in range(ends)])]
    ppermute x4, waiting for transfers between devices: 2.82 us -> 1.22 us  [x_shift(): return lax.ppermute(value, ('x', 'core'), route)]
    pallas_call x2, Pallas kernels: 7.6 us -> 9.2 us  [finish(): pl.pallas_call(functools.partial(finish_kernel, strand, len(sources)), ou...]
    pallas_call x4 -> x3, Pallas kernels: 2.81 us -> 3.25 us  [fence(): pl.pallas_call(functools.partial(fence_kernel, len(values)), out_shape=[j...]
  transfers between devices with their start and end apart: 20 -> 18, of which waited for: 9 -> 7; matrix products, arithmetic and copies ran while one was open for 2% -> 2% of each run, Pallas kernels for 30% -> 27%
where the time goes in v4:
time: 93.9 us; the launch traced here: 93.6 us
  Pallas kernels  32.7 us (35%)
  waiting for transfers between devices  28.9 us (31%)
  starting transfers between devices  25.8 us (27%)
  local copies, waits for them, and re-layouts  4.73 us (5%)
  other arithmetic  1.22 us (1%)
    pallas_call x2, Pallas kernels, partial_sum(): pl.pallas_call(functools.partial(partial_kernel, len(sources), prev is No...  13.6 us
    ppermute x1, waiting for transfers between devices, per_device(): lax.ppermute(reverse_tracks, SEQ, [(i, ends - 1 - i) for i in range(ends)])  13.3 us
    pallas_call x2, Pallas kernels, finish(): pl.pallas_call(functools.partial(finish_kernel, strand, len(sources)), ou...  9.2 us
    ppermute x3, waiting for transfers between devices, y_shift(): return lax.ppermute(value, ('y_hi', 'y_lo', 'core'), route)  8.14 us
    ppermute x4, starting transfers between devices, x_shift(): return lax.ppermute(value, ('x', 'core'), route)  7.81 us
    ppermute x8, starting transfers between devices, core_swap(): return lax.ppermute(value, 'core', [(0, 1), (1, 0)])  7.29 us
    pallas_call x1, Pallas kernels, prepare(): pl.pallas_call(prepare_kernel, out_shape=[jax.ShapeDtypeStruct((2, rows +...  6.71 us
    ppermute x1, starting transfers between devices, per_device(): lax.ppermute(reverse_tracks, SEQ, [(i, ends - 1 - i) for i in range(ends)])  3.6 us
  transfers between devices with their start and end apart: 18, of which 7 were waited for; matrix products, arithmetic and copies ran while one was open for 2% of the time, Pallas kernels for 27%

profile of v4, /device:TPU:1, one launch (start us, length us, event | category | flops | bytes accessed | tf_op | source)
XLA Modules:
  0.0 93.6 jit_solution(1093608079933977339)
XLA Ops:
  0.0 3.2 %collective-permute-start.2 = (bf16[3,96,1536]{2,1,0:T(8,128)(2,1)}, bf16[3,96,1536]{2,1,0:T(8,128)(2,1)S(1)}, u32[]{:S(2)}, u32[]{:S(2)}) collective-permute-start(bf16[3,96,1536]{2,1,0:T(8,128)(2,1)} %bitcast.20), channel_id=1, source_target_pairs={{0,1},{1,0},{2,3},{3,2},{4,5},{5,4},{6,7},{7,6},{8,9},{9,8},{10,11... | collective-permute-start | bytes 2654216 | tf_op jit(solution)/shard_map/ppermute | solution.py:24
  3.2 1.0 %collective-permute-start.1 = (bf16[3,96,1536]{2,1,0:T(8,128)(2,1)}, bf16[3,96,1536]{2,1,0:T(8,128)(2,1)}, u32[]{:S(2)}, u32[]{:S(2)}) collective-permute-start(bf16[3,96,1536]{2,1,0:T(8,128)(2,1)} %bitcast.21), channel_id=1, source_target_pairs={{0,2},{1,131},{2,128},{3,1},{128,130},{129,3},{130,0},{131,129},{4... | collective-permute-start | bytes 2654216 | tf_op jit(solution)/shard_map/ppermute | solution.py:38
  4.2 2.5 %collective-permute-start = (bf16[3,96,1536]{2,1,0:T(8,128)(2,1)}, bf16[3,96,1536]{2,1,0:T(8,128)(2,1)}, u32[]{:S(2)}, u32[]{:S(2)}) collective-permute-start(bf16[3,96,1536]{2,1,0:T(8,128)(2,1)} %bitcast.22), channel_id=1, source_target_pairs={{0,4},{1,13},{4,8},{5,1},{8,12},{9,5},{12,0},{13,9},{2,6},{3,15},{... | collective-permute-start | bytes 2654216 | tf_op jit(solution)/shard_map/ppermute | solution.py:31
  6.7 0.8 fusion
  7.6 1.9 %collective-permute-start.3 = (bf16[2,1536]{1,0:T(2,128)(2,1)S(1)}, bf16[2,1536]{1,0:T(2,128)(2,1)S(1)}, u32[]{:S(2)}, u32[]{:S(2)}) collective-permute-start(bf16[2,1536]{1,0:T(2,128)(2,1)S(1)} %pad_maximum_fusion), channel_id=1, source_target_pairs={{0,1},{1,2},{2,3},{3,4},{4,5},{5,6},{6,7},{7,8},{8,9},{9,10},{10,1... | collective-permute-start | bytes 18440 | tf_op jit(solution)/shard_map/ppermute | solution.py:241
  9.5 2.4 %collective-permute-start.4 = (bf16[2,1536]{1,0:T(2,128)(2,1)S(1)}, bf16[2,1536]{1,0:T(2,128)(2,1)S(1)}, u32[]{:S(2)}, u32[]{:S(2)}) collective-permute-start(bf16[2,1536]{1,0:T(2,128)(2,1)S(1)} %pad_maximum_fusion.1), channel_id=1, source_target_pairs={{1,0},{2,1},{3,2},{4,3},{5,4},{6,5},{7,6},{8,7},{9,8},{10,9},{11,1... | collective-permute-start | bytes 18440 | tf_op jit(solution)/shard_map/ppermute | solution.py:242
  11.9 0.0 collective-permute-done.3.refs_3_
  11.9 3.1 %collective-permute-done.4.refs_4_ = bf16[2,1536]{1,0:T(2,128)(2,1)S(1)} collective-permute-done((bf16[2,1536]{1,0:T(2,128)(2,1)S(1)}, bf16[2,1536]{1,0:T(2,128)(2,1)S(1)}, u32[]{:S(2)}, u32[]{:S(2)}) %collective-permute-start.4) | collective-permute-done | bytes 6176 | tf_op jit(solution)/shard_map/ppermute | solution.py:242
  15.0 0.8 collective-permute-done.1.refs_1_
  15.8 1.2 %collective-permute-done.refs_0_ = bf16[3,96,1536]{2,1,0:T(8,128)(2,1)} collective-permute-done((bf16[3,96,1536]{2,1,0:T(8,128)(2,1)}, bf16[3,96,1536]{2,1,0:T(8,128)(2,1)}, u32[]{:S(2)}, u32[]{:S(2)}) %collective-permute-start) | collective-permute-done | bytes 884768 | tf_op jit(solution)/shard_map/ppermute | solution.py:31
  17.0 2.7 %fence.3 = (bf16[3,96,1536]{2,1,0:T(8,128)(2,1)}, bf16[3,96,1536]{2,1,0:T(8,128)(2,1)}, bf16[3,96,1536]{2,1,0:T(8,128)(2,1)S(1)}, bf16[2,1536]{1,0:T(2,128)(2,1)S(1)}, bf16[2,1536]{1,0:T(2,128)(2,1)S(1)}) custom-call(bf16[3,96,1536]{2,1,0:T(8,128)(2,1)} %collective-permute-done.refs_0_, ...), custom_call_target="tpu_custom_call", output_to_operand_aliasing={{0}: (0, {}), {1}: (1, {}), {2}: (2, {}), {3}: (3, {}), {4}... | custom-call | tf_op jit(solution)/shard_map/fence/pallas_call | solution.py:49
  19.7 0.9 %collective-permute-start.13 = (bf16[3,96,1536]{2,1,0:T(8,128)(2,1)}, bf16[3,96,1536]{2,1,0:T(8,128)(2,1)}, u32[]{:S(2)}, u32[]{:S(2)}) collective-permute-start(bf16[3,96,1536]{2,1,0:T(8,128)(2,1)} %get-tuple-element.25.refs_4_), channel_id=1, source_target_pairs={{0,2},{1,131},{2,128},{3,1},{128,130},{129,3},{130,0},{131,129},{4... | collective-permute-start | bytes 2654216 | tf_op jit(solution)/shard_map/ppermute | solution.py:38
  20.7 2.6 %collective-permute-start.6 = (bf16[3,96,1536]{2,1,0:T(8,128)(2,1)S(1)}, bf16[3,96,1536]{2,1,0:T(8,128)(2,1)S(1)}, u32[]{:S(2)}, u32[]{:S(2)}) collective-permute-start(bf16[3,96,1536]{2,1,0:T(8,128)(2,1)S(1)} %get-tuple-element.26.refs_1_), channel_id=1, source_target_pairs={{0,4},{1,13},{4,8},{5,1},{8,12},{9,5},{12,0},{13,9},{2,6},{3,15},{... | collective-permute-start | bytes 2654216 | tf_op jit(solution)/shard_map/ppermute | solution.py:31
  23.3 0.0 collective-permute-start.7
  23.3 1.6 %collective-permute-start.5 = (bf16[3,96,1536]{2,1,0:T(8,128)(2,1)}, bf16[3,96,1536]{2,1,0:T(8,128)(2,1)S(1)}, u32[]{:S(2)}, u32[]{:S(2)}) collective-permute-start(bf16[3,96,1536]{2,1,0:T(8,128)(2,1)} %get-tuple-element.25.refs_4_), channel_id=1, source_target_pairs={{0,4},{1,13},{4,8},{5,1},{8,12},{9,5},{12,0},{13,9},{2,6},{3,15},{... | collective-permute-start | bytes 2654216 | tf_op jit(solution)/shard_map/ppermute | solution.py:31
  24.9 7.3 %collective-permute-done.13.refs_6_ = bf16[3,96,1536]{2,1,0:T(8,128)(2,1)} collective-permute-done((bf16[3,96,1536]{2,1,0:T(8,128)(2,1)}, bf16[3,96,1536]{2,1,0:T(8,128)(2,1)}, u32[]{:S(2)}, u32[]{:S(2)}) %collective-permute-start.13) | collective-permute-done | bytes 884768 | tf_op jit(solution)/shard_map/ppermute | solution.py:38
  32.2 2.9 %collective-permute-start.14 = (bf16[3,96,1536]{2,1,0:T(8,128)(2,1)}, bf16[3,96,1536]{2,1,0:T(8,128)(2,1)}, u32[]{:S(2)}, u32[]{:S(2)}) collective-permute-start(bf16[3,96,1536]{2,1,0:T(8,128)(2,1)} %collective-permute-done.13.refs_6_), channel_id=1, source_target_pairs={{0,1},{1,0},{2,3},{3,2},{4,5},{5,4},{6,7},{7,6},{8,9},{9,8},{10,11... | collective-permute-start | bytes 2654216 | tf_op jit(solution)/shard_map/ppermute | solution.py:24
  35.1 0.7 stack.73.place_ref
  35.8 0.7 copy-done.3
  36.5 1.3 %copy-done.4 = bf16[384,1536]{1,0:T(8,128)(2,1)S(1)} copy-done((bf16[384,1536]{1,0:T(8,128)(2,1)S(1)}, bf16[384,1536]{1,0:T(8,128)(2,1)}, u32[]{:S(2)}) %copy-start.4) | copy-done | bytes 1179672
  37.7 1.3 %copy-done.5 = bf16[384,1536]{1,0:T(8,128)(2,1)S(1)} copy-done((bf16[384,1536]{1,0:T(8,128)(2,1)S(1)}, bf16[384,1536]{1,0:T(8,128)(2,1)}, u32[]{:S(2)}) %copy-start.5) | copy-done | bytes 1179672
  39.0 6.7 %prepare.1 = (bf16[2,400,768]{2,1,0:T(8,128)(2,1)S(1)}, bf16[2,400,384]{2,1,0:T(8,128)(2,1)S(1)}, bf16[2,400,384]{2,1,0:T(8,128)(2,1)S(1)}, f32[8,128]{1,0:T(8,128)S(1)}) custom-call(s32[16]{0:T(128)S(1)} %copy-done.3, bf16[384,1536]{1,0:T(8,128)(2,1)S(1)} %copy-done.4, bf16[384,1536]{1,0:T(8,128)(2,1)S(1)} %copy-done.5, ...), custom_call_target="tpu_custom_call" | custom-call | flops 3623878656 | bytes 4718592 | tf_op jit(solution)/shard_map/prepare/pallas_call | solution.py:104
  45.7 0.0 copy-start.6
  45.7 0.0 collective-permute-done.5.refs_0_
  45.8 0.3 fence.4
  46.1 0.1 collective-permute-start.11
  46.2 0.5 collective-permute-start.10
  46.7 1.1 %collective-permute-start.8 = (bf16[3,96,1536]{2,1,0:T(8,128)(2,1)S(1)}, bf16[3,96,1536]{2,1,0:T(8,128)(2,1)S(1)}, u32[]{:S(2)}, u32[]{:S(2)}) collective-permute-start(bf16[3,96,1536]{2,1,0:T(8,128)(2,1)S(1)} %get-tuple-element.29.refs_3_), channel_id=1, source_target_pairs={{0,4},{1,13},{4,8},{5,1},{8,12},{9,5},{12,0},{13,9},{2,6},{3,15},{... | collective-permute-start | bytes 2654216 | tf_op jit(solution)/shard_map/ppermute | solution.py:31
  47.8 0.0 collective-permute-done.12.refs_5_
  47.8 0.8 collective-permute-start.9
  48.6 0.0 collective-permute-done.14.refs_7_
  48.6 8.6 %partial_sum.2 = (f32[2,384,1536]{2,1,0:T(8,128)S(1)}, f32[8,128]{1,0:T(8,128)}) custom-call(bf16[2,400,768]{2,1,0:T(8,128)(2,1)S(1)} %get-tuple-element.33.x_ref, bf16[3,96,1536]{2,1,0:T(8,128)(2,1)S(1)} %bitcast.23, bf16[3,96,1536]{2,1,0:T(8,128)(2,1)S(1)} %get-tuple-element.26.refs_1_, bf16[3,96,1536]{2,1,0:T(8,128)(2,1)} %get-tuple-element.27.refs_2_, ...), custom_call_target="tpu_custom_call" | custom-call | flops 5435817984 | bytes 7077888 | tf_op jit(solution)/shard_map/partial_sum/pallas_call | solution.py:160
  57.3 0.0 collective-permute-done.11.refs_3_
  57.3 0.0 collective-permute-done.10.refs_1_
  57.3 4.9 %partial_sum.3 = (f32[2,384,1536]{2,1,0:T(8,128)S(1)}, f32[8,128]{1,0:T(8,128)S(1)}) custom-call(bf16[2,400,384]{2,1,0:T(8,128)(2,1)S(1)} %get-tuple-element.31.x_ref, bf16[3,96,1536]{2,1,0:T(8,128)(2,1)S(1)} %get-tuple-element.30.refs_0_, bf16[3,96,1536]{2,1,0:T(8,128)(2,1)S(1)} %collective-permute-done.10.refs_1_, ...), custom_call_target="tpu_custom_call", output_to_operand_aliasing={{0}: (5, {})} | custom-call | flops 2717908992 | bytes 3538944 | tf_op jit(solution)/shard_map/partial_sum/pallas_call | solution.py:160
  62.2 0.0 copy-start.1
  62.2 0.0 copy-start.2
  62.2 0.0 collective-permute-done.8.refs_0_
  62.3 0.2 fence.5
  62.5 0.1 collective-permute-start.15
  62.6 0.5 collective-permute-start.16
  63.1 1.9 %collective-permute-done.15.refs_1_ = bf16[3,96,1536]{2,1,0:T(8,128)(2,1)S(1)} collective-permute-done((bf16[3,96,1536]{2,1,0:T(8,128)(2,1)S(1)}, bf16[3,96,1536]{2,1,0:T(8,128)(2,1)S(1)}, u32[]{:S(2)}, u32[]{:S(2)}) %collective-permute-start.15) | collective-permute-done | bytes 884768 | tf_op jit(solution)/shard_map/ppermute | solution.py:24
  65.0 1.3 %collective-permute-done.16.refs_3_ = bf16[3,96,1536]{2,1,0:T(8,128)(2,1)S(1)} collective-permute-done((bf16[3,96,1536]{2,1,0:T(8,128)(2,1)S(1)}, bf16[3,96,1536]{2,1,0:T(8,128)(2,1)S(1)}, u32[]{:S(2)}, u32[]{:S(2)}) %collective-permute-start.16) | collective-permute-done | bytes 884768 | tf_op jit(solution)/shard_map/ppermute | solution.py:24
  66.3 4.6 %finish.3 = bf16[384,1024]{1,0:T(8,128)(2,1)S(1)} custom-call(bf16[2,400,384]{2,1,0:T(8,128)(2,1)S(1)} %get-tuple-element.24.x_ref, bf16[3,96,1536]{2,1,0:T(8,128)(2,1)S(1)} %get-tuple-element.36.refs_0_, bf16[3,96,1536]{2,1,0:T(8,128)(2,1)S(1)} %collective-permute-done.15.refs_1_, bf16[3,96,1536]{2,1,0:T(8,128)(2,1)S(1)} %get-tuple-element.37.refs_2_, ...), custom_call_target="tpu_custom_call" | custom-call | flops 2566914048 | bytes 6684672 | tf_op jit(solution)/shard_map/finish/pallas_call | solution.py:199
  70.9 3.6 %collective-permute-start.17 = (bf16[384,1024]{1,0:T(8,128)(2,1)S(1)}, bf16[384,1024]{1,0:T(8,128)(2,1)S(1)}, u32[]{:S(2)}, u32[]{:S(2)}) collective-permute-start(bf16[384,1024]{1,0:T(8,128)(2,1)S(1)} %finish.3), channel_id=1, source_target_pairs={{0,15},{1,14},{2,13},{3,12},{4,11},{5,10},{6,9},{7,8},{8,7},{9,6},... | collective-permute-start | bytes 2359304 | tf_op jit(solution)/shard_map/ppermute | solution.py:267
  74.5 4.6 %finish.2 = bf16[384,1024]{1,0:T(8,128)(2,1)S(1)} custom-call(bf16[2,400,384]{2,1,0:T(8,128)(2,1)S(1)} %get-tuple-element.24.x_ref, bf16[3,96,1536]{2,1,0:T(8,128)(2,1)S(1)} %get-tuple-element.36.refs_0_, bf16[3,96,1536]{2,1,0:T(8,128)(2,1)S(1)} %collective-permute-done.15.refs_1_, bf16[3,96,1536]{2,1,0:T(8,128)(2,1)S(1)} %get-tuple-element.37.refs_2_, ...), custom_call_target="tpu_custom_call" | custom-call | flops 2566914048 | bytes 6684672 | tf_op jit(solution)/shard_map/finish/pallas_call | solution.py:199
  79.1 13.3 %collective-permute-done.17 = bf16[384,1024]{1,0:T(8,128)(2,1)S(1)} collective-permute-done((bf16[384,1024]{1,0:T(8,128)(2,1)S(1)}, bf16[384,1024]{1,0:T(8,128)(2,1)S(1)}, u32[]{:S(2)}, u32[]{:S(2)}) %collective-permute-start.17) | collective-permute-done | bytes 786464 | tf_op jit(solution)/shard_map/ppermute | solution.py:267
  92.4 1.2 %multiply_convert_fusion = bf16[384,1024]{1,0:T(8,128)(2,1)} fusion(bf16[384,1024]{1,0:T(8,128)(2,1)S(1)} %collective-permute-done.17, bf16[384,1024]{1,0:T(8,128)(2,1)S(1)} %finish.2), kind=kLoop, calls=%fused_computation | loop fusion | flops 1966080 | bytes 2359296 | tf_op jit(solution)/shard_map/convert_element_type | solution.py:269
  (15 shorter events, 0.1 us)
Async XLA Ops:
  0.0 15.0 %collective-permute-start.2 = (bf16[3,96,1536]{2,1,0:T(8,128)(2,1)}, bf16[3,96,1536]{2,1,0:T(8,128)(2,1)S(1)}, u32[]{:S(2)}, u32[]{:S(2)}) collective-permute-start(bf16[3,96,1536]{2,1,0:T(8,128)(2,1)} %bitcast.20), channel_id=1, source_target_pairs={{0,1},{1,0},{2,3},{3,2},{4,5},{5,4},{6,7},{7,6},{8,9},{9,8},{10,11... | collective-permute-start | bytes 2654216 | tf_op jit(solution)/shard_map/ppermute | solution.py:24
  3.2 12.6 %collective-permute-start.1 = (bf16[3,96,1536]{2,1,0:T(8,128)(2,1)}, bf16[3,96,1536]{2,1,0:T(8,128)(2,1)}, u32[]{:S(2)}, u32[]{:S(2)}) collective-permute-start(bf16[3,96,1536]{2,1,0:T(8,128)(2,1)} %bitcast.21), channel_id=1, source_target_pairs={{0,2},{1,131},{2,128},{3,1},{128,130},{129,3},{130,0},{131,129},{4... | collective-permute-start | bytes 2654216 | tf_op jit(solution)/shard_map/ppermute | solution.py:38
  4.2 12.8 %collective-permute-start = (bf16[3,96,1536]{2,1,0:T(8,128)(2,1)}, bf16[3,96,1536]{2,1,0:T(8,128)(2,1)}, u32[]{:S(2)}, u32[]{:S(2)}) collective-permute-start(bf16[3,96,1536]{2,1,0:T(8,128)(2,1)} %bitcast.22), channel_id=1, source_target_pairs={{0,4},{1,13},{4,8},{5,1},{8,12},{9,5},{12,0},{13,9},{2,6},{3,15},{... | collective-permute-start | bytes 2654216 | tf_op jit(solution)/shard_map/ppermute | solution.py:31
  7.6 4.4 %collective-permute-start.3 = (bf16[2,1536]{1,0:T(2,128)(2,1)S(1)}, bf16[2,1536]{1,0:T(2,128)(2,1)S(1)}, u32[]{:S(2)}, u32[]{:S(2)}) collective-permute-start(bf16[2,1536]{1,0:T(2,128)(2,1)S(1)} %pad_maximum_fusion), channel_id=1, source_target_pairs={{0,1},{1,2},{2,3},{3,4},{4,5},{5,6},{6,7},{7,8},{8,9},{9,10},{10,1... | collective-permute-start | bytes 18440 | tf_op jit(solution)/shard_map/ppermute | solution.py:241
  9.5 5.5 %collective-permute-start.4 = (bf16[2,1536]{1,0:T(2,128)(2,1)S(1)}, bf16[2,1536]{1,0:T(2,128)(2,1)S(1)}, u32[]{:S(2)}, u32[]{:S(2)}) collective-permute-start(bf16[2,1536]{1,0:T(2,128)(2,1)S(1)} %pad_maximum_fusion.1), channel_id=1, source_target_pairs={{1,0},{2,1},{3,2},{4,3},{5,4},{6,5},{7,6},{8,7},{9,8},{10,9},{11,1... | collective-permute-start | bytes 18440 | tf_op jit(solution)/shard_map/ppermute | solution.py:242
  19.7 12.5 %collective-permute-start.13 = (bf16[3,96,1536]{2,1,0:T(8,128)(2,1)}, bf16[3,96,1536]{2,1,0:T(8,128)(2,1)}, u32[]{:S(2)}, u32[]{:S(2)}) collective-permute-start(bf16[3,96,1536]{2,1,0:T(8,128)(2,1)} %get-tuple-element.25.refs_4_), channel_id=1, source_target_pairs={{0,2},{1,131},{2,128},{3,1},{128,130},{129,3},{130,0},{131,129},{4... | collective-permute-start | bytes 2654216 | tf_op jit(solution)/shard_map/ppermute | solution.py:38
  20.7 25.1 %collective-permute-start.6 = (bf16[3,96,1536]{2,1,0:T(8,128)(2,1)S(1)}, bf16[3,96,1536]{2,1,0:T(8,128)(2,1)S(1)}, u32[]{:S(2)}, u32[]{:S(2)}) collective-permute-start(bf16[3,96,1536]{2,1,0:T(8,128)(2,1)S(1)} %get-tuple-element.26.refs_1_), channel_id=1, source_target_pairs={{0,4},{1,13},{4,8},{5,1},{8,12},{9,5},{12,0},{13,9},{2,6},{3,15},{... | collective-permute-start | bytes 2654216 | tf_op jit(solution)/shard_map/ppermute | solution.py:31
  23.3 22.4 %collective-permute-start.7 = (bf16[3,96,1536]{2,1,0:T(8,128)(2,1)}, bf16[3,96,1536]{2,1,0:T(8,128)(2,1)S(1)}, u32[]{:S(2)}, u32[]{:S(2)}) collective-permute-start(bf16[3,96,1536]{2,1,0:T(8,128)(2,1)} %get-tuple-element.27.refs_2_), channel_id=1, source_target_pairs={{0,1},{1,0},{2,3},{3,2},{4,5},{5,4},{6,7},{7,6},{8,9},{9,8},{10,11... | collective-permute-start | bytes 2654216 | tf_op jit(solution)/shard_map/ppermute | solution.py:24
  23.3 22.4 %collective-permute-start.5 = (bf16[3,96,1536]{2,1,0:T(8,128)(2,1)}, bf16[3,96,1536]{2,1,0:T(8,128)(2,1)S(1)}, u32[]{:S(2)}, u32[]{:S(2)}) collective-permute-start(bf16[3,96,1536]{2,1,0:T(8,128)(2,1)} %get-tuple-element.25.refs_4_), channel_id=1, source_target_pairs={{0,4},{1,13},{4,8},{5,1},{8,12},{9,5},{12,0},{13,9},{2,6},{3,15},{... | collective-permute-start | bytes 2654216 | tf_op jit(solution)/shard_map/ppermute | solution.py:31
  24.9 22.9 %collective-permute-start.12 = (bf16[3,96,1536]{2,1,0:T(8,128)(2,1)}, bf16[3,96,1536]{2,1,0:T(8,128)(2,1)}, u32[]{:S(2)}, u32[]{:S(2)}) collective-permute-start(bf16[3,96,1536]{2,1,0:T(8,128)(2,1)} %get-tuple-element.25.refs_4_), channel_id=1, source_target_pairs={{0,1},{1,0},{2,3},{3,2},{4,5},{5,4},{6,7},{7,6},{8,9},{9,8},{10,11... | collective-permute-start | bytes 2654216 | tf_op jit(solution)/shard_map/ppermute | solution.py:24
  32.2 16.4 %collective-permute-start.14 = (bf16[3,96,1536]{2,1,0:T(8,128)(2,1)}, bf16[3,96,1536]{2,1,0:T(8,128)(2,1)}, u32[]{:S(2)}, u32[]{:S(2)}) collective-permute-start(bf16[3,96,1536]{2,1,0:T(8,128)(2,1)} %collective-permute-done.13.refs_6_), channel_id=1, source_target_pairs={{0,1},{1,0},{2,3},{3,2},{4,5},{5,4},{6,7},{7,6},{8,9},{9,8},{10,11... | collective-permute-start | bytes 2654216 | tf_op jit(solution)/shard_map/ppermute | solution.py:24
  35.8 0.7 copy-start.3
  36.4 1.3 %copy-start.4 = (bf16[384,1536]{1,0:T(8,128)(2,1)S(1)}, bf16[384,1536]{1,0:T(8,128)(2,1)}, u32[]{:S(2)}) copy-start(bf16[384,1536]{1,0:T(8,128)(2,1)} %forward_ref.1) | copy-start | bytes 3538948
  37.7 1.3 %copy-start.5 = (bf16[384,1536]{1,0:T(8,128)(2,1)S(1)}, bf16[384,1536]{1,0:T(8,128)(2,1)}, u32[]{:S(2)}) copy-start(bf16[384,1536]{1,0:T(8,128)(2,1)} %reverse_ref.1) | copy-start | bytes 3538948
  45.7 2.9 %copy-start.6 = (bf16[1,3,96,1536]{3,2,1,0:T(8,128)(2,1)S(1)}, bf16[1,3,96,1536]{3,2,1,0:T(8,128)(2,1)}, u32[]{:S(2)}) copy-start(bf16[1,3,96,1536]{3,2,1,0:T(8,128)(2,1)} %param.8) | copy-start | bytes 2654212
  46.1 11.2 %collective-permute-start.11 = (bf16[3,96,1536]{2,1,0:T(8,128)(2,1)S(1)}, bf16[3,96,1536]{2,1,0:T(8,128)(2,1)S(1)}, u32[]{:S(2)}, u32[]{:S(2)}) collective-permute-start(bf16[3,96,1536]{2,1,0:T(8,128)(2,1)S(1)} %get-tuple-element.32.refs_2_), channel_id=1, source_target_pairs={{0,1},{1,0},{2,3},{3,2},{4,5},{5,4},{6,7},{7,6},{8,9},{9,8},{10,11... | collective-permute-start | bytes 2654216 | tf_op jit(solution)/shard_map/ppermute | solution.py:24
  46.2 11.1 %collective-permute-start.10 = (bf16[3,96,1536]{2,1,0:T(8,128)(2,1)S(1)}, bf16[3,96,1536]{2,1,0:T(8,128)(2,1)S(1)}, u32[]{:S(2)}, u32[]{:S(2)}) collective-permute-start(bf16[3,96,1536]{2,1,0:T(8,128)(2,1)S(1)} %get-tuple-element.30.refs_0_), channel_id=1, source_target_pairs={{0,1},{1,0},{2,3},{3,2},{4,5},{5,4},{6,7},{7,6},{8,9},{9,8},{10,11... | collective-permute-start | bytes 2654216 | tf_op jit(solution)/shard_map/ppermute | solution.py:24
  46.7 15.6 %collective-permute-start.8 = (bf16[3,96,1536]{2,1,0:T(8,128)(2,1)S(1)}, bf16[3,96,1536]{2,1,0:T(8,128)(2,1)S(1)}, u32[]{:S(2)}, u32[]{:S(2)}) collective-permute-start(bf16[3,96,1536]{2,1,0:T(8,128)(2,1)S(1)} %get-tuple-element.29.refs_3_), channel_id=1, source_target_pairs={{0,4},{1,13},{4,8},{5,1},{8,12},{9,5},{12,0},{13,9},{2,6},{3,15},{... | collective-permute-start | bytes 2654216 | tf_op jit(solution)/shard_map/ppermute | solution.py:31
  47.8 14.5 %collective-permute-start.9 = (bf16[3,96,1536]{2,1,0:T(8,128)(2,1)S(1)}, bf16[3,96,1536]{2,1,0:T(8,128)(2,1)S(1)}, u32[]{:S(2)}, u32[]{:S(2)}) collective-permute-start(bf16[3,96,1536]{2,1,0:T(8,128)(2,1)S(1)} %get-tuple-element.30.refs_0_), channel_id=1, source_target_pairs={{0,2},{1,131},{2,128},{3,1},{128,130},{129,3},{130,0},{131,129},{4... | collective-permute-start | bytes 2654216 | tf_op jit(solution)/shard_map/ppermute | solution.py:38
  57.3 9.0 %copy-start = (bf16[1536,1024]{1,0:T(8,128)(2,1)S(1)}, bf16[1536,1024]{1,0:T(8,128)(2,1)}, u32[]{:S(2)}) copy-start(bf16[1536,1024]{1,0:T(8,128)(2,1)} %refs_6_.3) | copy-start | bytes 9437188
  62.2 4.1 %copy-start.1 = (f32[1,1536]{1,0:T(1,128)S(1)}, f32[1,1536]{1,0:T(1,128)}, u32[]{:S(2)}) copy-start(f32[1,1536]{1,0:T(1,128)} %refs_5_.3) | copy-start | bytes 18436
  62.2 4.0 %copy-start.2 = (f32[1024]{0:T(1024)S(1)}, f32[1024]{0:T(1024)}, u32[]{:S(2)}) copy-start(f32[1024]{0:T(1024)} %param.11) | copy-start | bytes 12292
  62.5 2.5 %collective-permute-start.15 = (bf16[3,96,1536]{2,1,0:T(8,128)(2,1)S(1)}, bf16[3,96,1536]{2,1,0:T(8,128)(2,1)S(1)}, u32[]{:S(2)}, u32[]{:S(2)}) collective-permute-start(bf16[3,96,1536]{2,1,0:T(8,128)(2,1)S(1)} %get-tuple-element.36.refs_0_), channel_id=1, source_target_pairs={{0,1},{1,0},{2,3},{3,2},{4,5},{5,4},{6,7},{7,6},{8,9},{9,8},{10,11... | collective-permute-start | bytes 2654216 | tf_op jit(solution)/shard_map/ppermute | solution.py:24
  62.6 3.7 %collective-permute-start.16 = (bf16[3,96,1536]{2,1,0:T(8,128)(2,1)S(1)}, bf16[3,96,1536]{2,1,0:T(8,128)(2,1)S(1)}, u32[]{:S(2)}, u32[]{:S(2)}) collective-permute-start(bf16[3,96,1536]{2,1,0:T(8,128)(2,1)S(1)} %get-tuple-element.37.refs_2_), channel_id=1, source_target_pairs={{0,1},{1,0},{2,3},{3,2},{4,5},{5,4},{6,7},{7,6},{8,9},{9,8},{10,11... | collective-permute-start | bytes 2654216 | tf_op jit(solution)/shard_map/ppermute | solution.py:24
  70.9 21.5 %collective-permute-start.17 = (bf16[384,1024]{1,0:T(8,128)(2,1)S(1)}, bf16[384,1024]{1,0:T(8,128)(2,1)S(1)}, u32[]{:S(2)}, u32[]{:S(2)}) collective-permute-start(bf16[384,1024]{1,0:T(8,128)(2,1)S(1)} %finish.3), channel_id=1, source_target_pairs={{0,15},{1,14},{2,13},{3,12},{4,11},{5,10},{6,9},{7,8},{8,7},{9,6},... | collective-permute-start | bytes 2359304 | tf_op jit(solution)/shard_map/ppermute | solution.py:267

commit v5 on v4

--- a/solution.py
+++ b/solution.py
@@ -226,8 +226,8 @@
     place = jnp.stack(
         [
             seq(x, y, core), seq(x, y, other), seq(x, over, core), seq(x, over, other),
-            seq(back, y, core), seq(fore, y, other), seq(back, over, core), seq(fore, over, other),
-            seq(far, y, core), seq(far, y, other), seq(back, y, other), seq(fore, y, core),
+            seq(back, y, core), seq(fore, y, other), seq(back, y, other), seq(fore, y, core),
+            seq(back, over, core), seq(fore, over, other), seq(far, y, core), seq(far, y, other),
             seq(back, over, other), seq(fore, over, core),
             seq(far, over, core), seq(far, over, other),
         ]
@@ -236,29 +236,29 @@
     near = x_shift(own)
     across = y_shift(own)
     sibling = core_swap(own)
+    second = x_shift(sibling)
     up = [(i, i + 1) for i in range(ends - 1)]
     down = [(b, a) for a, b in up]
     low = lax.ppermute(jnp.stack([forward_embed[-1], reverse_embed[-1]]), SEQ, up)
     high = lax.ppermute(jnp.stack([forward_embed[0], reverse_embed[0]]), SEQ, down)
-    near, across, sibling, low, high = fence(None, near, across, sibling, low, high)
+    x_1, x_2, x_3, token = prepare(place, forward_embed, reverse_embed, low, high)
+    near, across = fence(token, near, across)
 
     distant = x_shift(near)
     near_over = y_shift(near)
-    second = x_shift(sibling)
     across_b = core_swap(across)
     near_b = core_swap(near)
-    x_1, x_2, x_3, token = prepare(place, forward_embed, reverse_embed, low, high)
-    distant, second, across_b = fence(token, distant, second, across_b)
+    second_b = core_swap(second)
+    acc, token = partial_sum(
+        x_1, [own, sibling, across, across_b, near, near_b, second, second_b], None
+    )
+    distant, near_over, across_b = fence(token, distant, near_over, across_b)
 
     second_over = x_shift(across_b)
     distant_over = y_shift(distant)
+    near_over_b = core_swap(near_over)
     distant_b = core_swap(distant)
-    second_b = core_swap(second)
-    near_over_b = core_swap(near_over)
-    acc, _ = partial_sum(
-        x_1, [own, sibling, across, across_b, near, near_b, near_over, near_over_b], None
-    )
-    acc, token = partial_sum(x_2, [distant, distant_b, second, second_b], acc)
+    acc, token = partial_sum(x_2, [near_over, near_over_b, distant, distant_b], acc)
     second_over, distant_over = fence(token, second_over, distant_over)
 
     last = [second_over, core_swap(second_over), distant_over, core_swap(distant_over)]

time: 93.9 us -> 90.4 us (0.963)
  Pallas kernels: 32.7 us -> 27.8 us
  waiting for transfers between devices: 28.9 us -> 32.6 us
  starting transfers between devices: 25.8 us -> 23.7 us
  local copies, waits for them, and re-layouts: 4.73 us -> 3.47 us
  other arithmetic: 1.22 us -> 2.4 us
    ppermute x4, waiting for transfers between devices: 1.22 us -> 6.2 us  [x_shift(): return lax.ppermute(value, ('x', 'core'), route)]
    ppermute x3, waiting for transfers between devices: 8.14 us -> 3.52 us  [y_shift(): return lax.ppermute(value, ('y_hi', 'y_lo', 'core'), route)]
    ppermute x4, starting transfers between devices: 7.81 us -> 3.52 us  [x_shift(): return lax.ppermute(value, ('x', 'core'), route)]
    ppermute x3, starting transfers between devices: 2.75 us -> 5.99 us  [y_shift(): return lax.ppermute(value, ('y_hi', 'y_lo', 'core'), route)]
    pallas_call x2, Pallas kernels: 13.6 us -> 10.9 us  [partial_sum(): pl.pallas_call(functools.partial(partial_kernel, len(sources), prev is No...]
    pallas_call x3, Pallas kernels: 3.25 us -> 0.75 us  [fence(): pl.pallas_call(functools.partial(fence_kernel, len(values)), out_shape=[j...]
    ppermute x1, waiting for transfers between devices: 13.3 us -> 15 us  [per_device(): lax.ppermute(reverse_tracks, SEQ, [(i, ends - 1 - i) for i in range(ends)])]
    ppermute x8, waiting for transfers between devices: 3.2 us -> 4.92 us  [core_swap(): return lax.ppermute(value, 'core', [(0, 1), (1, 0)])]
  transfers between devices with their start and end apart: 18 -> 18, of which waited for: 7 -> 10; matrix products, arithmetic and copies ran while one was open for 2% -> 2% of each run, Pallas kernels for 27% -> 25%
where the time goes in v5:
time: 90.4 us; the launch traced here: 90.1 us
  waiting for transfers between devices  32.6 us (36%)
  Pallas kernels  27.8 us (31%)
  starting transfers between devices  23.7 us (26%)
  local copies, waits for them, and re-layouts  3.47 us (4%)
  other arithmetic  2.4 us (3%)
    ppermute x1, waiting for transfers between devices, per_device(): lax.ppermute(reverse_tracks, SEQ, [(i, ends - 1 - i) for i in range(ends)])  15 us
    pallas_call x2, Pallas kernels, partial_sum(): pl.pallas_call(functools.partial(partial_kernel, len(sources), prev is No...  10.9 us
    pallas_call x2, Pallas kernels, finish(): pl.pallas_call(functools.partial(finish_kernel, strand, len(sources)), ou...  9.21 us
    ppermute x8, starting transfers between devices, core_swap(): return lax.ppermute(value, 'core', [(0, 1), (1, 0)])  7.82 us
    pallas_call x1, Pallas kernels, prepare(): pl.pallas_call(prepare_kernel, out_shape=[jax.ShapeDtypeStruct((2, rows +...  6.87 us
    ppermute x4, waiting for transfers between devices, x_shift(): return lax.ppermute(value, ('x', 'core'), route)  6.2 us
    ppermute x3, starting transfers between devices, y_shift(): return lax.ppermute(value, ('y_hi', 'y_lo', 'core'), route)  5.99 us
    ppermute x8, waiting for transfers between devices, core_swap(): return lax.ppermute(value, 'core', [(0, 1), (1, 0)])  4.92 us
  transfers between devices with their start and end apart: 18, of which 10 were waited for; matrix products, arithmetic and copies ran while one was open for 2% of the time, Pallas kernels for 25%

profile of v5, /device:TPU:1, one launch (start us, length us, event | category | flops | bytes accessed | tf_op | source)
XLA Modules:
  0.0 90.1 jit_solution(12529932972286991134)
XLA Ops:
  0.0 3.2 %collective-permute-start.7 = (bf16[3,96,1536]{2,1,0:T(8,128)(2,1)}, bf16[3,96,1536]{2,1,0:T(8,128)(2,1)S(1)}, u32[]{:S(2)}, u32[]{:S(2)}) collective-permute-start(bf16[3,96,1536]{2,1,0:T(8,128)(2,1)} %bitcast.20), channel_id=1, source_target_pairs={{0,1},{1,0},{2,3},{3,2},{4,5},{5,4},{6,7},{7,6},{8,9},{9,8},{10,11... | collective-permute-start | bytes 2654216 | tf_op jit(solution)/shard_map/ppermute | solution.py:24
  3.2 1.0 %collective-permute-start.3 = (bf16[3,96,1536]{2,1,0:T(8,128)(2,1)}, bf16[3,96,1536]{2,1,0:T(8,128)(2,1)S(1)}, u32[]{:S(2)}, u32[]{:S(2)}) collective-permute-start(bf16[3,96,1536]{2,1,0:T(8,128)(2,1)} %bitcast.21), channel_id=1, source_target_pairs={{0,2},{1,131},{2,128},{3,1},{128,130},{129,3},{130,0},{131,129},{4... | collective-permute-start | bytes 2654216 | tf_op jit(solution)/shard_map/ppermute | solution.py:38
  4.2 2.5 %collective-permute-start.2 = (bf16[3,96,1536]{2,1,0:T(8,128)(2,1)}, bf16[3,96,1536]{2,1,0:T(8,128)(2,1)S(1)}, u32[]{:S(2)}, u32[]{:S(2)}) collective-permute-start(bf16[3,96,1536]{2,1,0:T(8,128)(2,1)} %bitcast.22), channel_id=1, source_target_pairs={{0,4},{1,13},{4,8},{5,1},{8,12},{9,5},{12,0},{13,9},{2,6},{3,15},{... | collective-permute-start | bytes 2654216 | tf_op jit(solution)/shard_map/ppermute | solution.py:31
  6.7 0.0 collective-permute-done.7.refs_1_
  6.7 0.5 collective-permute-start.9
  7.3 0.8 fusion
  8.1 0.6 pad_maximum_fusion
  8.7 1.9 %collective-permute-start = (bf16[2,1536]{1,0:T(2,128)(2,1)}, bf16[2,1536]{1,0:T(2,128)(2,1)S(1)}, u32[]{:S(2)}, u32[]{:S(2)}) collective-permute-start(bf16[2,1536]{1,0:T(2,128)(2,1)} %pad_maximum_fusion), channel_id=1, source_target_pairs={{0,1},{1,2},{2,3},{3,4},{4,5},{5,6},{6,7},{7,8},{8,9},{9,10},{10,1... | collective-permute-start | bytes 18440 | tf_op jit(solution)/shard_map/ppermute | solution.py:242
  10.6 0.6 pad_maximum_fusion.1
  11.2 2.4 %collective-permute-start.1 = (bf16[2,1536]{1,0:T(2,128)(2,1)}, bf16[2,1536]{1,0:T(2,128)(2,1)}, u32[]{:S(2)}, u32[]{:S(2)}) collective-permute-start(bf16[2,1536]{1,0:T(2,128)(2,1)} %pad_maximum_fusion.1), channel_id=1, source_target_pairs={{1,0},{2,1},{3,2},{4,3},{5,4},{6,5},{7,6},{8,7},{9,8},{10,9},{11,1... | collective-permute-start | bytes 18440 | tf_op jit(solution)/shard_map/ppermute | solution.py:243
  13.7 0.1 stack.73.place_ref
  13.8 2.9 %collective-permute-done.1.high_ref = bf16[2,1536]{1,0:T(2,128)(2,1)} collective-permute-done((bf16[2,1536]{1,0:T(2,128)(2,1)}, bf16[2,1536]{1,0:T(2,128)(2,1)}, u32[]{:S(2)}, u32[]{:S(2)}) %collective-permute-start.1) | collective-permute-done | bytes 6176 | tf_op jit(solution)/shard_map/ppermute | solution.py:243
  16.7 1.3 %copy-done.3 = bf16[384,1536]{1,0:T(8,128)(2,1)S(1)} copy-done((bf16[384,1536]{1,0:T(8,128)(2,1)S(1)}, bf16[384,1536]{1,0:T(8,128)(2,1)}, u32[]{:S(2)}) %copy-start.3) | copy-done | bytes 1179672
  17.9 1.3 %copy-done.4 = bf16[384,1536]{1,0:T(8,128)(2,1)S(1)} copy-done((bf16[384,1536]{1,0:T(8,128)(2,1)S(1)}, bf16[384,1536]{1,0:T(8,128)(2,1)}, u32[]{:S(2)}) %copy-start.4) | copy-done | bytes 1179672
  19.2 6.9 %prepare.1 = (bf16[2,400,768]{2,1,0:T(8,128)(2,1)S(1)}, bf16[2,400,384]{2,1,0:T(8,128)(2,1)S(1)}, bf16[2,400,384]{2,1,0:T(8,128)(2,1)S(1)}, f32[8,128]{1,0:T(8,128)S(1)}) custom-call(s32[16]{0:T(128)S(1)} %stack.73.place_ref, bf16[384,1536]{1,0:T(8,128)(2,1)S(1)} %copy-done.3, bf16[384,1536]{1,0:T(8,128)(2,1)S(1)} %copy-done.4, ...), custom_call_target="tpu_custom_call" | custom-call | flops 3623878656 | bytes 4718592 | tf_op jit(solution)/shard_map/prepare/pallas_call | solution.py:104
  26.1 0.0 copy-start.5
  26.1 0.0 collective-permute-done.3.refs_1_
  26.1 0.2 fence.3
  26.3 0.1 collective-permute-start.6
  26.4 0.5 collective-permute-start.8
  26.9 0.2 collective-permute-start.10
  27.2 3.2 %collective-permute-start.5 = (bf16[3,96,1536]{2,1,0:T(8,128)(2,1)S(1)}, bf16[3,96,1536]{2,1,0:T(8,128)(2,1)S(1)}, u32[]{:S(2)}, u32[]{:S(2)}) collective-permute-start(bf16[3,96,1536]{2,1,0:T(8,128)(2,1)S(1)} %get-tuple-element.22.refs_4_), channel_id=1, source_target_pairs={{0,2},{1,131},{2,128},{3,1},{128,130},{129,3},{130,0},{131,129},{4... | collective-permute-start | bytes 2654216 | tf_op jit(solution)/shard_map/ppermute | solution.py:38
  30.4 0.0 collective-permute-start.4
  30.5 0.9 %collective-permute-done.10.refs_7_ = bf16[3,96,1536]{2,1,0:T(8,128)(2,1)S(1)} collective-permute-done((bf16[3,96,1536]{2,1,0:T(8,128)(2,1)S(1)}, bf16[3,96,1536]{2,1,0:T(8,128)(2,1)S(1)}, u32[]{:S(2)}, u32[]{:S(2)}) %collective-permute-start.10) | collective-permute-done | bytes 884768 | tf_op jit(solution)/shard_map/ppermute | solution.py:24
  31.4 6.0 %partial_sum.2 = (f32[2,384,1536]{2,1,0:T(8,128)S(1)}, f32[8,128]{1,0:T(8,128)S(1)}) custom-call(bf16[2,400,768]{2,1,0:T(8,128)(2,1)S(1)} %get-tuple-element.24.x_ref, bf16[3,96,1536]{2,1,0:T(8,128)(2,1)S(1)} %bitcast.23, bf16[3,96,1536]{2,1,0:T(8,128)(2,1)S(1)} %collective-permute-done.7.refs_1_, bf16[3,96,1536]{2,1,0:T(8,128)(2,1)S(1)} %get-tuple-element.23.refs_2_, ...), custom_call_target="tpu_custom_call" | custom-call | flops 5435817984 | bytes 7077888 | tf_op jit(solution)/shard_map/partial_sum/pallas_call | solution.py:160
  37.4 3.0 %collective-permute-done.5.refs_1_ = bf16[3,96,1536]{2,1,0:T(8,128)(2,1)S(1)} collective-permute-done((bf16[3,96,1536]{2,1,0:T(8,128)(2,1)S(1)}, bf16[3,96,1536]{2,1,0:T(8,128)(2,1)S(1)}, u32[]{:S(2)}, u32[]{:S(2)}) %collective-permute-start.5) | collective-permute-done | bytes 884768 | tf_op jit(solution)/shard_map/ppermute | solution.py:38
  40.4 2.2 %collective-permute-done.4.refs_0_ = bf16[3,96,1536]{2,1,0:T(8,128)(2,1)S(1)} collective-permute-done((bf16[3,96,1536]{2,1,0:T(8,128)(2,1)S(1)}, bf16[3,96,1536]{2,1,0:T(8,128)(2,1)S(1)}, u32[]{:S(2)}, u32[]{:S(2)}) %collective-permute-start.4) | collective-permute-done | bytes 884768 | tf_op jit(solution)/shard_map/ppermute | solution.py:31
  42.6 0.3 fence.4
  43.0 1.3 %collective-permute-start.13 = (bf16[3,96,1536]{2,1,0:T(8,128)(2,1)S(1)}, bf16[3,96,1536]{2,1,0:T(8,128)(2,1)S(1)}, u32[]{:S(2)}, u32[]{:S(2)}) collective-permute-start(bf16[3,96,1536]{2,1,0:T(8,128)(2,1)S(1)} %get-tuple-element.29.refs_0_), channel_id=1, source_target_pairs={{0,1},{1,0},{2,3},{3,2},{4,5},{5,4},{6,7},{7,6},{8,9},{9,8},{10,11... | collective-permute-start | bytes 2654216 | tf_op jit(solution)/shard_map/ppermute | solution.py:24
  44.2 0.1 collective-permute-start.14
  44.3 0.5 collective-permute-start.11
  44.8 1.7 %collective-permute-start.12 = (bf16[3,96,1536]{2,1,0:T(8,128)(2,1)S(1)}, bf16[3,96,1536]{2,1,0:T(8,128)(2,1)S(1)}, u32[]{:S(2)}, u32[]{:S(2)}) collective-permute-start(bf16[3,96,1536]{2,1,0:T(8,128)(2,1)S(1)} %get-tuple-element.27.refs_2_), channel_id=1, source_target_pairs={{0,2},{1,131},{2,128},{3,1},{128,130},{129,3},{130,0},{131,129},{4... | collective-permute-start | bytes 2654216 | tf_op jit(solution)/shard_map/ppermute | solution.py:38
  46.5 1.0 %collective-permute-done.14.refs_3_ = bf16[3,96,1536]{2,1,0:T(8,128)(2,1)S(1)} collective-permute-done((bf16[3,96,1536]{2,1,0:T(8,128)(2,1)S(1)}, bf16[3,96,1536]{2,1,0:T(8,128)(2,1)S(1)}, u32[]{:S(2)}, u32[]{:S(2)}) %collective-permute-start.14) | collective-permute-done | bytes 884768 | tf_op jit(solution)/shard_map/ppermute | solution.py:24
  47.5 4.9 %partial_sum.3 = (f32[2,384,1536]{2,1,0:T(8,128)S(1)}, f32[8,128]{1,0:T(8,128)S(1)}) custom-call(bf16[2,400,384]{2,1,0:T(8,128)(2,1)S(1)} %get-tuple-element.28.x_ref, bf16[3,96,1536]{2,1,0:T(8,128)(2,1)S(1)} %get-tuple-element.29.refs_0_, bf16[3,96,1536]{2,1,0:T(8,128)(2,1)S(1)} %collective-permute-done.13.refs_1_, ...), custom_call_target="tpu_custom_call", output_to_operand_aliasing={{0}: (5, {})} | custom-call | flops 2717908992 | bytes 3538944 | tf_op jit(solution)/shard_map/partial_sum/pallas_call | solution.py:160
  52.5 0.0 copy-start.1
  52.5 0.0 copy-start.2
  52.5 4.0 %collective-permute-done.11.refs_0_ = bf16[3,96,1536]{2,1,0:T(8,128)(2,1)S(1)} collective-permute-done((bf16[3,96,1536]{2,1,0:T(8,128)(2,1)S(1)}, bf16[3,96,1536]{2,1,0:T(8,128)(2,1)S(1)}, u32[]{:S(2)}, u32[]{:S(2)}) %collective-permute-start.11) | collective-permute-done | bytes 884768 | tf_op jit(solution)/shard_map/ppermute | solution.py:31
  56.5 0.5 collective-permute-done.12.refs_1_
  57.0 0.2 fence.5
  57.2 2.1 %collective-permute-start.15 = (bf16[3,96,1536]{2,1,0:T(8,128)(2,1)S(1)}, bf16[3,96,1536]{2,1,0:T(8,128)(2,1)S(1)}, u32[]{:S(2)}, u32[]{:S(2)}) collective-permute-start(bf16[3,96,1536]{2,1,0:T(8,128)(2,1)S(1)} %get-tuple-element.32.refs_0_), channel_id=1, source_target_pairs={{0,1},{1,0},{2,3},{3,2},{4,5},{5,4},{6,7},{7,6},{8,9},{9,8},{10,11... | collective-permute-start | bytes 2654216 | tf_op jit(solution)/shard_map/ppermute | solution.py:24
  59.3 0.3 collective-permute-start.16
  59.6 1.7 %collective-permute-done.15.refs_1_ = bf16[3,96,1536]{2,1,0:T(8,128)(2,1)S(1)} collective-permute-done((bf16[3,96,1536]{2,1,0:T(8,128)(2,1)S(1)}, bf16[3,96,1536]{2,1,0:T(8,128)(2,1)S(1)}, u32[]{:S(2)}, u32[]{:S(2)}) %collective-permute-start.15) | collective-permute-done | bytes 884768 | tf_op jit(solution)/shard_map/ppermute | solution.py:24
  61.3 1.3 %collective-permute-done.16.refs_3_ = bf16[3,96,1536]{2,1,0:T(8,128)(2,1)S(1)} collective-permute-done((bf16[3,96,1536]{2,1,0:T(8,128)(2,1)S(1)}, bf16[3,96,1536]{2,1,0:T(8,128)(2,1)S(1)}, u32[]{:S(2)}, u32[]{:S(2)}) %collective-permute-start.16) | collective-permute-done | bytes 884768 | tf_op jit(solution)/shard_map/ppermute | solution.py:24
  62.6 4.6 %finish.3 = bf16[384,1024]{1,0:T(8,128)(2,1)S(1)} custom-call(bf16[2,400,384]{2,1,0:T(8,128)(2,1)S(1)} %get-tuple-element.20.x_ref, bf16[3,96,1536]{2,1,0:T(8,128)(2,1)S(1)} %get-tuple-element.32.refs_0_, bf16[3,96,1536]{2,1,0:T(8,128)(2,1)S(1)} %collective-permute-done.15.refs_1_, bf16[3,96,1536]{2,1,0:T(8,128)(2,1)S(1)} %get-tuple-element.33.refs_2_, ...), custom_call_target="tpu_custom_call" | custom-call | flops 2566914048 | bytes 6684672 | tf_op jit(solution)/shard_map/finish/pallas_call | solution.py:199
  67.2 2.1 %collective-permute-start.17 = (bf16[384,1024]{1,0:T(8,128)(2,1)S(1)}, bf16[384,1024]{1,0:T(8,128)(2,1)S(1)}, u32[]{:S(2)}, u32[]{:S(2)}) collective-permute-start(bf16[384,1024]{1,0:T(8,128)(2,1)S(1)} %finish.3), channel_id=1, source_target_pairs={{0,15},{1,14},{2,13},{3,12},{4,11},{5,10},{6,9},{7,8},{8,7},{9,6},... | collective-permute-start | bytes 2359304 | tf_op jit(solution)/shard_map/ppermute | solution.py:267
  69.3 4.6 %finish.2 = bf16[384,1024]{1,0:T(8,128)(2,1)S(1)} custom-call(bf16[2,400,384]{2,1,0:T(8,128)(2,1)S(1)} %get-tuple-element.20.x_ref, bf16[3,96,1536]{2,1,0:T(8,128)(2,1)S(1)} %get-tuple-element.32.refs_0_, bf16[3,96,1536]{2,1,0:T(8,128)(2,1)S(1)} %collective-permute-done.15.refs_1_, bf16[3,96,1536]{2,1,0:T(8,128)(2,1)S(1)} %get-tuple-element.33.refs_2_, ...), custom_call_target="tpu_custom_call" | custom-call | flops 2566914048 | bytes 6684672 | tf_op jit(solution)/shard_map/finish/pallas_call | solution.py:199
  73.9 15.0 %collective-permute-done.17 = bf16[384,1024]{1,0:T(8,128)(2,1)S(1)} collective-permute-done((bf16[384,1024]{1,0:T(8,128)(2,1)S(1)}, bf16[384,1024]{1,0:T(8,128)(2,1)S(1)}, u32[]{:S(2)}, u32[]{:S(2)}) %collective-permute-start.17) | collective-permute-done | bytes 786464 | tf_op jit(solution)/shard_map/ppermute | solution.py:267
  88.9 1.2 %multiply_convert_fusion = bf16[384,1024]{1,0:T(8,128)(2,1)} fusion(bf16[384,1024]{1,0:T(8,128)(2,1)S(1)} %collective-permute-done.17, bf16[384,1024]{1,0:T(8,128)(2,1)S(1)} %finish.2), kind=kLoop, calls=%fused_computation | loop fusion | flops 1966080 | bytes 2359296 | tf_op jit(solution)/shard_map/convert_element_type | solution.py:269
  (13 shorter events, 0.0 us)
Async XLA Ops:
  0.0 6.7 %collective-permute-start.7 = (bf16[3,96,1536]{2,1,0:T(8,128)(2,1)}, bf16[3,96,1536]{2,1,0:T(8,128)(2,1)S(1)}, u32[]{:S(2)}, u32[]{:S(2)}) collective-permute-start(bf16[3,96,1536]{2,1,0:T(8,128)(2,1)} %bitcast.20), channel_id=1, source_target_pairs={{0,1},{1,0},{2,3},{3,2},{4,5},{5,4},{6,7},{7,6},{8,9},{9,8},{10,11... | collective-permute-start | bytes 2654216 | tf_op jit(solution)/shard_map/ppermute | solution.py:24
  3.2 22.9 %collective-permute-start.3 = (bf16[3,96,1536]{2,1,0:T(8,128)(2,1)}, bf16[3,96,1536]{2,1,0:T(8,128)(2,1)S(1)}, u32[]{:S(2)}, u32[]{:S(2)}) collective-permute-start(bf16[3,96,1536]{2,1,0:T(8,128)(2,1)} %bitcast.21), channel_id=1, source_target_pairs={{0,2},{1,131},{2,128},{3,1},{128,130},{129,3},{130,0},{131,129},{4... | collective-permute-start | bytes 2654216 | tf_op jit(solution)/shard_map/ppermute | solution.py:38
  4.2 21.9 %collective-permute-start.2 = (bf16[3,96,1536]{2,1,0:T(8,128)(2,1)}, bf16[3,96,1536]{2,1,0:T(8,128)(2,1)S(1)}, u32[]{:S(2)}, u32[]{:S(2)}) collective-permute-start(bf16[3,96,1536]{2,1,0:T(8,128)(2,1)} %bitcast.22), channel_id=1, source_target_pairs={{0,4},{1,13},{4,8},{5,1},{8,12},{9,5},{12,0},{13,9},{2,6},{3,15},{... | collective-permute-start | bytes 2654216 | tf_op jit(solution)/shard_map/ppermute | solution.py:31
  6.7 20.2 %collective-permute-start.9 = (bf16[3,96,1536]{2,1,0:T(8,128)(2,1)S(1)}, bf16[3,96,1536]{2,1,0:T(8,128)(2,1)S(1)}, u32[]{:S(2)}, u32[]{:S(2)}) collective-permute-start(bf16[3,96,1536]{2,1,0:T(8,128)(2,1)S(1)} %collective-permute-done.7.refs_1_), channel_id=1, source_target_pairs={{0,4},{1,13},{4,8},{5,1},{8,12},{9,5},{12,0},{13,9},{2,6},{3,15},{... | collective-permute-start | bytes 2654216 | tf_op jit(solution)/shard_map/ppermute | solution.py:31
  8.7 5.1 %collective-permute-start = (bf16[2,1536]{1,0:T(2,128)(2,1)}, bf16[2,1536]{1,0:T(2,128)(2,1)S(1)}, u32[]{:S(2)}, u32[]{:S(2)}) collective-permute-start(bf16[2,1536]{1,0:T(2,128)(2,1)} %pad_maximum_fusion), channel_id=1, source_target_pairs={{0,1},{1,2},{2,3},{3,4},{4,5},{5,6},{6,7},{7,8},{8,9},{9,10},{10,1... | collective-permute-start | bytes 18440 | tf_op jit(solution)/shard_map/ppermute | solution.py:242
  11.2 5.4 %collective-permute-start.1 = (bf16[2,1536]{1,0:T(2,128)(2,1)}, bf16[2,1536]{1,0:T(2,128)(2,1)}, u32[]{:S(2)}, u32[]{:S(2)}) collective-permute-start(bf16[2,1536]{1,0:T(2,128)(2,1)} %pad_maximum_fusion.1), channel_id=1, source_target_pairs={{1,0},{2,1},{3,2},{4,3},{5,4},{6,5},{7,6},{8,7},{9,8},{10,9},{11,1... | collective-permute-start | bytes 18440 | tf_op jit(solution)/shard_map/ppermute | solution.py:243
  16.7 1.3 %copy-start.3 = (bf16[384,1536]{1,0:T(8,128)(2,1)S(1)}, bf16[384,1536]{1,0:T(8,128)(2,1)}, u32[]{:S(2)}) copy-start(bf16[384,1536]{1,0:T(8,128)(2,1)} %forward_ref.1) | copy-start | bytes 3538948
  17.9 1.3 %copy-start.4 = (bf16[384,1536]{1,0:T(8,128)(2,1)S(1)}, bf16[384,1536]{1,0:T(8,128)(2,1)}, u32[]{:S(2)}) copy-start(bf16[384,1536]{1,0:T(8,128)(2,1)} %reverse_ref.1) | copy-start | bytes 3538948
  26.1 5.3 %copy-start.5 = (bf16[1,3,96,1536]{3,2,1,0:T(8,128)(2,1)S(1)}, bf16[1,3,96,1536]{3,2,1,0:T(8,128)(2,1)}, u32[]{:S(2)}) copy-start(bf16[1,3,96,1536]{3,2,1,0:T(8,128)(2,1)} %param.8) | copy-start | bytes 2654212
  26.3 4.1 %collective-permute-start.6 = (bf16[3,96,1536]{2,1,0:T(8,128)(2,1)S(1)}, bf16[3,96,1536]{2,1,0:T(8,128)(2,1)S(1)}, u32[]{:S(2)}, u32[]{:S(2)}) collective-permute-start(bf16[3,96,1536]{2,1,0:T(8,128)(2,1)S(1)} %get-tuple-element.23.refs_2_), channel_id=1, source_target_pairs={{0,1},{1,0},{2,3},{3,2},{4,5},{5,4},{6,7},{7,6},{8,9},{9,8},{10,11... | collective-permute-start | bytes 2654216 | tf_op jit(solution)/shard_map/ppermute | solution.py:24
  26.4 4.0 %collective-permute-start.8 = (bf16[3,96,1536]{2,1,0:T(8,128)(2,1)S(1)}, bf16[3,96,1536]{2,1,0:T(8,128)(2,1)S(1)}, u32[]{:S(2)}, u32[]{:S(2)}) collective-permute-start(bf16[3,96,1536]{2,1,0:T(8,128)(2,1)S(1)} %get-tuple-element.22.refs_4_), channel_id=1, source_target_pairs={{0,1},{1,0},{2,3},{3,2},{4,5},{5,4},{6,7},{7,6},{8,9},{9,8},{10,11... | collective-permute-start | bytes 2654216 | tf_op jit(solution)/shard_map/ppermute | solution.py:24
  26.9 4.4 %collective-permute-start.10 = (bf16[3,96,1536]{2,1,0:T(8,128)(2,1)S(1)}, bf16[3,96,1536]{2,1,0:T(8,128)(2,1)S(1)}, u32[]{:S(2)}, u32[]{:S(2)}) collective-permute-start(bf16[3,96,1536]{2,1,0:T(8,128)(2,1)S(1)} %collective-permute-done.9.refs_6_), channel_id=1, source_target_pairs={{0,1},{1,0},{2,3},{3,2},{4,5},{5,4},{6,7},{7,6},{8,9},{9,8},{10,11... | collective-permute-start | bytes 2654216 | tf_op jit(solution)/shard_map/ppermute | solution.py:24
  27.2 13.2 %collective-permute-start.5 = (bf16[3,96,1536]{2,1,0:T(8,128)(2,1)S(1)}, bf16[3,96,1536]{2,1,0:T(8,128)(2,1)S(1)}, u32[]{:S(2)}, u32[]{:S(2)}) collective-permute-start(bf16[3,96,1536]{2,1,0:T(8,128)(2,1)S(1)} %get-tuple-element.22.refs_4_), channel_id=1, source_target_pairs={{0,2},{1,131},{2,128},{3,1},{128,130},{129,3},{130,0},{131,129},{4... | collective-permute-start | bytes 2654216 | tf_op jit(solution)/shard_map/ppermute | solution.py:38
  30.4 12.2 %collective-permute-start.4 = (bf16[3,96,1536]{2,1,0:T(8,128)(2,1)S(1)}, bf16[3,96,1536]{2,1,0:T(8,128)(2,1)S(1)}, u32[]{:S(2)}, u32[]{:S(2)}) collective-permute-start(bf16[3,96,1536]{2,1,0:T(8,128)(2,1)S(1)} %get-tuple-element.22.refs_4_), channel_id=1, source_target_pairs={{0,4},{1,13},{4,8},{5,1},{8,12},{9,5},{12,0},{13,9},{2,6},{3,15},{... | collective-permute-start | bytes 2654216 | tf_op jit(solution)/shard_map/ppermute | solution.py:31
  43.0 3.6 %collective-permute-start.13 = (bf16[3,96,1536]{2,1,0:T(8,128)(2,1)S(1)}, bf16[3,96,1536]{2,1,0:T(8,128)(2,1)S(1)}, u32[]{:S(2)}, u32[]{:S(2)}) collective-permute-start(bf16[3,96,1536]{2,1,0:T(8,128)(2,1)S(1)} %get-tuple-element.29.refs_0_), channel_id=1, source_target_pairs={{0,1},{1,0},{2,3},{3,2},{4,5},{5,4},{6,7},{7,6},{8,9},{9,8},{10,11... | collective-permute-start | bytes 2654216 | tf_op jit(solution)/shard_map/ppermute | solution.py:24
  44.2 3.3 %collective-permute-start.14 = (bf16[3,96,1536]{2,1,0:T(8,128)(2,1)S(1)}, bf16[3,96,1536]{2,1,0:T(8,128)(2,1)S(1)}, u32[]{:S(2)}, u32[]{:S(2)}) collective-permute-start(bf16[3,96,1536]{2,1,0:T(8,128)(2,1)S(1)} %get-tuple-element.27.refs_2_), channel_id=1, source_target_pairs={{0,1},{1,0},{2,3},{3,2},{4,5},{5,4},{6,7},{7,6},{8,9},{9,8},{10,11... | collective-permute-start | bytes 2654216 | tf_op jit(solution)/shard_map/ppermute | solution.py:24
  44.3 12.2 %collective-permute-start.11 = (bf16[3,96,1536]{2,1,0:T(8,128)(2,1)S(1)}, bf16[3,96,1536]{2,1,0:T(8,128)(2,1)S(1)}, u32[]{:S(2)}, u32[]{:S(2)}) collective-permute-start(bf16[3,96,1536]{2,1,0:T(8,128)(2,1)S(1)} %get-tuple-element.26), channel_id=1, source_target_pairs={{0,4},{1,13},{4,8},{5,1},{8,12},{9,5},{12,0},{13,9},{2,6},{3,15},{... | collective-permute-start | bytes 2654216 | tf_op jit(solution)/shard_map/ppermute | solution.py:31
  44.8 12.2 %collective-permute-start.12 = (bf16[3,96,1536]{2,1,0:T(8,128)(2,1)S(1)}, bf16[3,96,1536]{2,1,0:T(8,128)(2,1)S(1)}, u32[]{:S(2)}, u32[]{:S(2)}) collective-permute-start(bf16[3,96,1536]{2,1,0:T(8,128)(2,1)S(1)} %get-tuple-element.27.refs_2_), channel_id=1, source_target_pairs={{0,2},{1,131},{2,128},{3,1},{128,130},{129,3},{130,0},{131,129},{4... | collective-permute-start | bytes 2654216 | tf_op jit(solution)/shard_map/ppermute | solution.py:38
  47.5 15.1 %copy-start = (bf16[1536,1024]{1,0:T(8,128)(2,1)S(1)}, bf16[1536,1024]{1,0:T(8,128)(2,1)}, u32[]{:S(2)}) copy-start(bf16[1536,1024]{1,0:T(8,128)(2,1)} %refs_6_.3) | copy-start | bytes 9437188
  52.5 10.1 %copy-start.1 = (f32[1,1536]{1,0:T(1,128)S(1)}, f32[1,1536]{1,0:T(1,128)}, u32[]{:S(2)}) copy-start(f32[1,1536]{1,0:T(1,128)} %refs_5_.3) | copy-start | bytes 18436
  52.5 10.1 %copy-start.2 = (f32[1024]{0:T(1024)S(1)}, f32[1024]{0:T(1024)}, u32[]{:S(2)}) copy-start(f32[1024]{0:T(1024)} %param.11) | copy-start | bytes 12292
  57.2 4.1 %collective-permute-start.15 = (bf16[3,96,1536]{2,1,0:T(8,128)(2,1)S(1)}, bf16[3,96,1536]{2,1,0:T(8,128)(2,1)S(1)}, u32[]{:S(2)}, u32[]{:S(2)}) collective-permute-start(bf16[3,96,1536]{2,1,0:T(8,128)(2,1)S(1)} %get-tuple-element.32.refs_0_), channel_id=1, source_target_pairs={{0,1},{1,0},{2,3},{3,2},{4,5},{5,4},{6,7},{7,6},{8,9},{9,8},{10,11... | collective-permute-start | bytes 2654216 | tf_op jit(solution)/shard_map/ppermute | solution.py:24
  59.3 3.3 %collective-permute-start.16 = (bf16[3,96,1536]{2,1,0:T(8,128)(2,1)S(1)}, bf16[3,96,1536]{2,1,0:T(8,128)(2,1)S(1)}, u32[]{:S(2)}, u32[]{:S(2)}) collective-permute-start(bf16[3,96,1536]{2,1,0:T(8,128)(2,1)S(1)} %get-tuple-element.33.refs_2_), channel_id=1, source_target_pairs={{0,1},{1,0},{2,3},{3,2},{4,5},{5,4},{6,7},{7,6},{8,9},{9,8},{10,11... | collective-permute-start | bytes 2654216 | tf_op jit(solution)/shard_map/ppermute | solution.py:24
  67.2 21.7 %collective-permute-start.17 = (bf16[384,1024]{1,0:T(8,128)(2,1)S(1)}, bf16[384,1024]{1,0:T(8,128)(2,1)S(1)}, u32[]{:S(2)}, u32[]{:S(2)}) collective-permute-start(bf16[384,1024]{1,0:T(8,128)(2,1)S(1)} %finish.3), channel_id=1, source_target_pairs={{0,15},{1,14},{2,13},{3,12},{4,11},{5,10},{6,9},{7,8},{8,7},{9,6},... | collective-permute-start | bytes 2359304 | tf_op jit(solution)/shard_map/ppermute | solution.py:267

commit v6 on v5

v6 whole, which is shorter than its diff:
```python
import functools

import jax
import jax.numpy as jnp
from jax import lax
from jax.experimental import pallas as pl
from jax.experimental.pallas import tpu as pltpu
from jax.sharding import Mesh
from jax.sharding import PartitionSpec as P

AXES = ("y_hi", "z", "x", "y_lo", "core")
SEQ = ("x", "y_lo", "core")
XN, YN, CN = 4, 4, 2
VMEM_LIMIT = 24 * 1024 * 1024
EDGE = 16
TILE = 512
PARTS = (8, 4, 4)
ROWS = 128
AWAY = 128
TOKEN = jax.ShapeDtypeStruct((8, 128), jnp.float32)
INV_SQRT2 = 0.7071067811865476


def core_swap(value):
    return lax.ppermute(value, "core", [(0, 1), (1, 0)])


def x_shift(value):
    route = []
    for x in range(XN):
        route += [(x * 2, (x + 1) % XN * 2), (x * 2 + 1, (x - 1) % XN * 2 + 1)]
    return lax.ppermute(value, ("x", "core"), route)


def y_shift(value):
    route = []
    for y in range(YN):
        route += [(y * 2, (y + 1) % YN * 2), (y * 2 + 1, (y - 1) % YN * 2 + 1)]
    return lax.ppermute(value, ("y_hi", "y_lo", "core"), route)


def fence_kernel(count, *refs):
    for source, target in zip(refs[:count], refs[-count:]):
        target[...] = source[...]


def fence(token, *values):
    inside = pl.BlockSpec(memory_space=pltpu.VMEM)
    operands = values if token is None else (*values, token)
    return pl.pallas_call(
        functools.partial(fence_kernel, len(values)),
        out_shape=[jax.ShapeDtypeStruct(v.shape, v.dtype) for v in values],
        in_specs=[inside] * len(operands),
        out_specs=[inside] * len(values),
        input_output_aliases={i: i for i in range(len(values))},
        compiler_params=pltpu.CompilerParams(vmem_limit_bytes=8 * 1024 * 1024),
        name="fence",
    )(*operands)


def edge_tile(after, before):
    width = after.shape[1]
    edge = lax.broadcasted_iota(jnp.int32, (EDGE, width), 0)
    tile = jnp.where(edge == 0, after, jnp.where(edge == EDGE - 1, before, 0.0))
    return tile.astype(jnp.bfloat16)


def prepare_kernel(place_ref, forward_ref, reverse_ref, low_ref, high_ref, *refs):
    x_refs, y_refs, move_refs, away_ref, token_ref = refs[:3], refs[3:6], refs[6:9], *refs[9:11]
    full_ref, flip_ref, reverse_vmem, sem = refs[11:]
    token_ref[...] = jnp.zeros_like(token_ref)
    rows, width = forward_ref.shape
    kept = rows - AWAY
    part = width // 16
    forward_copy = pltpu.make_async_copy(forward_ref, full_ref.at[pl.ds(0, rows), :], sem.at[0])
    forward_copy.start()
    reverse_copy = pltpu.make_async_copy(reverse_ref, reverse_vmem, sem.at[1])
    reverse_copy.start()
    begin = 0
    for move_ref, count in zip(move_refs, PARTS):
        size = count * part
        lane = lax.broadcasted_iota(jnp.int32, (1, size), 1)
        wanted = jnp.zeros((1, size), jnp.int32)
        for block in range(count):
            inside = (lane >= block * part) & (lane < (block + 1) * part)
            wanted = jnp.where(inside, lane + (place_ref[begin + block] - block) * part, wanted)
        source = lax.broadcasted_iota(jnp.int32, (width, size), 0)
        move_ref[...] = jnp.where(source == wanted, 1.0, 0.0).astype(jnp.bfloat16)
        begin += count
    low = low_ref[...].astype(jnp.float32)
    high = high_ref[...].astype(jnp.float32)
    row = lax.broadcasted_iota(jnp.int32, (rows, rows), 0)
    column = lax.broadcasted_iota(jnp.int32, (rows, rows), 1)
    flip = jnp.where(row + column == rows - 1, 1.0, 0.0).astype(jnp.bfloat16)
    reverse_copy.wait()
    flipped = jnp.dot(flip, reverse_vmem[...], preferred_element_type=jnp.float32)
    flip_ref[:kept, :] = flipped[:kept].astype(jnp.bfloat16)
    flip_ref[kept:, :] = edge_tile(flipped[kept : kept + 1], high[1:2])
    away_ref[:AWAY, :] = flipped[kept:].astype(jnp.bfloat16)
    away_ref[AWAY:, :] = edge_tile(low[1:2], flipped[kept - 1 : kept])
    full_ref[rows:, :] = edge_tile(high[0:1], low[0:1])
    forward_copy.wait()
    for x_ref, y_ref, move_ref in zip(x_refs, y_refs, move_refs):
        for source_ref, target_ref in ((full_ref, x_ref), (flip_ref, y_ref)):
            target_ref[...] = jnp.dot(
                source_ref[...], move_ref[...], preferred_element_type=jnp.float32
            ).astype(jnp.bfloat16)


def prepare(place, forward_embed, reverse_embed, low, high):
    rows, width = forward_embed.shape
    kept = rows - AWAY
    part = width // 16
    inside = pl.BlockSpec(memory_space=pltpu.VMEM)

    def stripes(height):
        return [jax.ShapeDtypeStruct((height, count * part), jnp.bfloat16) for count in PARTS]

    outs = pl.pallas_call(
        prepare_kernel,
        out_shape=stripes(rows + EDGE)
        + stripes(kept + EDGE)
        + stripes(width)
        + [jax.ShapeDtypeStruct((AWAY + EDGE, width), jnp.bfloat16), TOKEN],
        in_specs=[pl.BlockSpec(memory_space=pltpu.SMEM)]
        + [pl.BlockSpec(memory_space=pltpu.HBM)] * 2
        + [inside] * 2,
        out_specs=[inside] * 11,
        scratch_shapes=[
            pltpu.VMEM((rows + EDGE, width), jnp.bfloat16),
            pltpu.VMEM((kept + EDGE, width), jnp.bfloat16),
            pltpu.VMEM((rows, width), jnp.bfloat16),
            pltpu.SemaphoreType.DMA((2,)),
        ],
        compiler_params=pltpu.CompilerParams(vmem_limit_bytes=VMEM_LIMIT),
        cost_estimate=pl.CostEstimate(
            flops=4 * rows * width * width, bytes_accessed=8 * rows * width, transcendentals=0
        ),
        name="prepare",
    )(place, forward_embed, reverse_embed, low, high)
    return list(zip(outs[:3], outs[3:6])), outs[6:9], outs[9], outs[10]


def convolve(x, flipped, blocks, columns):
    rows = x.shape[0] - EDGE
    total = None
    for tap in range(3):
        weight = jnp.concatenate([block[tap, :, columns] for block in blocks], axis=0)
        value = jnp.dot(x, weight, preferred_element_type=jnp.float32)
        shift = tap - 1 if flipped else 1 - tap
        if shift:
            value = pltpu.roll(value, shift % (rows + EDGE), 0)
        value = value[:rows]
        total = value if total is None else total + value
    return total


def partial_kernel(count, first, *refs):
    strands, blocks, refs = refs[:2], refs[2 : 2 + count], refs[2 + count :]
    out_refs, token_ref = refs[-3:-1], refs[-1]
    token_ref[...] = jnp.zeros_like(token_ref)
    channels = out_refs[0].shape[1]
    for start in range(0, channels, TILE):
        columns = pl.ds(start, TILE)
        for strand in range(2):
            acc = convolve(strands[strand][...], strand == 1, blocks, columns)
            if not first:
                acc = acc + refs[strand][:, columns]
            out_refs[strand][:, columns] = acc


def partial_sum(strands, sources, prev):
    rows = [x.shape[0] - EDGE for x in strands]
    depth, channels = strands[0].shape[1], sources[0].shape[2]
    operands = [*strands, *sources] + ([] if prev is None else list(prev))
    inside = pl.BlockSpec(memory_space=pltpu.VMEM)
    last = len(operands)
    forward, reverse, token = pl.pallas_call(
        functools.partial(partial_kernel, len(sources), prev is None),
        out_shape=[jax.ShapeDtypeStruct((count, channels), jnp.float32) for count in rows]
        + [TOKEN],
        in_specs=[inside] * last,
        out_specs=[inside] * 3,
        input_output_aliases={} if prev is None else {last - 2: 0, last - 1: 1},
        compiler_params=pltpu.CompilerParams(vmem_limit_bytes=VMEM_LIMIT),
        cost_estimate=pl.CostEstimate(
            flops=6 * sum(rows) * depth * channels,
            bytes_accessed=6 * depth * channels,
            transcendentals=0,
        ),
        name="partial_sum",
    )(*operands)
    return (forward, reverse), token


def gelu(acc):
    return (0.5 * acc * (1.0 + lax.erf(acc * INV_SQRT2))).astype(jnp.bfloat16)


def predict(hidden_ref, head_ref, head_bias_ref, out_ref):
    rows = out_ref.shape[0]
    for row in range(0, rows, ROWS):
        here = pl.ds(row, ROWS)
        logits = jnp.dot(hidden_ref[here, :], head_ref[...], preferred_element_type=jnp.float32)
        logits = logits + head_bias_ref[...]
        tracks = jnp.maximum(logits, 0.0) + jnp.log1p(jnp.exp(-jnp.abs(logits)))
        out_ref[here, :] = tracks.astype(jnp.bfloat16)


def finish_kernel(flipped, count, x_ref, *refs):
    sources, refs = refs[:count], refs[count:]
    prev_ref, bias_ref, head_ref, head_bias_ref, out_ref, hidden_ref = refs
    for start in range(0, hidden_ref.shape[1], TILE):
        here = pl.ds(start, TILE)
        acc = convolve(x_ref[...], flipped, sources, here)
        hidden_ref[:, here] = gelu(acc + prev_ref[:, here] + bias_ref[:, here])
    predict(hidden_ref, head_ref, head_bias_ref, out_ref)


def finish(flipped, x, sources, prev, bias, head, head_bias):
    rows, depth = x.shape[0] - EDGE, x.shape[1]
    channels, tracks = head.shape
    inside = pl.BlockSpec(memory_space=pltpu.VMEM)
    return pl.pallas_call(
        functools.partial(finish_kernel, flipped, len(sources)),
        out_shape=jax.ShapeDtypeStruct((rows, tracks), jnp.bfloat16),
        in_specs=[inside] * (len(sources) + 5),
        out_specs=inside,
        scratch_shapes=[pltpu.VMEM((rows, channels), jnp.bfloat16)],
        compiler_params=pltpu.CompilerParams(vmem_limit_bytes=VMEM_LIMIT),
        cost_estimate=pl.CostEstimate(
            flops=2 * rows * channels * (3 * depth + tracks),
            bytes_accessed=6 * depth * channels + 2 * channels * tracks,
            transcendentals=rows * channels,
        ),
        name="finish",
    )(x, *sources, prev, bias, head, head_bias[None])


def whole_kernel(sizes, away_ref, *refs):
    moves, refs = refs[: len(sizes)], refs[len(sizes) :]
    sources, refs = refs[: sum(sizes)], refs[sum(sizes) :]
    bias_ref, head_ref, head_bias_ref, out_ref, hidden_ref = refs
    stripes = [
        jnp.dot(away_ref[...], move[...], preferred_element_type=jnp.float32).astype(jnp.bfloat16)
        for move in moves
    ]
    for start in range(0, hidden_ref.shape[1], TILE):
        here = pl.ds(start, TILE)
        acc, begin = bias_ref[:, here], 0
        for stripe, count in zip(stripes, sizes):
            acc = acc + convolve(stripe, True, sources[begin : begin + count], here)
            begin += count
        hidden_ref[:, here] = gelu(acc)
    predict(hidden_ref, head_ref, head_bias_ref, out_ref)


def whole(away, moves, sources, bias, head, head_bias):
    rows = away.shape[0] - EDGE
    channels, tracks = head.shape
    inside = pl.BlockSpec(memory_space=pltpu.VMEM)
    return pl.pallas_call(
        functools.partial(whole_kernel, PARTS),
        out_shape=jax.ShapeDtypeStruct((rows, tracks), jnp.bfloat16),
        in_specs=[inside] * (len(moves) + len(sources) + 4),
        out_specs=inside,
        scratch_shapes=[pltpu.VMEM((rows, channels), jnp.bfloat16)],
        compiler_params=pltpu.CompilerParams(vmem_limit_bytes=VMEM_LIMIT),
        cost_estimate=pl.CostEstimate(
            flops=2 * rows * channels * (4 * channels + tracks),
            bytes_accessed=6 * channels * channels,
            transcendentals=rows * channels,
        ),
        name="whole",
    )(away, *moves, *sources, bias, head, head_bias[None])


def per_device(forward_embed, reverse_embed, conv_weight, conv_bias, head_weight, head_bias):
    own = conv_weight[0]
    x, y, core = lax.axis_index("x"), lax.axis_index("y_lo"), lax.axis_index("core")
    ends = XN * 2 * CN

    def seq(x_of, y_of, core_of):
        return (x_of % XN) * 4 + y_of * 2 + core_of

    step = 1 - 2 * core
    back, fore, far = x - step + XN, x + step + XN, x + 2
    other, over = 1 - core, 1 - y
    place = jnp.stack(
        [
            seq(x, y, core), seq(x, y, other), seq(x, over, core), seq(x, over, other),
            seq(back, y, core), seq(fore, y, other), seq(back, y, other), seq(fore, y, core),
            seq(back, over, core), seq(fore, over, other), seq(far, y, core), seq(far, y, other),
            seq(back, over, other), seq(fore, over, core),
            seq(far, over, core), seq(far, over, other),
        ]
    ).astype(jnp.int32)

    near = x_shift(own)
    across = y_shift(own)
    sibling = core_swap(own)
    second = x_shift(sibling)
    up = [(i, i + 1) for i in range(ends - 1)]
    down = [(b, a) for a, b in up]
    low = lax.ppermute(jnp.stack([forward_embed[-1], reverse_embed[-1]]), SEQ, up)
    high = lax.ppermute(jnp.stack([forward_embed[0], reverse_embed[0]]), SEQ, down)
    (x_1, x_2, x_3), moves, away, token = prepare(place, forward_embed, reverse_embed, low, high)
    near, across = fence(token, near, across)

    distant = x_shift(near)
    near_over = y_shift(near)
    across_b = core_swap(across)
    near_b = core_swap(near)
    second_b = core_swap(second)
    shards_1 = [own, sibling, across, across_b, near, near_b, second, second_b]
    acc, token = partial_sum(x_1, shards_1, None)
    distant, near_over, across_b = fence(token, distant, near_over, across_b)
    shards_1[3] = across_b

    second_over = x_shift(across_b)
    distant_over = y_shift(distant)
    near_over_b = core_swap(near_over)
    distant_b = core_swap(distant)
    shards_2 = [near_over, near_over_b, distant, distant_b]
    acc, token = partial_sum(x_2, shards_2, acc)
    second_over, distant_over, away = fence(token, second_over, distant_over, away)

    mirror = [(i, ends - 1 - i) for i in range(ends)]
    away = lax.ppermute(away, SEQ, mirror)
    shards_3 = [second_over, core_swap(second_over), distant_over, core_swap(distant_over)]
    rest = (conv_bias, head_weight, head_bias)
    reverse_tracks = finish(True, x_3[1], shards_3, acc[1], *rest)
    mirrored = lax.ppermute(reverse_tracks, SEQ, mirror)
    forward_tracks = finish(False, x_3[0], shards_3, acc[0], *rest)
    away_tracks = whole(away, moves, shards_1 + shards_2 + shards_3, *rest)
    reverse = jnp.concatenate([mirrored, away_tracks])
    mean = 0.5 * (forward_tracks.astype(jnp.float32) + reverse.astype(jnp.float32))
    return mean.astype(jnp.bfloat16)


def solution(mesh):
    fine = Mesh(mesh.devices.reshape(2, 8, XN, 2, CN), AXES)
    return jax.shard_map(
        per_device,
        mesh=fine,
        in_specs=(
            P(AXES, None),
            P(AXES, None),
            P(None, None, SEQ, None),
            P(),
            P(),
            P(),
        ),
        out_specs=P(AXES, None),
        check_vma=False,
    )
```

time: 90.4 us -> 86.9 us (0.961)
  waiting for transfers between devices: 32.6 us -> 25.4 us
  starting transfers between devices: 23.7 us -> 25.8 us
  Pallas kernels: 27.8 us -> 29.4 us
    ppermute x1 -> x2, waiting for transfers between devices: 15 us -> 8.92 us  [the longest x1 6.46 us: per_device(): mirrored = lax.ppermute(reverse_tracks, SEQ, mirror)]
    pallas_call x3 -> x4, Pallas kernels: 16.1 us -> 19.2 us  [the longest x2 7.77 us: finish(): pl.pallas_call(functools.partial(finish_kernel, flipped, len(sources)), o...]
    ppermute x8, waiting for transfers between devices: 4.92 us -> 2.66 us  [core_swap(): return lax.ppermute(value, 'core', [(0, 1), (1, 0)])]
    ppermute x4, starting transfers between devices: 3.52 us -> 5.34 us  [x_shift(): return lax.ppermute(value, ('x', 'core'), route)]
    pallas_call x2, Pallas kernels: 10.9 us -> 9.42 us  [partial_sum(): pl.pallas_call(functools.partial(partial_kernel, len(sources), prev is No...]
    ppermute x1 -> x2, starting transfers between devices: 2.06 us -> 2.75 us  [the longest x1 1.4 us: per_device(): mirrored = lax.ppermute(reverse_tracks, SEQ, mirror)]
  transfers between devices with their start and end apart: 18 -> 19, of which waited for: 10 -> 10; matrix products, arithmetic and copies ran while one was open for 2% -> 2% of each run, Pallas kernels for 25% -> 33%
where the time goes in v6:
time: 86.9 us; the launch traced here: 86.6 us
  Pallas kernels  29.4 us (34%)
  starting transfers between devices  25.8 us (30%)
  waiting for transfers between devices  25.4 us (29%)
  local copies, waits for them, and re-layouts  3.47 us (4%)
  other arithmetic  2.39 us (3%)
    pallas_call x2, Pallas kernels, partial_sum(): pl.pallas_call(functools.partial(partial_kernel, len(sources), prev is No...  9.42 us
    pallas_call x2, Pallas kernels, finish(): pl.pallas_call(functools.partial(finish_kernel, flipped, len(sources)), o...  7.77 us
    ppermute x8, starting transfers between devices, core_swap(): return lax.ppermute(value, 'core', [(0, 1), (1, 0)])  7.43 us
    pallas_call x1, Pallas kernels, prepare(): pl.pallas_call(prepare_kernel, out_shape=stripes(rows + EDGE) + stripes(k...  7.18 us
    ppermute x4, waiting for transfers between devices, x_shift(): return lax.ppermute(value, ('x', 'core'), route)  6.87 us
    ppermute x1, waiting for transfers between devices, per_device(): mirrored = lax.ppermute(reverse_tracks, SEQ, mirror)  6.46 us
    ppermute x3, starting transfers between devices, y_shift(): return lax.ppermute(value, ('y_hi', 'y_lo', 'core'), route)  5.94 us
    ppermute x4, starting transfers between devices, x_shift(): return lax.ppermute(value, ('x', 'core'), route)  5.34 us
  transfers between devices with their start and end apart: 19, of which 10 were waited for; matrix products, arithmetic and copies ran while one was open for 2% of the time, Pallas kernels for 33%

profile of v6, /device:TPU:1, one launch (start us, length us, event | category | flops | bytes accessed | tf_op | source)
XLA Modules:
  0.0 86.6 jit_solution(6035764854947122724)
XLA Ops:
  0.0 3.2 %collective-permute-start.7 = (bf16[3,96,1536]{2,1,0:T(8,128)(2,1)}, bf16[3,96,1536]{2,1,0:T(8,128)(2,1)S(1)}, u32[]{:S(2)}, u32[]{:S(2)}) collective-permute-start(bf16[3,96,1536]{2,1,0:T(8,128)(2,1)} %bitcast.18), channel_id=1, source_target_pairs={{0,1},{1,0},{2,3},{3,2},{4,5},{5,4},{6,7},{7,6},{8,9},{9,8},{10,11... | collective-permute-start | bytes 2654216 | tf_op jit(solution)/shard_map/ppermute | solution.py:25
  3.2 0.7 collective-permute-start.2
  4.0 2.7 %collective-permute-start.3 = (bf16[3,96,1536]{2,1,0:T(8,128)(2,1)}, bf16[3,96,1536]{2,1,0:T(8,128)(2,1)S(1)}, u32[]{:S(2)}, u32[]{:S(2)}) collective-permute-start(bf16[3,96,1536]{2,1,0:T(8,128)(2,1)} %bitcast.20), channel_id=1, source_target_pairs={{0,2},{1,131},{2,128},{3,1},{128,130},{129,3},{130,0},{131,129},{4... | collective-permute-start | bytes 2654216 | tf_op jit(solution)/shard_map/ppermute | solution.py:39
  6.7 0.5 collective-permute-start.9
  7.3 0.8 fusion
  8.1 0.6 pad_maximum_fusion
  8.7 1.9 %collective-permute-start = (bf16[2,1536]{1,0:T(2,128)(2,1)}, bf16[2,1536]{1,0:T(2,128)(2,1)S(1)}, u32[]{:S(2)}, u32[]{:S(2)}) collective-permute-start(bf16[2,1536]{1,0:T(2,128)(2,1)} %pad_maximum_fusion), channel_id=1, source_target_pairs={{0,1},{1,2},{2,3},{3,4},{4,5},{5,6},{6,7},{7,8},{8,9},{9,10},{10,1... | collective-permute-start | bytes 18440 | tf_op jit(solution)/shard_map/ppermute | solution.py:305
  10.6 0.6 pad_maximum_fusion.1
  11.2 2.4 %collective-permute-start.1 = (bf16[2,1536]{1,0:T(2,128)(2,1)}, bf16[2,1536]{1,0:T(2,128)(2,1)}, u32[]{:S(2)}, u32[]{:S(2)}) collective-permute-start(bf16[2,1536]{1,0:T(2,128)(2,1)} %pad_maximum_fusion.1), channel_id=1, source_target_pairs={{1,0},{2,1},{3,2},{4,3},{5,4},{6,5},{7,6},{8,7},{9,8},{10,9},{11,1... | collective-permute-start | bytes 18440 | tf_op jit(solution)/shard_map/ppermute | solution.py:306
  13.7 0.1 stack.73.place_ref
  13.8 2.9 %collective-permute-done.1.high_ref = bf16[2,1536]{1,0:T(2,128)(2,1)} collective-permute-done((bf16[2,1536]{1,0:T(2,128)(2,1)}, bf16[2,1536]{1,0:T(2,128)(2,1)}, u32[]{:S(2)}, u32[]{:S(2)}) %collective-permute-start.1) | collective-permute-done | bytes 6176 | tf_op jit(solution)/shard_map/ppermute | solution.py:306
  16.7 1.3 %copy-done.4 = bf16[384,1536]{1,0:T(8,128)(2,1)S(1)} copy-done((bf16[384,1536]{1,0:T(8,128)(2,1)S(1)}, bf16[384,1536]{1,0:T(8,128)(2,1)}, u32[]{:S(2)}) %copy-start.4) | copy-done | bytes 1179672
  17.9 1.3 %copy-done.5 = bf16[384,1536]{1,0:T(8,128)(2,1)S(1)} copy-done((bf16[384,1536]{1,0:T(8,128)(2,1)S(1)}, bf16[384,1536]{1,0:T(8,128)(2,1)}, u32[]{:S(2)}) %copy-start.5) | copy-done | bytes 1179672
  19.2 7.2 %prepare.1 = (bf16[400,768]{1,0:T(8,128)(2,1)S(1)}, bf16[400,384]{1,0:T(8,128)(2,1)S(1)}, bf16[400,384]{1,0:T(8,128)(2,1)S(1)}, bf16[272,768]{1,0:T(8,128)(2,1)S...) custom-call(s32[16]{0:T(128)S(1)} %stack.73.place_ref, ...), custom_call_target="tpu_custom_call" | custom-call | flops 3623878656 | bytes 4718592 | tf_op jit(solution)/shard_map/prepare/pallas_call | solution.py:119
  26.4 0.0 copy-start.1
  26.4 0.2 fence.3
  26.7 0.1 collective-permute-start.6
  26.8 0.5 collective-permute-start.8
  27.3 0.1 collective-permute-start.10
  27.4 2.1 %collective-permute-start.4 = (bf16[3,96,1536]{2,1,0:T(8,128)(2,1)S(1)}, bf16[3,96,1536]{2,1,0:T(8,128)(2,1)S(1)}, u32[]{:S(2)}, u32[]{:S(2)}) collective-permute-start(bf16[3,96,1536]{2,1,0:T(8,128)(2,1)S(1)} %get-tuple-element.32.refs_6_.refs_7_), channel_id=1, source_target_pairs={{0,4},{1,13},{4,8},{5,1},{8,12},{9,5},{12,0},{13,9},{2,6},{3,15},{... | collective-permute-start | bytes 2654216 | tf_op jit(solution)/shard_map/ppermute | solution.py:32
  29.5 1.5 %collective-permute-start.5 = (bf16[3,96,1536]{2,1,0:T(8,128)(2,1)S(1)}, bf16[3,96,1536]{2,1,0:T(8,128)(2,1)S(1)}, u32[]{:S(2)}, u32[]{:S(2)}) collective-permute-start(bf16[3,96,1536]{2,1,0:T(8,128)(2,1)S(1)} %get-tuple-element.32.refs_6_.refs_7_), channel_id=1, source_target_pairs={{0,2},{1,131},{2,128},{3,1},{128,130},{129,3},{130,0},{131,129},{4... | collective-permute-start | bytes 2654216 | tf_op jit(solution)/shard_map/ppermute | solution.py:39
  30.9 0.8 collective-permute-done.10.refs_9_.refs_10_
  31.7 5.1 %partial_sum.2 = (f32[384,1536]{1,0:T(8,128)S(1)}, f32[256,1536]{1,0:T(8,128)S(1)}, f32[8,128]{1,0:T(8,128)S(1)}) custom-call(bf16[400,768]{1,0:T(8,128)(2,1)S(1)} %get-tuple-element.34.refs_0_, bf16[272,768]{1,0:T(8,128)(2,1)S(1)} %get-tuple-element.35.refs_1_, bf16[3,96,1536]{2,1,0:T(8,128)(2,1)S(1)} %bitcast.21, ...), custom_call_target="tpu_custom_call" | custom-call | flops 4529848320 | bytes 7077888 | tf_op jit(solution)/shard_map/partial_sum/pallas_call | solution.py:178
  36.8 2.8 %collective-permute-done.4.refs_0_ = bf16[3,96,1536]{2,1,0:T(8,128)(2,1)S(1)} collective-permute-done((bf16[3,96,1536]{2,1,0:T(8,128)(2,1)S(1)}, bf16[3,96,1536]{2,1,0:T(8,128)(2,1)S(1)}, u32[]{:S(2)}, u32[]{:S(2)}) %collective-permute-start.4) | collective-permute-done | bytes 884768 | tf_op jit(solution)/shard_map/ppermute | solution.py:32
  39.6 2.1 %collective-permute-done.5.refs_1_ = bf16[3,96,1536]{2,1,0:T(8,128)(2,1)S(1)} collective-permute-done((bf16[3,96,1536]{2,1,0:T(8,128)(2,1)S(1)}, bf16[3,96,1536]{2,1,0:T(8,128)(2,1)S(1)}, u32[]{:S(2)}, u32[]{:S(2)}) %collective-permute-start.5) | collective-permute-done | bytes 884768 | tf_op jit(solution)/shard_map/ppermute | solution.py:39
  41.7 0.3 fence.4
  42.0 1.9 %collective-permute-start.13 = (bf16[3,96,1536]{2,1,0:T(8,128)(2,1)S(1)}, bf16[3,96,1536]{2,1,0:T(8,128)(2,1)S(1)}, u32[]{:S(2)}, u32[]{:S(2)}) collective-permute-start(bf16[3,96,1536]{2,1,0:T(8,128)(2,1)S(1)} %get-tuple-element.42.refs_2_.refs_11_), channel_id=1, source_target_pairs={{0,1},{1,0},{2,3},{3,2},{4,5},{5,4},{6,7},{7,6},{8,9},{9,8},{10,11... | collective-permute-start | bytes 2654216 | tf_op jit(solution)/shard_map/ppermute | solution.py:25
  43.9 0.1 collective-permute-start.14
  44.0 2.0 %collective-permute-start.11 = (bf16[3,96,1536]{2,1,0:T(8,128)(2,1)S(1)}, bf16[3,96,1536]{2,1,0:T(8,128)(2,1)S(1)}, u32[]{:S(2)}, u32[]{:S(2)}) collective-permute-start(bf16[3,96,1536]{2,1,0:T(8,128)(2,1)S(1)} %get-tuple-element.37.refs_6_), channel_id=1, source_target_pairs={{0,4},{1,13},{4,8},{5,1},{8,12},{9,5},{12,0},{13,9},{2,6},{3,15},{... | collective-permute-start | bytes 2654216 | tf_op jit(solution)/shard_map/ppermute | solution.py:32
  45.9 1.7 %collective-permute-start.12 = (bf16[3,96,1536]{2,1,0:T(8,128)(2,1)S(1)}, bf16[3,96,1536]{2,1,0:T(8,128)(2,1)S(1)}, u32[]{:S(2)}, u32[]{:S(2)}) collective-permute-start(bf16[3,96,1536]{2,1,0:T(8,128)(2,1)S(1)} %get-tuple-element.38.refs_4_.refs_13_), channel_id=1, source_target_pairs={{0,2},{1,131},{2,128},{3,1},{128,130},{129,3},{130,0},{131,129},{4... | collective-permute-start | bytes 2654216 | tf_op jit(solution)/shard_map/ppermute | solution.py:39
  47.7 4.4 %partial_sum.3 = (f32[384,1536]{1,0:T(8,128)S(1)}, f32[256,1536]{1,0:T(8,128)S(1)}, f32[8,128]{1,0:T(8,128)S(1)}) custom-call(bf16[400,384]{1,0:T(8,128)(2,1)S(1)} %get-tuple-element.40.refs_0_, bf16[272,384]{1,0:T(8,128)(2,1)S(1)} %get-tuple-element.41.refs_1_, ...), custom_call_target="tpu_custom_call", output_to_operand_aliasing={{0}: (6, {}), {1}: (7, {})} | custom-call | flops 2264924160 | bytes 3538944 | tf_op jit(solution)/shard_map/partial_sum/pallas_call | solution.py:178
  52.1 0.0 copy-start.2
  52.1 0.0 copy-start.3
  52.1 4.1 %collective-permute-done.11.refs_0_ = bf16[3,96,1536]{2,1,0:T(8,128)(2,1)S(1)} collective-permute-done((bf16[3,96,1536]{2,1,0:T(8,128)(2,1)S(1)}, bf16[3,96,1536]{2,1,0:T(8,128)(2,1)S(1)}, u32[]{:S(2)}, u32[]{:S(2)}) %collective-permute-start.11) | collective-permute-done | bytes 884768 | tf_op jit(solution)/shard_map/ppermute | solution.py:32
  56.2 2.0 %collective-permute-done.12.refs_1_ = bf16[3,96,1536]{2,1,0:T(8,128)(2,1)S(1)} collective-permute-done((bf16[3,96,1536]{2,1,0:T(8,128)(2,1)S(1)}, bf16[3,96,1536]{2,1,0:T(8,128)(2,1)S(1)}, u32[]{:S(2)}, u32[]{:S(2)}) %collective-permute-start.12) | collective-permute-done | bytes 884768 | tf_op jit(solution)/shard_map/ppermute | solution.py:39
  58.1 0.3 fence.5
  58.4 1.4 %collective-permute-start.15 = (bf16[3,96,1536]{2,1,0:T(8,128)(2,1)S(1)}, bf16[3,96,1536]{2,1,0:T(8,128)(2,1)S(1)}, u32[]{:S(2)}, u32[]{:S(2)}) collective-permute-start(bf16[3,96,1536]{2,1,0:T(8,128)(2,1)S(1)} %get-tuple-element.46.refs_0_.refs_15_), channel_id=1, source_target_pairs={{0,1},{1,0},{2,3},{3,2},{4,5},{5,4},{6,7},{7,6},{8,9},{9,8},{10,11... | collective-permute-start | bytes 2654216 | tf_op jit(solution)/shard_map/ppermute | solution.py:25
  59.8 0.1 collective-permute-start.16
  59.9 1.3 %collective-permute-start.18 = (bf16[144,1536]{1,0:T(8,128)(2,1)S(1)}, bf16[144,1536]{1,0:T(8,128)(2,1)S(1)}, u32[]{:S(2)}, u32[]{:S(2)}) collective-permute-start(bf16[144,1536]{1,0:T(8,128)(2,1)S(1)} %get-tuple-element.51), channel_id=1, source_target_pairs={{0,15},{1,14},{2,13},{3,12},{4,11},{5,10},{6,9},{7,8},{8,7},{9,6},... | collective-permute-start | bytes 1327112 | tf_op jit(solution)/shard_map/ppermute | solution.py:329
  61.2 0.6 collective-permute-done.15.refs_1_.refs_16_
  61.8 1.3 %collective-permute-done.16.refs_3_.refs_18_ = bf16[3,96,1536]{2,1,0:T(8,128)(2,1)S(1)} collective-permute-done((bf16[3,96,1536]{2,1,0:T(8,128)(2,1)S(1)}, bf16[3,96,1536]{2,1,0:T(8,128)(2,1)S(1)}, u32[]{:S(2)}, u32[]{:S(2)}) %collective-permute-start.16) | collective-permute-done | bytes 884768 | tf_op jit(solution)/shard_map/ppermute | solution.py:25
  63.1 3.1 %finish.3 = bf16[256,1024]{1,0:T(8,128)(2,1)S(1)} custom-call(bf16[272,384]{1,0:T(8,128)(2,1)S(1)} %get-tuple-element.49.x_ref, bf16[3,96,1536]{2,1,0:T(8,128)(2,1)S(1)} %get-tuple-element.46.refs_0_.refs_15_, bf16[3,96,1536]{2,1,0:T(8,128)(2,1)S(1)} %collective-permute-done.15.refs_1_.refs_16_, bf16[3,96,1536]{2,1,0:T(8,128)(2,1)S(1)} %get-tuple-element.47.refs_2_.refs_17_, ...), custom_call_target="tpu_custom_call" | custom-call | flops 1711276032 | bytes 6684672 | tf_op jit(solution)/shard_map/finish/pallas_call | solution.py:224
  66.3 1.4 %collective-permute-start.17 = (bf16[256,1024]{1,0:T(8,128)(2,1)S(1)}, bf16[256,1024]{1,0:T(8,128)(2,1)S(1)}, u32[]{:S(2)}, u32[]{:S(2)}) collective-permute-start(bf16[256,1024]{1,0:T(8,128)(2,1)S(1)} %finish.3), channel_id=1, source_target_pairs={{0,15},{1,14},{2,13},{3,12},{4,11},{5,10},{6,9},{7,8},{8,7},{9,6},... | collective-permute-start | bytes 1572872 | tf_op jit(solution)/shard_map/ppermute | solution.py:333
  67.7 4.6 %finish.2 = bf16[384,1024]{1,0:T(8,128)(2,1)S(1)} custom-call(bf16[400,384]{1,0:T(8,128)(2,1)S(1)} %get-tuple-element.30.x_ref, bf16[3,96,1536]{2,1,0:T(8,128)(2,1)S(1)} %get-tuple-element.46.refs_0_.refs_15_, bf16[3,96,1536]{2,1,0:T(8,128)(2,1)S(1)} %collective-permute-done.15.refs_1_.refs_16_, bf16[3,96,1536]{2,1,0:T(8,128)(2,1)S(1)} %get-tuple-element.47.refs_2_.refs_17_, ...), custom_call_target="tpu_custom_call" | custom-call | flops 2566914048 | bytes 6684672 | tf_op jit(solution)/shard_map/finish/pallas_call | solution.py:224
  72.3 2.5 %collective-permute-done.18.away_ref = bf16[144,1536]{1,0:T(8,128)(2,1)S(1)} collective-permute-done((bf16[144,1536]{1,0:T(8,128)(2,1)S(1)}, bf16[144,1536]{1,0:T(8,128)(2,1)S(1)}, u32[]{:S(2)}, u32[]{:S(2)}) %collective-permute-start.18) | collective-permute-done | bytes 442400 | tf_op jit(solution)/shard_map/ppermute | solution.py:329
  74.7 4.2 %whole.1 = bf16[128,1024]{1,0:T(8,128)(2,1)S(1)} custom-call(bf16[144,1536]{1,0:T(8,128)(2,1)S(1)} %collective-permute-done.18.away_ref, bf16[1536,768]{1,0:T(8,128)(2,1)S(1)} %get-tuple-element.52.refs_0_, bf16[1536,384]{1,0:T(8,128)(2,1)S(1)} %get-tuple-element.53.refs_1_, bf16[1536,384]{1,0:T(8,128)(2,1)S(1)} %get-tuple-element.54.refs_2_, ...), custom_call_target="tpu_custom_call" | custom-call | flops 2818572288 | bytes 14155776 | tf_op jit(solution)/shard_map/whole/pallas_call | solution.py:262
  79.0 6.5 %collective-permute-done.17 = bf16[256,1024]{1,0:T(8,128)(2,1)S(1)} collective-permute-done((bf16[256,1024]{1,0:T(8,128)(2,1)S(1)}, bf16[256,1024]{1,0:T(8,128)(2,1)S(1)}, u32[]{:S(2)}, u32[]{:S(2)}) %collective-permute-start.17) | collective-permute-done | bytes 524320 | tf_op jit(solution)/shard_map/ppermute | solution.py:333
  85.4 1.2 %multiply_convert_fusion = bf16[384,1024]{1,0:T(8,128)(2,1)} fusion(bf16[384,1024]{1,0:T(8,128)(2,1)S(1)} %finish.2, bf16[128,1024]{1,0:T(8,128)(2,1)S(1)} %whole.1, bf16[256,1024]{1,0:T(8,128)(2,1)S(1)} %collective-permute-done.17), kind=kLoop, calls=%fused_computation | loop fusion | flops 3145728 | bytes 2359296 | tf_op jit(solution)/shard_map/convert_element_type | solution.py:338
  (16 shorter events, 0.0 us)
Async XLA Ops:
  0.0 6.7 %collective-permute-start.7 = (bf16[3,96,1536]{2,1,0:T(8,128)(2,1)}, bf16[3,96,1536]{2,1,0:T(8,128)(2,1)S(1)}, u32[]{:S(2)}, u32[]{:S(2)}) collective-permute-start(bf16[3,96,1536]{2,1,0:T(8,128)(2,1)} %bitcast.18), channel_id=1, source_target_pairs={{0,1},{1,0},{2,3},{3,2},{4,5},{5,4},{6,7},{7,6},{8,9},{9,8},{10,11... | collective-permute-start | bytes 2654216 | tf_op jit(solution)/shard_map/ppermute | solution.py:25
  3.2 23.2 %collective-permute-start.2 = (bf16[3,96,1536]{2,1,0:T(8,128)(2,1)}, bf16[3,96,1536]{2,1,0:T(8,128)(2,1)S(1)}, u32[]{:S(2)}, u32[]{:S(2)}) collective-permute-start(bf16[3,96,1536]{2,1,0:T(8,128)(2,1)} %bitcast.19), channel_id=1, source_target_pairs={{0,4},{1,13},{4,8},{5,1},{8,12},{9,5},{12,0},{13,9},{2,6},{3,15},{... | collective-permute-start | bytes 2654216 | tf_op jit(solution)/shard_map/ppermute | solution.py:32
  4.0 22.4 %collective-permute-start.3 = (bf16[3,96,1536]{2,1,0:T(8,128)(2,1)}, bf16[3,96,1536]{2,1,0:T(8,128)(2,1)S(1)}, u32[]{:S(2)}, u32[]{:S(2)}) collective-permute-start(bf16[3,96,1536]{2,1,0:T(8,128)(2,1)} %bitcast.20), channel_id=1, source_target_pairs={{0,2},{1,131},{2,128},{3,1},{128,130},{129,3},{130,0},{131,129},{4... | collective-permute-start | bytes 2654216 | tf_op jit(solution)/shard_map/ppermute | solution.py:39
  6.7 20.5 %collective-permute-start.9 = (bf16[3,96,1536]{2,1,0:T(8,128)(2,1)S(1)}, bf16[3,96,1536]{2,1,0:T(8,128)(2,1)S(1)}, u32[]{:S(2)}, u32[]{:S(2)}) collective-permute-start(bf16[3,96,1536]{2,1,0:T(8,128)(2,1)S(1)} %collective-permute-done.7.refs_3_.refs_4_), channel_id=1, source_target_pairs={{0,4},{1,13},{4,8},{5,1},{8,12},{9,5},{12,0},{13,9},{2,6},{3,15},{... | collective-permute-start | bytes 2654216 | tf_op jit(solution)/shard_map/ppermute | solution.py:32
  8.7 5.1 %collective-permute-start = (bf16[2,1536]{1,0:T(2,128)(2,1)}, bf16[2,1536]{1,0:T(2,128)(2,1)S(1)}, u32[]{:S(2)}, u32[]{:S(2)}) collective-permute-start(bf16[2,1536]{1,0:T(2,128)(2,1)} %pad_maximum_fusion), channel_id=1, source_target_pairs={{0,1},{1,2},{2,3},{3,4},{4,5},{5,6},{6,7},{7,8},{8,9},{9,10},{10,1... | collective-permute-start | bytes 18440 | tf_op jit(solution)/shard_map/ppermute | solution.py:305
  11.2 5.4 %collective-permute-start.1 = (bf16[2,1536]{1,0:T(2,128)(2,1)}, bf16[2,1536]{1,0:T(2,128)(2,1)}, u32[]{:S(2)}, u32[]{:S(2)}) collective-permute-start(bf16[2,1536]{1,0:T(2,128)(2,1)} %pad_maximum_fusion.1), channel_id=1, source_target_pairs={{1,0},{2,1},{3,2},{4,3},{5,4},{6,5},{7,6},{8,7},{9,8},{10,9},{11,1... | collective-permute-start | bytes 18440 | tf_op jit(solution)/shard_map/ppermute | solution.py:306
  16.7 1.3 %copy-start.4 = (bf16[384,1536]{1,0:T(8,128)(2,1)S(1)}, bf16[384,1536]{1,0:T(8,128)(2,1)}, u32[]{:S(2)}) copy-start(bf16[384,1536]{1,0:T(8,128)(2,1)} %forward_ref.1) | copy-start | bytes 3538948
  17.9 1.3 %copy-start.5 = (bf16[384,1536]{1,0:T(8,128)(2,1)S(1)}, bf16[384,1536]{1,0:T(8,128)(2,1)}, u32[]{:S(2)}) copy-start(bf16[384,1536]{1,0:T(8,128)(2,1)} %reverse_ref.1) | copy-start | bytes 3538948
  26.4 5.3 %copy-start.1 = (bf16[1,3,96,1536]{3,2,1,0:T(8,128)(2,1)S(1)}, bf16[1,3,96,1536]{3,2,1,0:T(8,128)(2,1)}, u32[]{:S(2)}) copy-start(bf16[1,3,96,1536]{3,2,1,0:T(8,128)(2,1)} %param.8) | copy-start | bytes 2654212
  26.7 4.3 %collective-permute-start.6 = (bf16[3,96,1536]{2,1,0:T(8,128)(2,1)S(1)}, bf16[3,96,1536]{2,1,0:T(8,128)(2,1)S(1)}, u32[]{:S(2)}, u32[]{:S(2)}) collective-permute-start(bf16[3,96,1536]{2,1,0:T(8,128)(2,1)S(1)} %get-tuple-element.33.refs_4_.refs_5_), channel_id=1, source_target_pairs={{0,1},{1,0},{2,3},{3,2},{4,5},{5,4},{6,7},{7,6},{8,9},{9,8},{10,11... | collective-permute-start | bytes 2654216 | tf_op jit(solution)/shard_map/ppermute | solution.py:25
  26.8 4.2 %collective-permute-start.8 = (bf16[3,96,1536]{2,1,0:T(8,128)(2,1)S(1)}, bf16[3,96,1536]{2,1,0:T(8,128)(2,1)S(1)}, u32[]{:S(2)}, u32[]{:S(2)}) collective-permute-start(bf16[3,96,1536]{2,1,0:T(8,128)(2,1)S(1)} %get-tuple-element.32.refs_6_.refs_7_), channel_id=1, source_target_pairs={{0,1},{1,0},{2,3},{3,2},{4,5},{5,4},{6,7},{7,6},{8,9},{9,8},{10,11... | collective-permute-start | bytes 2654216 | tf_op jit(solution)/shard_map/ppermute | solution.py:25
  27.3 4.4 %collective-permute-start.10 = (bf16[3,96,1536]{2,1,0:T(8,128)(2,1)S(1)}, bf16[3,96,1536]{2,1,0:T(8,128)(2,1)S(1)}, u32[]{:S(2)}, u32[]{:S(2)}) collective-permute-start(bf16[3,96,1536]{2,1,0:T(8,128)(2,1)S(1)} %collective-permute-done.9.refs_8_.refs_9_), channel_id=1, source_target_pairs={{0,1},{1,0},{2,3},{3,2},{4,5},{5,4},{6,7},{7,6},{8,9},{9,8},{10,11... | collective-permute-start | bytes 2654216 | tf_op jit(solution)/shard_map/ppermute | solution.py:25
  27.4 12.2 %collective-permute-start.4 = (bf16[3,96,1536]{2,1,0:T(8,128)(2,1)S(1)}, bf16[3,96,1536]{2,1,0:T(8,128)(2,1)S(1)}, u32[]{:S(2)}, u32[]{:S(2)}) collective-permute-start(bf16[3,96,1536]{2,1,0:T(8,128)(2,1)S(1)} %get-tuple-element.32.refs_6_.refs_7_), channel_id=1, source_target_pairs={{0,4},{1,13},{4,8},{5,1},{8,12},{9,5},{12,0},{13,9},{2,6},{3,15},{... | collective-permute-start | bytes 2654216 | tf_op jit(solution)/shard_map/ppermute | solution.py:32
  29.5 12.2 %collective-permute-start.5 = (bf16[3,96,1536]{2,1,0:T(8,128)(2,1)S(1)}, bf16[3,96,1536]{2,1,0:T(8,128)(2,1)S(1)}, u32[]{:S(2)}, u32[]{:S(2)}) collective-permute-start(bf16[3,96,1536]{2,1,0:T(8,128)(2,1)S(1)} %get-tuple-element.32.refs_6_.refs_7_), channel_id=1, source_target_pairs={{0,2},{1,131},{2,128},{3,1},{128,130},{129,3},{130,0},{131,129},{4... | collective-permute-start | bytes 2654216 | tf_op jit(solution)/shard_map/ppermute | solution.py:39
  42.0 5.7 %collective-permute-start.13 = (bf16[3,96,1536]{2,1,0:T(8,128)(2,1)S(1)}, bf16[3,96,1536]{2,1,0:T(8,128)(2,1)S(1)}, u32[]{:S(2)}, u32[]{:S(2)}) collective-permute-start(bf16[3,96,1536]{2,1,0:T(8,128)(2,1)S(1)} %get-tuple-element.42.refs_2_.refs_11_), channel_id=1, source_target_pairs={{0,1},{1,0},{2,3},{3,2},{4,5},{5,4},{6,7},{7,6},{8,9},{9,8},{10,11... | collective-permute-start | bytes 2654216 | tf_op jit(solution)/shard_map/ppermute | solution.py:25
  43.9 3.8 %collective-permute-start.14 = (bf16[3,96,1536]{2,1,0:T(8,128)(2,1)S(1)}, bf16[3,96,1536]{2,1,0:T(8,128)(2,1)S(1)}, u32[]{:S(2)}, u32[]{:S(2)}) collective-permute-start(bf16[3,96,1536]{2,1,0:T(8,128)(2,1)S(1)} %get-tuple-element.38.refs_4_.refs_13_), channel_id=1, source_target_pairs={{0,1},{1,0},{2,3},{3,2},{4,5},{5,4},{6,7},{7,6},{8,9},{9,8},{10,11... | collective-permute-start | bytes 2654216 | tf_op jit(solution)/shard_map/ppermute | solution.py:25
  44.0 12.2 %collective-permute-start.11 = (bf16[3,96,1536]{2,1,0:T(8,128)(2,1)S(1)}, bf16[3,96,1536]{2,1,0:T(8,128)(2,1)S(1)}, u32[]{:S(2)}, u32[]{:S(2)}) collective-permute-start(bf16[3,96,1536]{2,1,0:T(8,128)(2,1)S(1)} %get-tuple-element.37.refs_6_), channel_id=1, source_target_pairs={{0,4},{1,13},{4,8},{5,1},{8,12},{9,5},{12,0},{13,9},{2,6},{3,15},{... | collective-permute-start | bytes 2654216 | tf_op jit(solution)/shard_map/ppermute | solution.py:32
  45.9 12.2 %collective-permute-start.12 = (bf16[3,96,1536]{2,1,0:T(8,128)(2,1)S(1)}, bf16[3,96,1536]{2,1,0:T(8,128)(2,1)S(1)}, u32[]{:S(2)}, u32[]{:S(2)}) collective-permute-start(bf16[3,96,1536]{2,1,0:T(8,128)(2,1)S(1)} %get-tuple-element.38.refs_4_.refs_13_), channel_id=1, source_target_pairs={{0,2},{1,131},{2,128},{3,1},{128,130},{129,3},{130,0},{131,129},{4... | collective-permute-start | bytes 2654216 | tf_op jit(solution)/shard_map/ppermute | solution.py:39
  47.7 15.4 %copy-start = (bf16[1536,1024]{1,0:T(8,128)(2,1)S(1)}, bf16[1536,1024]{1,0:T(8,128)(2,1)}, u32[]{:S(2)}) copy-start(bf16[1536,1024]{1,0:T(8,128)(2,1)} %refs_20_.1) | copy-start | bytes 9437188
  52.1 11.0 %copy-start.2 = (f32[1,1536]{1,0:T(1,128)S(1)}, f32[1,1536]{1,0:T(1,128)}, u32[]{:S(2)}) copy-start(f32[1,1536]{1,0:T(1,128)} %refs_19_.1) | copy-start | bytes 18436
  52.1 11.0 %copy-start.3 = (f32[1024]{0:T(1024)S(1)}, f32[1024]{0:T(1024)}, u32[]{:S(2)}) copy-start(f32[1024]{0:T(1024)} %param.11) | copy-start | bytes 12292
  58.4 3.4 %collective-permute-start.15 = (bf16[3,96,1536]{2,1,0:T(8,128)(2,1)S(1)}, bf16[3,96,1536]{2,1,0:T(8,128)(2,1)S(1)}, u32[]{:S(2)}, u32[]{:S(2)}) collective-permute-start(bf16[3,96,1536]{2,1,0:T(8,128)(2,1)S(1)} %get-tuple-element.46.refs_0_.refs_15_), channel_id=1, source_target_pairs={{0,1},{1,0},{2,3},{3,2},{4,5},{5,4},{6,7},{7,6},{8,9},{9,8},{10,11... | collective-permute-start | bytes 2654216 | tf_op jit(solution)/shard_map/ppermute | solution.py:25
  59.8 3.3 %collective-permute-start.16 = (bf16[3,96,1536]{2,1,0:T(8,128)(2,1)S(1)}, bf16[3,96,1536]{2,1,0:T(8,128)(2,1)S(1)}, u32[]{:S(2)}, u32[]{:S(2)}) collective-permute-start(bf16[3,96,1536]{2,1,0:T(8,128)(2,1)S(1)} %get-tuple-element.47.refs_2_.refs_17_), channel_id=1, source_target_pairs={{0,1},{1,0},{2,3},{3,2},{4,5},{5,4},{6,7},{7,6},{8,9},{9,8},{10,11... | collective-permute-start | bytes 2654216 | tf_op jit(solution)/shard_map/ppermute | solution.py:25
  59.9 14.9 %collective-permute-start.18 = (bf16[144,1536]{1,0:T(8,128)(2,1)S(1)}, bf16[144,1536]{1,0:T(8,128)(2,1)S(1)}, u32[]{:S(2)}, u32[]{:S(2)}) collective-permute-start(bf16[144,1536]{1,0:T(8,128)(2,1)S(1)} %get-tuple-element.51), channel_id=1, source_target_pairs={{0,15},{1,14},{2,13},{3,12},{4,11},{5,10},{6,9},{7,8},{8,7},{9,6},... | collective-permute-start | bytes 1327112 | tf_op jit(solution)/shard_map/ppermute | solution.py:329
  66.3 19.2 %collective-permute-start.17 = (bf16[256,1024]{1,0:T(8,128)(2,1)S(1)}, bf16[256,1024]{1,0:T(8,128)(2,1)S(1)}, u32[]{:S(2)}, u32[]{:S(2)}) collective-permute-start(bf16[256,1024]{1,0:T(8,128)(2,1)S(1)} %finish.3), channel_id=1, source_target_pairs={{0,15},{1,14},{2,13},{3,12},{4,11},{5,10},{6,9},{7,8},{8,7},{9,6},... | collective-permute-start | bytes 1572872 | tf_op jit(solution)/shard_map/ppermute | solution.py:333

commit v7 on v6

--- a/solution.py
+++ b/solution.py
@@ -14,7 +14,7 @@
 VMEM_LIMIT = 24 * 1024 * 1024
 EDGE = 16
 TILE = 512
-PARTS = (8, 4, 4)
+PARTS = (8, 6, 2)
 ROWS = 128
 AWAY = 128
 TOKEN = jax.ShapeDtypeStruct((8, 128), jnp.float32)
@@ -304,30 +304,33 @@
     down = [(b, a) for a, b in up]
     low = lax.ppermute(jnp.stack([forward_embed[-1], reverse_embed[-1]]), SEQ, up)
     high = lax.ppermute(jnp.stack([forward_embed[0], reverse_embed[0]]), SEQ, down)
-    (x_1, x_2, x_3), moves, away, token = prepare(place, forward_embed, reverse_embed, low, high)
-    near, across = fence(token, near, across)
+    near, across, low, high = fence(None, near, across, low, high)
 
     distant = x_shift(near)
     near_over = y_shift(near)
     across_b = core_swap(across)
     near_b = core_swap(near)
+    across_b, low, high = fence(None, across_b, low, high)
+
+    second_over = x_shift(across_b)
     second_b = core_swap(second)
+    (x_1, x_2, x_3), moves, away, token = prepare(place, forward_embed, reverse_embed, low, high)
     shards_1 = [own, sibling, across, across_b, near, near_b, second, second_b]
     acc, token = partial_sum(x_1, shards_1, None)
-    distant, near_over, across_b = fence(token, distant, near_over, across_b)
-    shards_1[3] = across_b
-
-    second_over = x_shift(across_b)
+    (distant,) = fence(token, distant)
+
     distant_over = y_shift(distant)
     near_over_b = core_swap(near_over)
     distant_b = core_swap(distant)
-    shards_2 = [near_over, near_over_b, distant, distant_b]
+    second_over_b = core_swap(second_over)
+    shards_2 = [near_over, near_over_b, distant, distant_b, second_over, second_over_b]
     acc, token = partial_sum(x_2, shards_2, acc)
-    second_over, distant_over, away = fence(token, second_over, distant_over, away)
+    (away,) = fence(token, away)
+    (distant_over,) = fence(token, distant_over)
 
     mirror = [(i, ends - 1 - i) for i in range(ends)]
     away = lax.ppermute(away, SEQ, mirror)
-    shards_3 = [second_over, core_swap(second_over), distant_over, core_swap(distant_over)]
+    shards_3 = [distant_over, core_swap(distant_over)]
     rest = (conv_bias, head_weight, head_bias)
     reverse_tracks = finish(True, x_3[1], shards_3, acc[1], *rest)
     mirrored = lax.ppermute(reverse_tracks, SEQ, mirror)

time: 86.9 us -> 94.2 us (1.084)
  Pallas kernels: 29.4 us -> 34.8 us
  starting transfers between devices: 25.8 us -> 28.4 us
  local copies, waits for them, and re-layouts: 3.47 us -> 4.66 us
  other arithmetic: 2.39 us -> 1.21 us
    pallas_call x2, Pallas kernels: 9.42 us -> 14.1 us  [partial_sum(): pl.pallas_call(functools.partial(partial_kernel, len(sources), prev is No...]
    ppermute x4, starting transfers between devices: 5.34 us -> 8.2 us  [x_shift(): return lax.ppermute(value, ('x', 'core'), route)]
    ppermute x1, waiting for transfers between devices: 6.46 us -> 3.84 us  [per_device(): mirrored = lax.ppermute(reverse_tracks, SEQ, mirror)]
    ppermute x3, starting transfers between devices: 5.94 us -> 3.56 us  [y_shift(): return lax.ppermute(value, ('y_hi', 'y_lo', 'core'), route)]
    pallas_call x1, Pallas kernels: 4.21 us -> 6.47 us  [whole(): pl.pallas_call(functools.partial(whole_kernel, PARTS), out_shape=jax.Shap...]
    ppermute x4, waiting for transfers between devices: 6.87 us -> 8.8 us  [x_shift(): return lax.ppermute(value, ('x', 'core'), route)]
    ppermute x8, starting transfers between devices: 7.43 us -> 9.14 us  [core_swap(): return lax.ppermute(value, 'core', [(0, 1), (1, 0)])]
    ppermute x1, waiting for transfers between devices: 2.46 us -> 4.15 us  [per_device(): away = lax.ppermute(away, SEQ, mirror)]
  transfers between devices with their start and end apart: 19 -> 19, of which waited for: 10 -> 9; matrix products, arithmetic and copies ran while one was open for 2% -> 2% of each run, Pallas kernels for 33% -> 37%
where the time goes in v7:
time: 94.2 us; the launch traced here: 93.9 us
  Pallas kernels  34.8 us (37%)
  starting transfers between devices  28.4 us (30%)
  waiting for transfers between devices  24.7 us (26%)
  local copies, waits for them, and re-layouts  4.66 us (5%)
  other arithmetic  1.21 us (1%)
    pallas_call x2, Pallas kernels, partial_sum(): pl.pallas_call(functools.partial(partial_kernel, len(sources), prev is No...  14.1 us
    ppermute x8, starting transfers between devices, core_swap(): return lax.ppermute(value, 'core', [(0, 1), (1, 0)])  9.14 us
    ppermute x4, waiting for transfers between devices, x_shift(): return lax.ppermute(value, ('x', 'core'), route)  8.8 us
    ppermute x4, starting transfers between devices, x_shift(): return lax.ppermute(value, ('x', 'core'), route)  8.2 us
    pallas_call x1, Pallas kernels, prepare(): pl.pallas_call(prepare_kernel, out_shape=stripes(rows + EDGE) + stripes(k...  7.1 us
    pallas_call x1, Pallas kernels, whole(): pl.pallas_call(functools.partial(whole_kernel, PARTS), out_shape=jax.Shap...  6.47 us
    pallas_call x2, Pallas kernels, finish(): pl.pallas_call(functools.partial(finish_kernel, flipped, len(sources)), o...  6.43 us
    ppermute x1, waiting for transfers between devices, per_device(): away = lax.ppermute(away, SEQ, mirror)  4.15 us
  transfers between devices with their start and end apart: 19, of which 9 were waited for; matrix products, arithmetic and copies ran while one was open for 2% of the time, Pallas kernels for 37%

profile of v7, /device:TPU:1, one launch (start us, length us, event | category | flops | bytes accessed | tf_op | source)
XLA Modules:
  0.0 93.9 jit_solution(12300524663504198281)
XLA Ops:
  0.0 3.2 %collective-permute-start.6 = (bf16[3,96,1536]{2,1,0:T(8,128)(2,1)}, bf16[3,96,1536]{2,1,0:T(8,128)(2,1)S(1)}, u32[]{:S(2)}, u32[]{:S(2)}) collective-permute-start(bf16[3,96,1536]{2,1,0:T(8,128)(2,1)} %bitcast.18), channel_id=1, source_target_pairs={{0,1},{1,0},{2,3},{3,2},{4,5},{5,4},{6,7},{7,6},{8,9},{9,8},{10,11... | collective-permute-start | bytes 2654216 | tf_op jit(solution)/shard_map/ppermute | solution.py:25
  3.2 1.0 %collective-permute-start.1 = (bf16[3,96,1536]{2,1,0:T(8,128)(2,1)}, bf16[3,96,1536]{2,1,0:T(8,128)(2,1)S(1)}, u32[]{:S(2)}, u32[]{:S(2)}) collective-permute-start(bf16[3,96,1536]{2,1,0:T(8,128)(2,1)} %bitcast.19), channel_id=1, source_target_pairs={{0,2},{1,131},{2,128},{3,1},{128,130},{129,3},{130,0},{131,129},{4... | collective-permute-start | bytes 2654216 | tf_op jit(solution)/shard_map/ppermute | solution.py:39
  4.2 2.5 %collective-permute-start = (bf16[3,96,1536]{2,1,0:T(8,128)(2,1)}, bf16[3,96,1536]{2,1,0:T(8,128)(2,1)S(1)}, u32[]{:S(2)}, u32[]{:S(2)}) collective-permute-start(bf16[3,96,1536]{2,1,0:T(8,128)(2,1)} %bitcast.20), channel_id=1, source_target_pairs={{0,4},{1,13},{4,8},{5,1},{8,12},{9,5},{12,0},{13,9},{2,6},{3,15},{... | collective-permute-start | bytes 2654216 | tf_op jit(solution)/shard_map/ppermute | solution.py:32
  6.7 0.8 fusion
  7.6 1.9 %collective-permute-start.2 = (bf16[2,1536]{1,0:T(2,128)(2,1)S(1)}, bf16[2,1536]{1,0:T(2,128)(2,1)S(1)}, u32[]{:S(2)}, u32[]{:S(2)}) collective-permute-start(bf16[2,1536]{1,0:T(2,128)(2,1)S(1)} %pad_maximum_fusion), channel_id=1, source_target_pairs={{0,1},{1,2},{2,3},{3,4},{4,5},{5,6},{6,7},{7,8},{8,9},{9,10},{10,1... | collective-permute-start | bytes 18440 | tf_op jit(solution)/shard_map/ppermute | solution.py:305
  9.5 2.4 %collective-permute-start.3 = (bf16[2,1536]{1,0:T(2,128)(2,1)S(1)}, bf16[2,1536]{1,0:T(2,128)(2,1)S(1)}, u32[]{:S(2)}, u32[]{:S(2)}) collective-permute-start(bf16[2,1536]{1,0:T(2,128)(2,1)S(1)} %pad_maximum_fusion.1), channel_id=1, source_target_pairs={{1,0},{2,1},{3,2},{4,3},{5,4},{6,5},{7,6},{8,7},{9,8},{10,9},{11,1... | collective-permute-start | bytes 18440 | tf_op jit(solution)/shard_map/ppermute | solution.py:306
  11.9 0.0 collective-permute-done.2.refs_2_
  11.9 3.0 %collective-permute-done.3.refs_3_ = bf16[2,1536]{1,0:T(2,128)(2,1)S(1)} collective-permute-done((bf16[2,1536]{1,0:T(2,128)(2,1)S(1)}, bf16[2,1536]{1,0:T(2,128)(2,1)S(1)}, u32[]{:S(2)}, u32[]{:S(2)}) %collective-permute-start.3) | collective-permute-done | bytes 6176 | tf_op jit(solution)/shard_map/ppermute | solution.py:306
  14.9 0.8 collective-permute-done.1.refs_1_
  15.7 1.3 %collective-permute-done.refs_0_ = bf16[3,96,1536]{2,1,0:T(8,128)(2,1)S(1)} collective-permute-done((bf16[3,96,1536]{2,1,0:T(8,128)(2,1)}, bf16[3,96,1536]{2,1,0:T(8,128)(2,1)S(1)}, u32[]{:S(2)}, u32[]{:S(2)}) %collective-permute-start) | collective-permute-done | bytes 884768 | tf_op jit(solution)/shard_map/ppermute | solution.py:32
  17.0 0.2 fence.5
  17.2 0.8 collective-permute-start.4
  18.0 2.4 %collective-permute-start.8 = (bf16[3,96,1536]{2,1,0:T(8,128)(2,1)S(1)}, bf16[3,96,1536]{2,1,0:T(8,128)(2,1)}, u32[]{:S(2)}, u32[]{:S(2)}) collective-permute-start(bf16[3,96,1536]{2,1,0:T(8,128)(2,1)S(1)} %collective-permute-done.6.refs_3_.refs_4_), channel_id=1, source_target_pairs={{0,4},{1,13},{4,8},{5,1},{8,12},{9,5},{12,0},{13,9},{2,6},{3,15},{... | collective-permute-start | bytes 2654216 | tf_op jit(solution)/shard_map/ppermute | solution.py:32
  20.5 0.6 collective-permute-start.11
  21.1 0.0 collective-permute-done.4.refs_0_
  21.1 0.1 fence.6
  21.2 1.8 %collective-permute-start.14 = (bf16[3,96,1536]{2,1,0:T(8,128)(2,1)S(1)}, bf16[3,96,1536]{2,1,0:T(8,128)(2,1)}, u32[]{:S(2)}, u32[]{:S(2)}) collective-permute-start(bf16[3,96,1536]{2,1,0:T(8,128)(2,1)S(1)} %get-tuple-element.37.refs_5_.refs_6_), channel_id=1, source_target_pairs={{0,4},{1,13},{4,8},{5,1},{8,12},{9,5},{12,0},{13,9},{2,6},{3,15},{... | collective-permute-start | bytes 2654216 | tf_op jit(solution)/shard_map/ppermute | solution.py:32
  23.0 7.5 %collective-permute-done.8.refs_8_.refs_9_ = bf16[3,96,1536]{2,1,0:T(8,128)(2,1)} collective-permute-done((bf16[3,96,1536]{2,1,0:T(8,128)(2,1)S(1)}, bf16[3,96,1536]{2,1,0:T(8,128)(2,1)}, u32[]{:S(2)}, u32[]{:S(2)}) %collective-permute-start.8) | collective-permute-done | bytes 884768 | tf_op jit(solution)/shard_map/ppermute | solution.py:32
  30.4 2.0 %collective-permute-start.9 = (bf16[3,96,1536]{2,1,0:T(8,128)(2,1)}, bf16[3,96,1536]{2,1,0:T(8,128)(2,1)}, u32[]{:S(2)}, u32[]{:S(2)}) collective-permute-start(bf16[3,96,1536]{2,1,0:T(8,128)(2,1)} %collective-permute-done.8.refs_8_.refs_9_), channel_id=1, source_target_pairs={{0,1},{1,0},{2,3},{3,2},{4,5},{5,4},{6,7},{7,6},{8,9},{9,8},{10,11... | collective-permute-start | bytes 2654216 | tf_op jit(solution)/shard_map/ppermute | solution.py:25
  32.5 1.5 %collective-permute-start.5 = (bf16[3,96,1536]{2,1,0:T(8,128)(2,1)S(1)}, bf16[3,96,1536]{2,1,0:T(8,128)(2,1)S(1)}, u32[]{:S(2)}, u32[]{:S(2)}) collective-permute-start(bf16[3,96,1536]{2,1,0:T(8,128)(2,1)S(1)} %get-tuple-element.34.refs_6_.refs_7_), channel_id=1, source_target_pairs={{0,4},{1,13},{4,8},{5,1},{8,12},{9,5},{12,0},{13,9},{2,6},{3,15},{... | collective-permute-start | bytes 2654216 | tf_op jit(solution)/shard_map/ppermute | solution.py:32
  34.0 0.6 stack.73.place_ref
  34.7 0.0 collective-permute-start.12
  34.7 0.6 copy-done.6
  35.3 1.3 %copy-done.7 = bf16[384,1536]{1,0:T(8,128)(2,1)S(1)} copy-done((bf16[384,1536]{1,0:T(8,128)(2,1)S(1)}, bf16[384,1536]{1,0:T(8,128)(2,1)}, u32[]{:S(2)}) %copy-start.7) | copy-done | bytes 1179672
  36.6 1.3 %copy-done.8 = bf16[384,1536]{1,0:T(8,128)(2,1)S(1)} copy-done((bf16[384,1536]{1,0:T(8,128)(2,1)S(1)}, bf16[384,1536]{1,0:T(8,128)(2,1)}, u32[]{:S(2)}) %copy-start.8) | copy-done | bytes 1179672
  37.9 7.1 %prepare.1 = (bf16[400,768]{1,0:T(8,128)(2,1)S(1)}, bf16[400,576]{1,0:T(8,128)(2,1)S(1)}, bf16[400,192]{1,0:T(8,128)(2,1)S(1)}, bf16[272,768]{1,0:T(8,128)(2,1)S...) custom-call(s32[16]{0:T(128)S(1)} %copy-done.6, ...), custom_call_target="tpu_custom_call" | custom-call | flops 3623878656 | bytes 4718592 | tf_op jit(solution)/shard_map/prepare/pallas_call | solution.py:119
  45.0 0.6 collective-permute-start.15
  45.6 6.7 %partial_sum.2 = (f32[384,1536]{1,0:T(8,128)S(1)}, f32[256,1536]{1,0:T(8,128)S(1)}, f32[8,128]{1,0:T(8,128)S(1)}) custom-call(bf16[400,768]{1,0:T(8,128)(2,1)S(1)} %get-tuple-element.35.refs_0_, bf16[272,768]{1,0:T(8,128)(2,1)S(1)} %get-tuple-element.36.refs_1_, bf16[3,96,1536]{2,1,0:T(8,128)(2,1)S(1)} %bitcast.21, bf16[3,96,1536]{2,1,0:T(8,128)(2,1)S(1)} %copy-done.3, ...), custom_call_target="tpu_custom_call" | custom-call | flops 4529848320 | bytes 7077888 | tf_op jit(solution)/shard_map/partial_sum/pallas_call | solution.py:178
  52.3 0.1 fence.7.refs_4_.refs_13_
  52.4 0.1 collective-permute-start.13
  52.5 2.0 %collective-permute-start.10 = (bf16[3,96,1536]{2,1,0:T(8,128)(2,1)S(1)}, bf16[3,96,1536]{2,1,0:T(8,128)(2,1)S(1)}, u32[]{:S(2)}, u32[]{:S(2)}) collective-permute-start(bf16[3,96,1536]{2,1,0:T(8,128)(2,1)S(1)} %fence.7.refs_4_.refs_13_), channel_id=1, source_target_pairs={{0,2},{1,131},{2,128},{3,1},{128,130},{129,3},{130,0},{131,129},{4... | collective-permute-start | bytes 2654216 | tf_op jit(solution)/shard_map/ppermute | solution.py:39
  54.5 0.4 collective-permute-done.13.refs_5_.refs_14_
  54.9 7.4 %partial_sum.3 = (f32[384,1536]{1,0:T(8,128)S(1)}, f32[256,1536]{1,0:T(8,128)S(1)}, f32[8,128]{1,0:T(8,128)S(1)}) custom-call(bf16[400,576]{1,0:T(8,128)(2,1)S(1)} %get-tuple-element.39.refs_0_, bf16[272,576]{1,0:T(8,128)(2,1)S(1)} %get-tuple-element.40.refs_1_, ...), custom_call_target="tpu_custom_call", output_to_operand_aliasing={{0}: (8, {}), {1}: (9, {})} | custom-call | flops 3397386240 | bytes 5308416 | tf_op jit(solution)/shard_map/partial_sum/pallas_call | solution.py:178
  62.4 0.0 copy-start.4
  62.4 0.0 copy-start.5
  62.4 2.6 %collective-permute-done.10.refs_0_ = bf16[3,96,1536]{2,1,0:T(8,128)(2,1)S(1)} collective-permute-done((bf16[3,96,1536]{2,1,0:T(8,128)(2,1)S(1)}, bf16[3,96,1536]{2,1,0:T(8,128)(2,1)S(1)}, u32[]{:S(2)}, u32[]{:S(2)}) %collective-permute-start.10) | collective-permute-done | bytes 884768 | tf_op jit(solution)/shard_map/ppermute | solution.py:39
  65.0 0.1 fence.8.refs_0_.refs_17_
  65.1 2.4 %collective-permute-start.16 = (bf16[3,96,1536]{2,1,0:T(8,128)(2,1)S(1)}, bf16[3,96,1536]{2,1,0:T(8,128)(2,1)S(1)}, u32[]{:S(2)}, u32[]{:S(2)}) collective-permute-start(bf16[3,96,1536]{2,1,0:T(8,128)(2,1)S(1)} %fence.8.refs_0_.refs_17_), channel_id=1, source_target_pairs={{0,1},{1,0},{2,3},{3,2},{4,5},{5,4},{6,7},{7,6},{8,9},{9,8},{10,11... | collective-permute-start | bytes 2654216 | tf_op jit(solution)/shard_map/ppermute | solution.py:25
  67.5 0.1 fence.9
  67.5 0.9 collective-permute-start.18
  68.4 1.1 %collective-permute-done.16.refs_1_.refs_18_ = bf16[3,96,1536]{2,1,0:T(8,128)(2,1)S(1)} collective-permute-done((bf16[3,96,1536]{2,1,0:T(8,128)(2,1)S(1)}, bf16[3,96,1536]{2,1,0:T(8,128)(2,1)S(1)}, u32[]{:S(2)}, u32[]{:S(2)}) %collective-permute-start.16) | collective-permute-done | bytes 884768 | tf_op jit(solution)/shard_map/ppermute | solution.py:25
  69.5 2.6 %finish.3 = bf16[256,1024]{1,0:T(8,128)(2,1)S(1)} custom-call(bf16[272,192]{1,0:T(8,128)(2,1)S(1)} %get-tuple-element.45.x_ref, bf16[3,96,1536]{2,1,0:T(8,128)(2,1)S(1)} %fence.8.refs_0_.refs_17_, bf16[3,96,1536]{2,1,0:T(8,128)(2,1)S(1)} %collective-permute-done.16.refs_1_.refs_18_, f32[256,1536]{1,0:T(8,128)S(1)} %get-tuple-element.46.refs_2_, ...), custom_call_target="tpu_custom_call" | custom-call | flops 1258291200 | bytes 4915200 | tf_op jit(solution)/shard_map/finish/pallas_call | solution.py:224
  72.1 2.3 %collective-permute-start.17 = (bf16[256,1024]{1,0:T(8,128)(2,1)S(1)}, bf16[256,1024]{1,0:T(8,128)(2,1)S(1)}, u32[]{:S(2)}, u32[]{:S(2)}) collective-permute-start(bf16[256,1024]{1,0:T(8,128)(2,1)S(1)} %finish.3), channel_id=1, source_target_pairs={{0,15},{1,14},{2,13},{3,12},{4,11},{5,10},{6,9},{7,8},{8,7},{9,6},... | collective-permute-start | bytes 1572872 | tf_op jit(solution)/shard_map/ppermute | solution.py:336
  74.4 3.8 %finish.2 = bf16[384,1024]{1,0:T(8,128)(2,1)S(1)} custom-call(bf16[400,192]{1,0:T(8,128)(2,1)S(1)} %get-tuple-element.33.x_ref, bf16[3,96,1536]{2,1,0:T(8,128)(2,1)S(1)} %fence.8.refs_0_.refs_17_, bf16[3,96,1536]{2,1,0:T(8,128)(2,1)S(1)} %collective-permute-done.16.refs_1_.refs_18_, f32[384,1536]{1,0:T(8,128)S(1)} %get-tuple-element.44.refs_2_, ...), custom_call_target="tpu_custom_call" | custom-call | flops 1887436800 | bytes 4915200 | tf_op jit(solution)/shard_map/finish/pallas_call | solution.py:224
  78.3 4.2 %collective-permute-done.18.away_ref = bf16[144,1536]{1,0:T(8,128)(2,1)S(1)} collective-permute-done((bf16[144,1536]{1,0:T(8,128)(2,1)S(1)}, bf16[144,1536]{1,0:T(8,128)(2,1)S(1)}, u32[]{:S(2)}, u32[]{:S(2)}) %collective-permute-start.18) | collective-permute-done | bytes 442400 | tf_op jit(solution)/shard_map/ppermute | solution.py:332
  82.5 6.5 %whole.1 = bf16[128,1024]{1,0:T(8,128)(2,1)S(1)} custom-call(bf16[144,1536]{1,0:T(8,128)(2,1)S(1)} %collective-permute-done.18.away_ref, bf16[1536,768]{1,0:T(8,128)(2,1)S(1)} %get-tuple-element.48.refs_0_, bf16[1536,576]{1,0:T(8,128)(2,1)S(1)} %get-tuple-element.49.refs_1_, bf16[1536,192]{1,0:T(8,128)(2,1)S(1)} %get-tuple-element.50.refs_2_, ...), custom_call_target="tpu_custom_call" | custom-call | flops 2818572288 | bytes 14155776 | tf_op jit(solution)/shard_map/whole/pallas_call | solution.py:262
  88.9 3.8 %collective-permute-done.17 = bf16[256,1024]{1,0:T(8,128)(2,1)S(1)} collective-permute-done((bf16[256,1024]{1,0:T(8,128)(2,1)S(1)}, bf16[256,1024]{1,0:T(8,128)(2,1)S(1)}, u32[]{:S(2)}, u32[]{:S(2)}) %collective-permute-start.17) | collective-permute-done | bytes 524320 | tf_op jit(solution)/shard_map/ppermute | solution.py:336
  92.8 1.2 %multiply_convert_fusion = bf16[384,1024]{1,0:T(8,128)(2,1)} fusion(bf16[384,1024]{1,0:T(8,128)(2,1)S(1)} %finish.2, bf16[128,1024]{1,0:T(8,128)(2,1)S(1)} %whole.1, bf16[256,1024]{1,0:T(8,128)(2,1)S(1)} %collective-permute-done.17), kind=kLoop, calls=%fused_computation | loop fusion | flops 3145728 | bytes 2359296 | tf_op jit(solution)/shard_map/convert_element_type | solution.py:341
  (24 shorter events, 0.1 us)
Async XLA Ops:
  0.0 18.0 %collective-permute-start.6 = (bf16[3,96,1536]{2,1,0:T(8,128)(2,1)}, bf16[3,96,1536]{2,1,0:T(8,128)(2,1)S(1)}, u32[]{:S(2)}, u32[]{:S(2)}) collective-permute-start(bf16[3,96,1536]{2,1,0:T(8,128)(2,1)} %bitcast.18), channel_id=1, source_target_pairs={{0,1},{1,0},{2,3},{3,2},{4,5},{5,4},{6,7},{7,6},{8,9},{9,8},{10,11... | collective-permute-start | bytes 2654216 | tf_op jit(solution)/shard_map/ppermute | solution.py:25
  3.2 12.5 %collective-permute-start.1 = (bf16[3,96,1536]{2,1,0:T(8,128)(2,1)}, bf16[3,96,1536]{2,1,0:T(8,128)(2,1)S(1)}, u32[]{:S(2)}, u32[]{:S(2)}) collective-permute-start(bf16[3,96,1536]{2,1,0:T(8,128)(2,1)} %bitcast.19), channel_id=1, source_target_pairs={{0,2},{1,131},{2,128},{3,1},{128,130},{129,3},{130,0},{131,129},{4... | collective-permute-start | bytes 2654216 | tf_op jit(solution)/shard_map/ppermute | solution.py:39
  4.2 12.8 %collective-permute-start = (bf16[3,96,1536]{2,1,0:T(8,128)(2,1)}, bf16[3,96,1536]{2,1,0:T(8,128)(2,1)S(1)}, u32[]{:S(2)}, u32[]{:S(2)}) collective-permute-start(bf16[3,96,1536]{2,1,0:T(8,128)(2,1)} %bitcast.20), channel_id=1, source_target_pairs={{0,4},{1,13},{4,8},{5,1},{8,12},{9,5},{12,0},{13,9},{2,6},{3,15},{... | collective-permute-start | bytes 2654216 | tf_op jit(solution)/shard_map/ppermute | solution.py:32
  7.6 4.4 %collective-permute-start.2 = (bf16[2,1536]{1,0:T(2,128)(2,1)S(1)}, bf16[2,1536]{1,0:T(2,128)(2,1)S(1)}, u32[]{:S(2)}, u32[]{:S(2)}) collective-permute-start(bf16[2,1536]{1,0:T(2,128)(2,1)S(1)} %pad_maximum_fusion), channel_id=1, source_target_pairs={{0,1},{1,2},{2,3},{3,4},{4,5},{5,6},{6,7},{7,8},{8,9},{9,10},{10,1... | collective-permute-start | bytes 18440 | tf_op jit(solution)/shard_map/ppermute | solution.py:305
  9.5 5.4 %collective-permute-start.3 = (bf16[2,1536]{1,0:T(2,128)(2,1)S(1)}, bf16[2,1536]{1,0:T(2,128)(2,1)S(1)}, u32[]{:S(2)}, u32[]{:S(2)}) collective-permute-start(bf16[2,1536]{1,0:T(2,128)(2,1)S(1)} %pad_maximum_fusion.1), channel_id=1, source_target_pairs={{1,0},{2,1},{3,2},{4,3},{5,4},{6,5},{7,6},{8,7},{9,8},{10,9},{11,1... | collective-permute-start | bytes 18440 | tf_op jit(solution)/shard_map/ppermute | solution.py:306
  17.2 3.8 %collective-permute-start.4 = (bf16[3,96,1536]{2,1,0:T(8,128)(2,1)S(1)}, bf16[3,96,1536]{2,1,0:T(8,128)(2,1)S(1)}, u32[]{:S(2)}, u32[]{:S(2)}) collective-permute-start(bf16[3,96,1536]{2,1,0:T(8,128)(2,1)S(1)} %get-tuple-element.28.refs_4_.refs_5_), channel_id=1, source_target_pairs={{0,1},{1,0},{2,3},{3,2},{4,5},{5,4},{6,7},{7,6},{8,9},{9,8},{10,11... | collective-permute-start | bytes 2654216 | tf_op jit(solution)/shard_map/ppermute | solution.py:25
  18.0 12.4 %copy-start.2 = (bf16[3,96,1536]{2,1,0:T(8,128)(2,1)}, bf16[3,96,1536]{2,1,0:T(8,128)(2,1)S(1)}, u32[]{:S(2)}) copy-start(bf16[3,96,1536]{2,1,0:T(8,128)(2,1)S(1)} %collective-permute-done.6.refs_3_.refs_4_) | copy-start | bytes 2654212
  18.0 12.4 %collective-permute-start.8 = (bf16[3,96,1536]{2,1,0:T(8,128)(2,1)S(1)}, bf16[3,96,1536]{2,1,0:T(8,128)(2,1)}, u32[]{:S(2)}, u32[]{:S(2)}) collective-permute-start(bf16[3,96,1536]{2,1,0:T(8,128)(2,1)S(1)} %collective-permute-done.6.refs_3_.refs_4_), channel_id=1, source_target_pairs={{0,4},{1,13},{4,8},{5,1},{8,12},{9,5},{12,0},{13,9},{2,6},{3,15},{... | collective-permute-start | bytes 2654216 | tf_op jit(solution)/shard_map/ppermute | solution.py:32
  20.5 14.2 %collective-permute-start.11 = (bf16[3,96,1536]{2,1,0:T(8,128)(2,1)S(1)}, bf16[3,96,1536]{2,1,0:T(8,128)(2,1)}, u32[]{:S(2)}, u32[]{:S(2)}) collective-permute-start(bf16[3,96,1536]{2,1,0:T(8,128)(2,1)S(1)} %get-tuple-element.34.refs_6_.refs_7_), channel_id=1, source_target_pairs={{0,2},{1,131},{2,128},{3,1},{128,130},{129,3},{130,0},{131,129},{4... | collective-permute-start | bytes 2654216 | tf_op jit(solution)/shard_map/ppermute | solution.py:39
  21.2 23.8 %collective-permute-start.14 = (bf16[3,96,1536]{2,1,0:T(8,128)(2,1)S(1)}, bf16[3,96,1536]{2,1,0:T(8,128)(2,1)}, u32[]{:S(2)}, u32[]{:S(2)}) collective-permute-start(bf16[3,96,1536]{2,1,0:T(8,128)(2,1)S(1)} %get-tuple-element.37.refs_5_.refs_6_), channel_id=1, source_target_pairs={{0,4},{1,13},{4,8},{5,1},{8,12},{9,5},{12,0},{13,9},{2,6},{3,15},{... | collective-permute-start | bytes 2654216 | tf_op jit(solution)/shard_map/ppermute | solution.py:32
  23.0 22.6 %collective-permute-start.7 = (bf16[3,96,1536]{2,1,0:T(8,128)(2,1)S(1)}, bf16[3,96,1536]{2,1,0:T(8,128)(2,1)}, u32[]{:S(2)}, u32[]{:S(2)}) collective-permute-start(bf16[3,96,1536]{2,1,0:T(8,128)(2,1)S(1)} %get-tuple-element.34.refs_6_.refs_7_), channel_id=1, source_target_pairs={{0,1},{1,0},{2,3},{3,2},{4,5},{5,4},{6,7},{7,6},{8,9},{9,8},{10,11... | collective-permute-start | bytes 2654216 | tf_op jit(solution)/shard_map/ppermute | solution.py:25
  30.4 15.1 %collective-permute-start.9 = (bf16[3,96,1536]{2,1,0:T(8,128)(2,1)}, bf16[3,96,1536]{2,1,0:T(8,128)(2,1)}, u32[]{:S(2)}, u32[]{:S(2)}) collective-permute-start(bf16[3,96,1536]{2,1,0:T(8,128)(2,1)} %collective-permute-done.8.refs_8_.refs_9_), channel_id=1, source_target_pairs={{0,1},{1,0},{2,3},{3,2},{4,5},{5,4},{6,7},{7,6},{8,9},{9,8},{10,11... | collective-permute-start | bytes 2654216 | tf_op jit(solution)/shard_map/ppermute | solution.py:25
  32.5 19.8 %collective-permute-start.5 = (bf16[3,96,1536]{2,1,0:T(8,128)(2,1)S(1)}, bf16[3,96,1536]{2,1,0:T(8,128)(2,1)S(1)}, u32[]{:S(2)}, u32[]{:S(2)}) collective-permute-start(bf16[3,96,1536]{2,1,0:T(8,128)(2,1)S(1)} %get-tuple-element.34.refs_6_.refs_7_), channel_id=1, source_target_pairs={{0,4},{1,13},{4,8},{5,1},{8,12},{9,5},{12,0},{13,9},{2,6},{3,15},{... | collective-permute-start | bytes 2654216 | tf_op jit(solution)/shard_map/ppermute | solution.py:32
  34.7 19.8 %collective-permute-start.12 = (bf16[3,96,1536]{2,1,0:T(8,128)(2,1)}, bf16[3,96,1536]{2,1,0:T(8,128)(2,1)S(1)}, u32[]{:S(2)}, u32[]{:S(2)}) collective-permute-start(bf16[3,96,1536]{2,1,0:T(8,128)(2,1)} %collective-permute-done.11.refs_2_.refs_11_), channel_id=1, source_target_pairs={{0,1},{1,0},{2,3},{3,2},{4,5},{5,4},{6,7},{7,6},{8,9},{9,8},{10,11... | collective-permute-start | bytes 2654216 | tf_op jit(solution)/shard_map/ppermute | solution.py:25
  34.7 0.6 copy-start.6
  35.3 1.3 %copy-start.7 = (bf16[384,1536]{1,0:T(8,128)(2,1)S(1)}, bf16[384,1536]{1,0:T(8,128)(2,1)}, u32[]{:S(2)}) copy-start(bf16[384,1536]{1,0:T(8,128)(2,1)} %forward_ref.1) | copy-start | bytes 3538948
  36.6 1.3 %copy-start.8 = (bf16[384,1536]{1,0:T(8,128)(2,1)S(1)}, bf16[384,1536]{1,0:T(8,128)(2,1)}, u32[]{:S(2)}) copy-start(bf16[384,1536]{1,0:T(8,128)(2,1)} %reverse_ref.1) | copy-start | bytes 3538948
  37.8 7.7 %copy-start.1 = (bf16[1,3,96,1536]{3,2,1,0:T(8,128)(2,1)S(1)}, bf16[1,3,96,1536]{3,2,1,0:T(8,128)(2,1)}, u32[]{:S(2)}) copy-start(bf16[1,3,96,1536]{3,2,1,0:T(8,128)(2,1)} %param.8) | copy-start | bytes 2654212
  37.8 7.7 %copy-start.3 = (bf16[3,96,1536]{2,1,0:T(8,128)(2,1)S(1)}, bf16[3,96,1536]{2,1,0:T(8,128)(2,1)}, u32[]{:S(2)}) copy-start(bf16[3,96,1536]{2,1,0:T(8,128)(2,1)} %copy-done.2) | copy-start | bytes 2654212
  45.0 9.5 %collective-permute-start.15 = (bf16[3,96,1536]{2,1,0:T(8,128)(2,1)}, bf16[3,96,1536]{2,1,0:T(8,128)(2,1)S(1)}, u32[]{:S(2)}, u32[]{:S(2)}) collective-permute-start(bf16[3,96,1536]{2,1,0:T(8,128)(2,1)} %collective-permute-done.14.refs_6_.refs_15_), channel_id=1, source_target_pairs={{0,1},{1,0},{2,3},{3,2},{4,5},{5,4},{6,7},{7,6},{8,9},{9,8},{10,11... | collective-permute-start | bytes 2654216 | tf_op jit(solution)/shard_map/ppermute | solution.py:25
  52.4 2.5 %collective-permute-start.13 = (bf16[3,96,1536]{2,1,0:T(8,128)(2,1)S(1)}, bf16[3,96,1536]{2,1,0:T(8,128)(2,1)S(1)}, u32[]{:S(2)}, u32[]{:S(2)}) collective-permute-start(bf16[3,96,1536]{2,1,0:T(8,128)(2,1)S(1)} %fence.7.refs_4_.refs_13_), channel_id=1, source_target_pairs={{0,1},{1,0},{2,3},{3,2},{4,5},{5,4},{6,7},{7,6},{8,9},{9,8},{10,11... | collective-permute-start | bytes 2654216 | tf_op jit(solution)/shard_map/ppermute | solution.py:25
  52.5 12.5 %collective-permute-start.10 = (bf16[3,96,1536]{2,1,0:T(8,128)(2,1)S(1)}, bf16[3,96,1536]{2,1,0:T(8,128)(2,1)S(1)}, u32[]{:S(2)}, u32[]{:S(2)}) collective-permute-start(bf16[3,96,1536]{2,1,0:T(8,128)(2,1)S(1)} %fence.7.refs_4_.refs_13_), channel_id=1, source_target_pairs={{0,2},{1,131},{2,128},{3,1},{128,130},{129,3},{130,0},{131,129},{4... | collective-permute-start | bytes 2654216 | tf_op jit(solution)/shard_map/ppermute | solution.py:39
  54.9 14.6 %copy-start = (bf16[1536,1024]{1,0:T(8,128)(2,1)S(1)}, bf16[1536,1024]{1,0:T(8,128)(2,1)}, u32[]{:S(2)}) copy-start(bf16[1536,1024]{1,0:T(8,128)(2,1)} %refs_20_.1) | copy-start | bytes 9437188
  62.4 7.2 %copy-start.4 = (f32[1,1536]{1,0:T(1,128)S(1)}, f32[1,1536]{1,0:T(1,128)}, u32[]{:S(2)}) copy-start(f32[1,1536]{1,0:T(1,128)} %refs_19_.1) | copy-start | bytes 18436
  62.4 7.2 %copy-start.5 = (f32[1024]{0:T(1024)S(1)}, f32[1024]{0:T(1024)}, u32[]{:S(2)}) copy-start(f32[1024]{0:T(1024)} %param.11) | copy-start | bytes 12292
  65.1 4.4 %collective-permute-start.16 = (bf16[3,96,1536]{2,1,0:T(8,128)(2,1)S(1)}, bf16[3,96,1536]{2,1,0:T(8,128)(2,1)S(1)}, u32[]{:S(2)}, u32[]{:S(2)}) collective-permute-start(bf16[3,96,1536]{2,1,0:T(8,128)(2,1)S(1)} %fence.8.refs_0_.refs_17_), channel_id=1, source_target_pairs={{0,1},{1,0},{2,3},{3,2},{4,5},{5,4},{6,7},{7,6},{8,9},{9,8},{10,11... | collective-permute-start | bytes 2654216 | tf_op jit(solution)/shard_map/ppermute | solution.py:25
  67.5 14.9 %collective-permute-start.18 = (bf16[144,1536]{1,0:T(8,128)(2,1)S(1)}, bf16[144,1536]{1,0:T(8,128)(2,1)S(1)}, u32[]{:S(2)}, u32[]{:S(2)}) collective-permute-start(bf16[144,1536]{1,0:T(8,128)(2,1)S(1)} %fence.9), channel_id=1, source_target_pairs={{0,15},{1,14},{2,13},{3,12},{4,11},{5,10},{6,9},{7,8},{8,7},{9,6},... | collective-permute-start | bytes 1327112 | tf_op jit(solution)/shard_map/ppermute | solution.py:332
  72.1 20.6 %collective-permute-start.17 = (bf16[256,1024]{1,0:T(8,128)(2,1)S(1)}, bf16[256,1024]{1,0:T(8,128)(2,1)S(1)}, u32[]{:S(2)}, u32[]{:S(2)}) collective-permute-start(bf16[256,1024]{1,0:T(8,128)(2,1)S(1)} %finish.3), channel_id=1, source_target_pairs={{0,15},{1,14},{2,13},{3,12},{4,11},{5,10},{6,9},{7,8},{8,7},{9,6},... | collective-permute-start | bytes 1572872 | tf_op jit(solution)/shard_map/ppermute | solution.py:336
